TPU v7x, 32 devices: a whole 2x2x4 slice. The times are simulated.
32 devices in a mesh: batch: 4 (over y, x), group: 8 (over z, core).
Axes of the slice: x: 2, y: 2, z: 4, core: 2. Of those that a mesh axis runs over, the one named last changes fastest.
Arguments:
- noise: bfloat16 [512, 99840], P('batch', 'group'), may hold values from -24 to 24
- data: bfloat16 [512, 99840], P('batch', 'group'), may hold values from -6 to 6
Outputs:
- targets: bfloat16 [512, 99840], P('batch', 'group')
- potential: float32 [512], replicated
All inputs are finite; a program needn't handle non-finite values.
Results may differ from a plain program's by a relative error of at most 0.007.
Values may be sent and summed in bfloat16 or wider, within the bound.
No kernel may reach another device: no remote copies, remote signals or barrier semaphores. Data moves between devices by JAX's collectives and lax.ppermute only.
A program may use at most 64 MiB of HBM per device.

v0:
```python
import jax
import jax.numpy as jnp
from jax import lax
from jax.sharding import PartitionSpec as P

ITERS = 4
FEAT = 99840


def combined_all(value, axis, join):
    pieces = jax.tree.map(lambda part: lax.all_gather(part, axis), value)
    head = jax.tree.map(lambda part: part[0], pieces)
    tail = jax.tree.map(lambda part: part[1:], pieces)
    total, _ = lax.scan(lambda total, slab: (join(total, slab), None), head, tail)
    return total


def combine_parts(first, second):
    top = jnp.maximum(first[0], second[0])
    total = first[1] * jnp.exp(first[0] - top) + second[1] * jnp.exp(second[0] - top)
    return (top, total)


def local_parts(values, axis):
    top = jnp.max(values, axis=axis)
    total = jnp.sum(jnp.exp(values - jnp.expand_dims(top, axis)), axis=axis)
    return (top, total)


def local(noise, data):
    eps = 2.0 / jnp.sqrt(jnp.float32(FEAT))
    batch_total = noise.shape[0] * lax.axis_size("batch")
    loga = -jnp.log(jnp.float32(batch_total))
    noise_sq = jnp.sum(jnp.square(noise.astype(jnp.float32)), axis=1)
    all_rows = lax.all_gather(data, "batch", axis=0, tiled=True)
    piece_sq = jnp.sum(jnp.square(all_rows.astype(jnp.float32)), axis=1)
    cross = lax.dot_general(
        noise, all_rows, (((1,), (1,)), ((), ())), preferred_element_type=jnp.float32
    )
    partial_value = noise_sq[:, None] + piece_sq[None, :] - 2.0 * cross
    cost = lax.psum(partial_value, "group") / jnp.float32(FEAT)
    potential = jnp.zeros((batch_total,), jnp.float32)
    for step in range(ITERS):
        top, total = local_parts((potential[None, :] - cost) / eps, 1)
        rowpot = eps * loga - eps * (top + jnp.log(total))
        parts = local_parts((rowpot[:, None] - cost) / eps, 0)
        top, total = combined_all(parts, "batch", combine_parts)
        potential = eps * loga - eps * (top + jnp.log(total))
    scores = (potential[None, :] - cost) / eps
    top, total = local_parts(scores, 1)
    weights = jnp.exp(scores - (top + jnp.log(total))[:, None]).astype(jnp.bfloat16)
    targets = jnp.dot(weights, all_rows, preferred_element_type=jnp.float32)
    return (targets.astype(jnp.bfloat16), potential)


def solution(mesh):
    in_specs = (P("batch", "group"), P("batch", "group"))
    out_specs = (P("batch", "group"), P())
    return jax.shard_map(local, mesh=mesh, in_specs=in_specs, out_specs=out_specs, check_vma=False)
```

profile of v0, /device:TPU:0, one launch (start us, length us, event | category | flops | bytes accessed | tf_op | source)
XLA Modules:
  0.0 301.8 jit_solution(15154404281146459594)
XLA Ops:
  8.0 3.2 %multiply_reduce_fusion.1 = f32[128]{0:T(128)S(1)} fusion(bf16[128,12480]{0,1:T(8,128)(2,1)} %param.10), kind=kLoop, calls=%fused_computation.14 | loop fusion | flops 4792192 | bytes 3195392 | tf_op jit(solution)/shard_map/reduce_sum | solution.py:34
  11.2 125.4 %all-gather.18.cloned.1.call-done = bf16[512,12480]{0,1:T(8,128)(2,1)} async-done(((bf16[128,12480]{0,1:T(8,128)(2,1)}), bf16[512,12480]{0,1:T(8,128)(2,1)}) %all-gather.18.cloned.1.call-update) | async-done | bytes 12779536 | tf_op jit(solution)/shard_map/all_gather | solution.py:35
  136.6 8.0 %multiply_reduce_fusion = f32[512]{0:T(512)S(1)} fusion(bf16[512,12480]{0,1:T(8,128)(2,1)} %all-gather.18.cloned.1.call-done), kind=kLoop, calls=%fused_computation.12 | loop fusion | flops 19168768 | bytes 12781568 | tf_op jit(solution)/shard_map/reduce_sum | solution.py:36
  145.0 2.7 fusion
  147.8 55.1 %all-reduce.2.cloned.1.call-done = f32[128,512]{1,0:T(8,128)} async-done(((f32[128,512]{1,0:T(8,128)}), f32[128,512]{1,0:T(8,128)}) %all-reduce.2.cloned.1.call-update) | async-done | bytes 262160 | tf_op jit(solution)/shard_map/psum | solution.py:41
  202.9 1.1 fusion.1
  204.0 1.1 exponential_reduce_fusion.8
  206.3 1.1 exponential_reduce_fusion.7
  207.4 8.0 %all-gather.9 = f32[4,1,512]{2,1,0:T(1,128)S(1)} all-gather(f32[1,1,512]{2,1,0:T(1,128)S(1)} %bitcast.95), channel_id=3, replica_groups=mesh['batch'=4,'group'=8] {'batch'}, dimensions={0}, use_global_device_ids=true | all-gather | bytes 10240 | tf_op jit(solution)/shard_map/all_gather | solution.py:11
  215.4 8.0 %all-gather.8 = f32[4,1,512]{2,1,0:T(1,128)S(1)} all-gather(f32[1,1,512]{2,1,0:T(1,128)S(1)} %bitcast.91), channel_id=2, replica_groups=mesh['batch'=4,'group'=8] {'batch'}, dimensions={0}, use_global_device_ids=true | all-gather | bytes 10240 | tf_op jit(solution)/shard_map/all_gather | solution.py:11
  224.7 1.1 exponential_reduce_fusion.6
  226.9 1.1 exponential_reduce_fusion.5
  228.0 7.1 %all-gather.11 = f32[4,1,512]{2,1,0:T(1,128)S(1)} all-gather(f32[1,1,512]{2,1,0:T(1,128)S(1)} %bitcast.96), channel_id=5, replica_groups=mesh['batch'=4,'group'=8] {'batch'}, dimensions={0}, use_global_device_ids=true | all-gather | bytes 10240 | tf_op jit(solution)/shard_map/all_gather | solution.py:11
  235.1 8.0 %all-gather.10 = f32[4,1,512]{2,1,0:T(1,128)S(1)} all-gather(f32[1,1,512]{2,1,0:T(1,128)S(1)} %bitcast.92), channel_id=4, replica_groups=mesh['batch'=4,'group'=8] {'batch'}, dimensions={0}, use_global_device_ids=true | all-gather | bytes 10240 | tf_op jit(solution)/shard_map/all_gather | solution.py:11
  244.4 1.1 exponential_reduce_fusion.4
  246.6 1.1 exponential_reduce_fusion.3
  247.7 7.1 %all-gather.13 = f32[4,1,512]{2,1,0:T(1,128)S(1)} all-gather(f32[1,1,512]{2,1,0:T(1,128)S(1)} %bitcast.97), channel_id=7, replica_groups=mesh['batch'=4,'group'=8] {'batch'}, dimensions={0}, use_global_device_ids=true | all-gather | bytes 10240 | tf_op jit(solution)/shard_map/all_gather | solution.py:11
  254.9 8.0 %all-gather.12 = f32[4,1,512]{2,1,0:T(1,128)S(1)} all-gather(f32[1,1,512]{2,1,0:T(1,128)S(1)} %bitcast.93), channel_id=6, replica_groups=mesh['batch'=4,'group'=8] {'batch'}, dimensions={0}, use_global_device_ids=true | all-gather | bytes 10240 | tf_op jit(solution)/shard_map/all_gather | solution.py:11
  264.2 1.1 exponential_reduce_fusion.2
  266.4 1.1 exponential_reduce_fusion.1
  267.5 7.1 %all-gather.15 = f32[4,1,512]{2,1,0:T(1,128)S(1)} all-gather(f32[1,1,512]{2,1,0:T(1,128)S(1)} %bitcast.98), channel_id=9, replica_groups=mesh['batch'=4,'group'=8] {'batch'}, dimensions={0}, use_global_device_ids=true | all-gather | bytes 10240 | tf_op jit(solution)/shard_map/all_gather | solution.py:11
  274.6 8.0 %all-gather.14 = f32[4,1,512]{2,1,0:T(1,128)S(1)} all-gather(f32[1,1,512]{2,1,0:T(1,128)S(1)} %bitcast.94), channel_id=8, replica_groups=mesh['batch'=4,'group'=8] {'batch'}, dimensions={0}, use_global_device_ids=true | all-gather | bytes 10240 | tf_op jit(solution)/shard_map/all_gather | solution.py:11
  283.9 1.1 exponential_reduce_fusion
  285.1 9.9 %convolution_convert_fusion = bf16[128,12480]{0,1:T(8,128)(2,1)} fusion(bf16[512,12480]{0,1:T(8,128)(2,1)} %all-gather.18.cloned.1.call-done, f32[128]{0:T(128)S(1)} %log_add_fusion, f32[512]{0:T(512)S(1)} %multiply_subtract_fusion, f32[128,512]{1,0:T(8,128)S(1)} %copy-done.1), kind=kOutput, calls=%fused_computation.13 | convolution fusion | flops 1637703680 | bytes 16239104 | tf_op jit(solution)/shard_map/dot_general | solution.py:52
  (81 shorter events, 10.9 us)
Async XLA Ops:
  7.2 129.4 %all-gather.18.cloned.1.call-start = ((), (), s32[]{:S(2)}) async-start(), calls=%async_computation | async-start | bytes 15974400 | tf_op jit(solution)/shard_map/all_gather | solution.py:35
  7.9 195.0 %all-reduce.2.cloned.1.call-start = ((), (), s32[]{:S(2)}) async-start(), calls=%async_computation.1 | async-start | bytes 524288 | tf_op jit(solution)/shard_map/psum | solution.py:41
  7.9 136.6 %copy-start.2 = (bf16[128,12480]{0,1:T(8,128)(2,1)S(1)}, bf16[128,12480]{0,1:T(8,128)(2,1)}, u32[]{:S(2)}) copy-start(bf16[128,12480]{0,1:T(8,128)(2,1)} %param.10) | copy-start | bytes 9584644
  136.6 8.5 %copy-start = (bf16[512,12480]{0,1:T(8,128)(2,1)S(1)}, bf16[512,12480]{0,1:T(8,128)(2,1)}, u32[]{:S(2)}) copy-start(bf16[512,12480]{0,1:T(8,128)(2,1)} %all-gather.18.cloned.1.call-done) | copy-start | bytes 38338564
  202.9 82.1 %copy-start.1 = (f32[128,512]{1,0:T(8,128)S(1)}, f32[128,512]{1,0:T(8,128)}, u32[]{:S(2)}) copy-start(f32[128,512]{1,0:T(8,128)} %all-reduce.2.cloned.1.call-done) | copy-start | bytes 786436
  282.8 12.1 %copy-start.3 = (f32[512]{0:T(512)}, f32[512]{0:T(512)S(1)}, u32[]{:S(2)}) copy-start(f32[512]{0:T(512)S(1)} %multiply_subtract_fusion) | copy-start | bytes 6148
Sparse Core Ops, SparseCore 0:
  9.8 126.7 all-gather.17
  147.9 54.9 all-reduce.1
where the time goes:
time: 303 us; the launch traced here: 302 us
  waiting for transfers between devices  181 us (60%)
  blocking collectives  61.4 us (20%)
  other arithmetic  31.3 us (10%)
  between operations  14.2 us (5%)
  matrix products  12.6 us (4%)
    all_gather x1, waiting for transfers between devices, local(): all_rows = lax.all_gather(data, 'batch', axis=0, tiled=True)  125 us
    all_gather x8, blocking collectives, combined_all(): pieces = jax.tree.map(lambda part: lax.all_gather(part, axis), value)  61.4 us
    psum x1, waiting for transfers between devices, local(): cost = lax.psum(partial_value, 'group') / jnp.float32(FEAT)  55.1 us
    reduce_sum x9, other arithmetic, local_parts(): total = jnp.sum(jnp.exp(values - jnp.expand_dims(top, axis)), axis=axis)  10.1 us
    dot_general x1, matrix products, local(): targets = jnp.dot(weights, all_rows, preferred_element_type=jnp.float32)  9.89 us
    reduce_max x9, other arithmetic, local_parts(): top = jnp.max(values, axis=axis)  9.68 us
    reduce_sum x1, other arithmetic, local(): piece_sq = jnp.sum(jnp.square(all_rows.astype(jnp.float32)), axis=1)  8.01 us
  transfers between devices with their start and end apart: 2, of which 2 were waited for; matrix products, arithmetic and copies ran while one was open for 1% of the time, Pallas kernels for 0%

commit v1 on v0

--- a/solution.py
+++ b/solution.py
@@ -1,6 +1,10 @@
+import functools
+
 import jax
 import jax.numpy as jnp
 from jax import lax
+from jax.experimental import pallas as pl
+from jax.experimental.pallas import tpu as pltpu
 from jax.sharding import PartitionSpec as P
 
 ITERS = 4
@@ -27,7 +31,7 @@
     return (top, total)
 
 
-def local(noise, data):
+def local_any(noise, data):
     eps = 2.0 / jnp.sqrt(jnp.float32(FEAT))
     batch_total = noise.shape[0] * lax.axis_size("batch")
     loga = -jnp.log(jnp.float32(batch_total))
@@ -53,7 +57,251 @@
     return (targets.astype(jnp.bfloat16), potential)
 
 
+X, Y, DIAG = 1, 2, 3
+
+
+def swap(value, way):
+    return lax.ppermute(value, "batch", [(i, i ^ way) for i in range(4)])
+
+
+VMEM = pl.BlockSpec(memory_space=pltpu.VMEM)
+SMEM = pl.BlockSpec(memory_space=pltpu.SMEM)
+HBM = pl.BlockSpec(memory_space=pltpu.HBM)
+
+
+def split_kernel(whole_ref, low_ref, high_ref, sem):
+    size = low_ref.shape[0]
+    copies = [
+        pltpu.make_async_copy(whole_ref.at[pl.ds(0, size), :], low_ref, sem.at[0]),
+        pltpu.make_async_copy(whole_ref.at[pl.ds(size, high_ref.shape[0]), :], high_ref, sem.at[1]),
+    ]
+    for copy in copies:
+        copy.start()
+    for copy in copies:
+        copy.wait()
+
+
+def split(whole, size):
+    feats, rows = whole.shape
+    return pl.pallas_call(
+        split_kernel,
+        out_shape=(
+            jax.ShapeDtypeStruct((size, rows), whole.dtype),
+            jax.ShapeDtypeStruct((feats - size, rows), whole.dtype),
+        ),
+        in_specs=[HBM],
+        out_specs=(VMEM, VMEM),
+        scratch_shapes=[pltpu.SemaphoreType.DMA((2,))],
+        cost_estimate=pl.CostEstimate(flops=0, bytes_accessed=4 * whole.size, transcendentals=0),
+    )(whole)
+
+
+DEPTH = 512
+
+
+def cross_kernel(spans, noise_ref, *refs):
+    *refs, out_ref = refs
+    width = noise_ref.shape[0]
+
+    def add(piece_ref, start, at, size, total):
+        cross, square = total
+        piece = piece_ref[pl.ds(at, size), :]
+        noise = noise_ref[:, pl.ds(start + at, size)]
+        cross = cross + jnp.dot(noise, piece, preferred_element_type=jnp.float32)
+        value = jnp.square(piece.astype(jnp.float32))
+        return cross, square + jnp.sum(value.reshape(size // 8, 8, width), axis=0)
+
+    for k, block_spans in enumerate(spans):
+        (prior_ref, *pieces), refs = refs[: 1 + len(block_spans)], refs[1 + len(block_spans):]
+        total = (jnp.zeros((width, width), jnp.float32), jnp.zeros((8, width), jnp.float32))
+        for (start, size), piece_ref in zip(block_spans, pieces):
+            whole = size // DEPTH
+
+            def step(t, total):
+                return add(piece_ref, start, pl.multiple_of(t * DEPTH, DEPTH), DEPTH, total)
+
+            total = lax.fori_loop(0, whole, step, total, unroll=2)
+            if size % DEPTH:
+                total = add(piece_ref, start, whole * DEPTH, size % DEPTH, total)
+        cross, square = total
+        out_ref[:, k * width : (k + 1) * width] = prior_ref[...] + (
+            jnp.sum(square, axis=0, keepdims=True) - 2.0 * cross
+        )
+
+
+def crossed(noise, *blocks):
+    rows = noise.shape[0]
+    spans = [block[2::2] for block in blocks]
+    values = [value for block in blocks for value in (block[0],) + block[1::2]]
+    flops = sum(2 * rows * rows * size for block_spans in spans for _, size in block_spans)
+    return pl.pallas_call(
+        functools.partial(cross_kernel, spans),
+        out_shape=jax.ShapeDtypeStruct((rows, rows * len(blocks)), jnp.float32),
+        in_specs=[VMEM] * (1 + len(values)),
+        out_specs=VMEM,
+        compiler_params=pltpu.CompilerParams(vmem_limit_bytes=16 * 2**20),
+        cost_estimate=pl.CostEstimate(flops=flops, bytes_accessed=flops // 64, transcendentals=0),
+    )(noise, *values)
+
+
+STEP = 64
+TILES = 10
+
+
+def pair_kernel(rows, feats, places, own_ref, *refs):
+    early_refs, late_refs, refs = refs[:4], refs[4:8], refs[8:]
+    pieces, refs = refs[: len(places)], refs[len(places):]
+    targets_ref, potential_ref, blocks, held, scores, out, in_sem, out_sem = refs
+    batch = 4 * rows
+    eps = 2.0 / FEAT**0.5
+    scale = -1.0 / (FEAT * eps)
+    loga = -jnp.log(jnp.float32(batch))
+    own = own_ref[0]
+
+    loads = []
+    for k, (start, r) in enumerate(places):
+        copy = pltpu.make_async_copy(
+            pieces[k],
+            held.at[pl.ds(start, pieces[k].shape[0]), pl.ds(r * rows, rows)],
+            in_sem.at[k],
+        )
+        copy.start()
+        loads.append(copy)
+
+    def block(i):
+        return pl.ds(pl.multiple_of(i * rows, rows), rows)
+
+    for p in range(4):
+        for r in range(DIAG):
+            blocks[block(own ^ p), block(own ^ (p ^ r))] = early_refs[p][:, block(r)] * scale
+        blocks[block(own ^ p), block(own ^ (p ^ DIAG))] = late_refs[p][...] * scale
+
+    def sweep(_, v):
+        u = []
+        top = jnp.full((1, batch), -jnp.inf, jnp.float32)
+        for c in range(batch // STEP):
+            k = blocks[pl.ds(c * STEP, STEP), :]
+            a = k + v
+            m = jnp.max(a, axis=1, keepdims=True)
+            s = jnp.sum(jnp.exp(a - m), axis=1, keepdims=True)
+            u.append(loga - (m + jnp.log(s)))
+            top = jnp.maximum(top, jnp.max(k + u[-1], axis=0, keepdims=True))
+        total = jnp.zeros((1, batch), jnp.float32)
+        for c in range(batch // STEP):
+            a = blocks[pl.ds(c * STEP, STEP), :] + u[c]
+            total = total + jnp.sum(jnp.exp(a - top), axis=0, keepdims=True)
+        return loga - (top + jnp.log(total))
+
+    v = lax.fori_loop(0, ITERS, sweep, jnp.zeros((1, batch), jnp.float32))
+    potential_ref[...] = v * eps
+
+    a = blocks[block(own), :] + v
+    m = jnp.max(a, axis=1, keepdims=True)
+    s = jnp.sum(jnp.exp(a - m), axis=1, keepdims=True)
+    scores[...] = jnp.exp(a - (m + jnp.log(s)))
+    w = jnp.concatenate([scores[:, block(own ^ r)].T for r in range(4)], axis=0).astype(jnp.bfloat16)
+    for copy in loads:
+        copy.wait()
+
+    tile = feats // TILES
+
+    def stored(t):
+        part = pl.ds(pl.multiple_of(t * tile, 16), tile)
+        return pltpu.make_async_copy(out.at[part, :], targets_ref.at[part, :], out_sem.at[t])
+
+    def multiply(t, _):
+        part = pl.ds(pl.multiple_of(t * tile, 16), tile)
+        out[part, :] = jnp.dot(held[part, :], w, preferred_element_type=jnp.float32).astype(jnp.bfloat16)
+        stored(t).start()
+        return 0
+
+    lax.fori_loop(0, TILES, multiply, 0)
+    for t in range(TILES):
+        stored(t).wait()
+
+
+def paired(own, early, late, pieces, places, rows, feats):
+    batch = 4 * rows
+    return pl.pallas_call(
+        functools.partial(pair_kernel, rows, feats, places),
+        out_shape=(
+            jax.ShapeDtypeStruct((feats, rows), jnp.bfloat16),
+            jax.ShapeDtypeStruct((1, batch), jnp.float32),
+        ),
+        in_specs=[SMEM] + [VMEM] * 8 + [HBM] * len(pieces),
+        out_specs=(HBM, VMEM),
+        scratch_shapes=[
+            pltpu.VMEM((batch, batch), jnp.float32),
+            pltpu.VMEM((feats, batch), jnp.bfloat16),
+            pltpu.VMEM((rows, batch), jnp.float32),
+            pltpu.VMEM((feats, rows), jnp.bfloat16),
+            pltpu.SemaphoreType.DMA((len(pieces),)),
+            pltpu.SemaphoreType.DMA((TILES,)),
+        ],
+        compiler_params=pltpu.CompilerParams(vmem_limit_bytes=58 * 2**20),
+        cost_estimate=pl.CostEstimate(
+            flops=2 * rows * batch * feats, bytes_accessed=10 * rows * feats, transcendentals=9 * batch * batch
+        ),
+    )(own, *early, *late, *pieces)
+
+
+def squared(values_t):
+    return jnp.sum(jnp.square(values_t.astype(jnp.float32)), axis=0)
+
+
+def group_sum(partial_value):
+    groups = lax.axis_size("group")
+    rows, width = partial_value.shape
+    parts = lax.all_to_all(partial_value, "group", 0, 0, tiled=True)
+    return jnp.sum(parts.reshape(groups, rows // groups, width), axis=0)
+
+
+def to_all(mine, axes, devices):
+    copies = jnp.broadcast_to(mine[None], (devices,) + mine.shape)
+    held = lax.all_to_all(copies, axes, 0, 0, tiled=True)
+    return held.reshape(devices * mine.shape[0], mine.shape[1])
+
+
+def local_square(noise, data):
+    rows, feats = noise.shape
+    groups = lax.axis_size("group")
+    noise_t, data_t = noise.T, data.T
+    own = lax.axis_index("batch").astype(jnp.int32).reshape(1)
+
+    half = feats // 256 * 128
+    low, high = (0, half), (half, feats - half)
+    d_low, d_high = split(data_t, half)
+    x_high, y_low = swap(d_high, X), swap(d_low, Y)
+    x_low, y_high = swap(d_low, X), swap(d_high, Y)
+    diag_low, diag_high = swap(y_low, X), swap(x_high, Y)
+
+    start = jnp.broadcast_to(squared(noise_t)[:, None], (rows, rows))
+    early = crossed(
+        noise,
+        (crossed(noise, (start, d_low, low, d_high, high)),),
+        (crossed(noise, (start, x_high, high)), x_low, low),
+        (crossed(noise, (start, y_low, low)), y_high, high),
+    )
+    early_own = to_all(group_sum(early), "group", groups)
+    early_rows = [early_own, swap(early_own, X), swap(early_own, Y), swap(early_own, DIAG)]
+    early_rows[0], diag_low, diag_high = lax.optimization_barrier((early_own, diag_low, diag_high))
+    late = crossed(noise, (start, diag_low, low, diag_high, high))
+    way = 1
+    while way < groups:
+        late = late + lax.ppermute(late, "group", [(g, g ^ way) for g in range(groups)])
+        way *= 2
+    late_rows = [late, swap(late, X), swap(late, Y), swap(late, DIAG)]
+
+    pieces = [d_low, d_high, x_low, x_high, y_low, y_high, diag_low, diag_high]
+    places = [(span[0], r) for r in range(4) for span in (low, high)]
+    targets_t, potential = paired(own, early_rows, late_rows, pieces, places, rows, feats)
+    return (targets_t.T, potential[0])
+
+
 def solution(mesh):
     in_specs = (P("batch", "group"), P("batch", "group"))
     out_specs = (P("batch", "group"), P())
+    groups = mesh.shape["group"]
+    paired_form = mesh.shape["batch"] == 4 and groups & (groups - 1) == 0
+    local = local_square if paired_form else local_any
     return jax.shard_map(local, mesh=mesh, in_specs=in_specs, out_specs=out_specs, check_vma=False)

time: 303 us -> 150 us (0.50)
  waiting for transfers between devices: 181 us -> 62.2 us
  blocking collectives: 61.4 us -> 23.7 us
  Pallas kernels: 0 us -> 34.2 us
  other arithmetic: 31.3 us -> 3.28 us
  starting transfers between devices: 0.08 us -> 20.2 us
  between operations: 14.2 us -> 0.79 us
  matrix products: 12.6 us -> 0 us
  local copies, waits for them, and re-layouts: 0.65 us -> 4.89 us
    all_gather x1 -> x0, waiting for transfers between devices: 125 us -> none  [local(): all_rows = lax.all_gather(data, 'batch', axis=0, tiled=True)]
    ppermute x0 -> x15, waiting for transfers between devices: none -> 62.2 us  [the longest x12 58.9 us: swap(): return lax.ppermute(value, 'batch', [(i, i ^ way) for i in range(4)])]
    all_gather x8 -> x0, blocking collectives: 61.4 us -> none  [combined_all(): pieces = jax.tree.map(lambda part: lax.all_gather(part, axis), value)]
    psum x1 -> x0, waiting for transfers between devices: 55.1 us -> none  [local(): cost = lax.psum(partial_value, 'group') / jnp.float32(FEAT)]
    pallas_call x0 -> x7, Pallas kernels: none -> 34.2 us  [the longest x5 18.2 us: crossed(): pl.pallas_call(functools.partial(cross_kernel, spans), out_shape=jax.Shap...]
    all_to_all x0 -> x2, blocking collectives: none -> 23.7 us  [the longest x1 13 us: group_sum(): parts = lax.all_to_all(partial_value, 'group', 0, 0, tiled=True)]
    ppermute x0 -> x15, starting transfers between devices: none -> 20.2 us  [the longest x12 15.8 us: swap(): return lax.ppermute(value, 'batch', [(i, i ^ way) for i in range(4)])]
    reduce_sum x11 -> x2, other arithmetic: 21.3 us -> 3.25 us  [the longest x1 3.24 us: squared(): return jnp.sum(jnp.square(values_t.astype(jnp.float32)), axis=0)]
  transfers between devices with their start and end apart: 2 -> 15, of which waited for: 2 -> 10; matrix products, arithmetic and copies ran while one was open for 1% -> 5% of each run, Pallas kernels for 0% -> 9%
where the time goes in v1:
time: 150 us; the launch traced here: 149 us
  waiting for transfers between devices  62.2 us (41%)
  Pallas kernels  34.2 us (23%)
  blocking collectives  23.7 us (16%)
  starting transfers between devices  20.2 us (13%)
  local copies, waits for them, and re-layouts  4.89 us (3%)
  other arithmetic  3.28 us (2%)
    ppermute x12, waiting for transfers between devices, swap(): return lax.ppermute(value, 'batch', [(i, i ^ way) for i in range(4)])  58.9 us
    pallas_call x5, Pallas kernels, crossed(): pl.pallas_call(functools.partial(cross_kernel, spans), out_shape=jax.Shap...  18.2 us
    ppermute x12, starting transfers between devices, swap(): return lax.ppermute(value, 'batch', [(i, i ^ way) for i in range(4)])  15.8 us
    all_to_all x1, blocking collectives, group_sum(): parts = lax.all_to_all(partial_value, 'group', 0, 0, tiled=True)  13 us
    pallas_call x1, Pallas kernels, paired(): pl.pallas_call(functools.partial(pair_kernel, rows, feats, places), out_s...  12.3 us
    all_to_all x1, blocking collectives, to_all(): held = lax.all_to_all(copies, axes, 0, 0, tiled=True)  10.7 us
    unnamed x21, local copies, waits for them, and re-layouts  4.8 us
    ppermute x3, starting transfers between devices, local_square(): lax.ppermute(late, 'group', [(g, g ^ way) for g in range(groups)])  4.36 us
  transfers between devices with their start and end apart: 15, of which 10 were waited for; matrix products, arithmetic and copies ran while one was open for 5% of the time, Pallas kernels for 9%

profile of v1, /device:TPU:0, one launch (start us, length us, event | category | flops | bytes accessed | tf_op | source)
XLA Modules:
  0.0 149.3 jit_solution(17197938624269648206)
XLA Ops:
  0.6 3.6 %shard_map.41 = (bf16[6144,128]{1,0:T(8,128)(2,1)}, bf16[6336,128]{1,0:T(8,128)(2,1)}) custom-call(bf16[12480,128]{1,0:T(8,128)(2,1)} %bitcast.7), custom_call_target="tpu_custom_call" | custom-call | bytes 6389760 | tf_op jit(solution)/shard_map/pallas_call | solution.py:86
  4.3 3.0 %collective-permute-start = (bf16[6336,128]{1,0:T(8,128)(2,1)}, bf16[6336,128]{1,0:T(8,128)(2,1)}, u32[]{:S(2)}, u32[]{:S(2)}) collective-permute-start(bf16[6336,128]{1,0:T(8,128)(2,1)} %get-tuple-element.10.refs_2_.refs_9_), channel_id=1, source_target_pairs={{0,8},{8,0},{16,24},{24,16},{1,9},{9,1},{17,25},{25,17},{2,10},{10... | collective-permute-start | bytes 4866056 | tf_op jit(solution)/shard_map/ppermute | solution.py:64
  7.3 1.5 %collective-permute-start.2 = (bf16[6144,128]{1,0:T(8,128)(2,1)}, bf16[6144,128]{1,0:T(8,128)(2,1)}, u32[]{:S(2)}, u32[]{:S(2)}) collective-permute-start(bf16[6144,128]{1,0:T(8,128)(2,1)} %get-tuple-element.9.refs_1_.refs_8_), channel_id=1, source_target_pairs={{0,16},{8,24},{16,0},{24,8},{1,17},{9,25},{17,1},{25,9},{2,18},{10... | collective-permute-start | bytes 4718600 | tf_op jit(solution)/shard_map/ppermute | solution.py:64
  9.4 34.5 %collective-permute-done.refs_1_.refs_11_ = bf16[6336,128]{1,0:T(8,128)(2,1)} collective-permute-done((bf16[6336,128]{1,0:T(8,128)(2,1)}, bf16[6336,128]{1,0:T(8,128)(2,1)}, u32[]{:S(2)}, u32[]{:S(2)}) %collective-permute-start) | collective-permute-done | bytes 1622048 | tf_op jit(solution)/shard_map/ppermute | solution.py:64
  43.9 2.1 %collective-permute-start.5 = (bf16[6336,128]{1,0:T(8,128)(2,1)}, bf16[6336,128]{1,0:T(8,128)(2,1)}, u32[]{:S(2)}, u32[]{:S(2)}) collective-permute-start(bf16[6336,128]{1,0:T(8,128)(2,1)} %collective-permute-done.refs_1_.refs_11_), channel_id=1, source_target_pairs={{0,16},{8,24},{16,0},{24,8},{1,17},{9,25},{17,1},{25,9},{2,18},{10... | collective-permute-start | bytes 4866056 | tf_op jit(solution)/shard_map/ppermute | solution.py:64
  47.4 4.2 %copy.7.noise_ref = bf16[128,12480]{1,0:T(8,128)(2,1)S(1)} copy(bf16[128,12480]{0,1:T(8,128)(2,1)} %param.2) | data formatting | bytes 6389760 | tf_op args[0]
  51.7 3.2 %multiply_reduce_fusion = f32[128]{0:T(128)S(1)} fusion(bf16[128,12480]{0,1:T(8,128)(2,1)} %param.2), kind=kLoop, calls=%fused_computation | loop fusion | flops 4792192 | bytes 3195392 | tf_op jit(solution)/shard_map/reduce_sum | solution.py:249
  55.0 2.9 %shard_map.42.refs_0_ = f32[128,128]{1,0:T(8,128)S(1)} custom-call(bf16[128,12480]{1,0:T(8,128)(2,1)S(1)} %copy.7.noise_ref, f32[128,128]{1,0:T(8,128)S(1)} %broadcast_in_dim.4.refs_0_, bf16[6144,128]{1,0:T(8,128)(2,1)S(1)} %copy-done.1, bf16[6336,128]{1,0:T(8,128)(2,1)S(1)} %copy-done), custom_call_target="tpu_custom_call" | custom-call | flops 408944640 | bytes 6389760 | tf_op jit(solution)/shard_map/pallas_call | solution.py:137
  57.9 2.8 %shard_map.44.refs_3_ = f32[128,128]{1,0:T(8,128)S(1)} custom-call(bf16[128,12480]{1,0:T(8,128)(2,1)S(1)} %copy.7.noise_ref, f32[128,128]{1,0:T(8,128)S(1)} %broadcast_in_dim.4.refs_0_, bf16[6144,128]{1,0:T(8,128)(2,1)} %collective-permute-done.2.refs_1_.refs_12_), custom_call_target="tpu_custom_call" | custom-call | flops 201326592 | bytes 3145728 | tf_op jit(solution)/shard_map/pallas_call | solution.py:137
  60.7 2.9 %shard_map.43.refs_1_ = f32[128,128]{1,0:T(8,128)S(1)} custom-call(bf16[128,12480]{1,0:T(8,128)(2,1)S(1)} %copy.7.noise_ref, f32[128,128]{1,0:T(8,128)S(1)} %broadcast_in_dim.4.refs_0_, bf16[6336,128]{1,0:T(8,128)(2,1)} %collective-permute-done.refs_1_.refs_11_), custom_call_target="tpu_custom_call" | custom-call | flops 207618048 | bytes 3244032 | tf_op jit(solution)/shard_map/pallas_call | solution.py:137
  63.6 13.9 %collective-permute-done.1.refs_2_.refs_10_ = bf16[6144,128]{1,0:T(8,128)(2,1)} collective-permute-done((bf16[6144,128]{1,0:T(8,128)(2,1)}, bf16[6144,128]{1,0:T(8,128)(2,1)}, u32[]{:S(2)}, u32[]{:S(2)}) %collective-permute-start.1) | collective-permute-done | bytes 1572896 | tf_op jit(solution)/shard_map/ppermute | solution.py:64
  77.6 2.1 %collective-permute-done.3.refs_4_.refs_13_ = bf16[6336,128]{1,0:T(8,128)(2,1)} collective-permute-done((bf16[6336,128]{1,0:T(8,128)(2,1)}, bf16[6336,128]{1,0:T(8,128)(2,1)}, u32[]{:S(2)}, u32[]{:S(2)}) %collective-permute-start.3) | collective-permute-done | bytes 1622048 | tf_op jit(solution)/shard_map/ppermute | solution.py:64
  79.7 4.8 %shard_map.45 = f32[128,384]{1,0:T(8,128)S(1)} custom-call(bf16[128,12480]{1,0:T(8,128)(2,1)S(1)} %copy.7.noise_ref, f32[128,128]{1,0:T(8,128)S(1)} %shard_map.42.refs_0_, f32[128,128]{1,0:T(8,128)S(1)} %shard_map.43.refs_1_, bf16[6144,128]{1,0:T(8,128)(2,1)} %collective-permute-done.1.refs_2_.refs_10_, f32[128,128]{1,0:T(8,128)S(1)} %shard_map.44.refs_3_, ...), custom_call_target="tpu_custom_call" | custom-call | flops 408944640 | bytes 6389760 | tf_op jit(solution)/shard_map/pallas_call | solution.py:137
  84.5 13.0 %all_to_all.14 = f32[8,16,384]{2,1,0:T(8,128)S(1)} all-to-all(f32[8,16,384]{2,1,0:T(8,128)S(1)} %bitcast.6), channel_id=1, replica_groups=mesh['batch'=4,'group'=8] {'group'}, dimensions={0} | all-to-all | bytes 393216 | tf_op jit(solution)/shard_map/all_to_all | solution.py:255
  97.5 10.7 %all_to_all.15 = f32[8,16,384]{2,1,0:T(8,128)S(1)} all-to-all(f32[8,16,384]{2,1,0:T(8,128)S(1)} %broadcast_in_dim.5), channel_id=1, replica_groups=mesh['batch'=4,'group'=8] {'group'}, dimensions={0} | all-to-all | bytes 393216 | tf_op jit(solution)/shard_map/all_to_all | solution.py:261
  108.3 2.2 %collective-permute-done.4.refs_1_.refs_14_ = bf16[6144,128]{1,0:T(8,128)(2,1)} collective-permute-done((bf16[6144,128]{1,0:T(8,128)(2,1)}, bf16[6144,128]{1,0:T(8,128)(2,1)}, u32[]{:S(2)}, u32[]{:S(2)}) %collective-permute-start.4) | collective-permute-done | bytes 1572896 | tf_op jit(solution)/shard_map/ppermute | solution.py:64
  110.5 2.5 %collective-permute-done.5.refs_2_.refs_15_ = bf16[6336,128]{1,0:T(8,128)(2,1)} collective-permute-done((bf16[6336,128]{1,0:T(8,128)(2,1)}, bf16[6336,128]{1,0:T(8,128)(2,1)}, u32[]{:S(2)}, u32[]{:S(2)}) %collective-permute-start.5) | collective-permute-done | bytes 1622048 | tf_op jit(solution)/shard_map/ppermute | solution.py:64
  113.0 4.8 %shard_map.46 = f32[128,128]{1,0:T(8,128)S(1)} custom-call(bf16[128,12480]{1,0:T(8,128)(2,1)S(1)} %copy.7.noise_ref, f32[128,128]{1,0:T(8,128)S(1)} %broadcast_in_dim.4.refs_0_, bf16[6144,128]{1,0:T(8,128)(2,1)} %collective-permute-done.4.refs_1_.refs_14_, bf16[6336,128]{1,0:T(8,128)(2,1)} %collective-permute-done.5.refs_2_.refs_15_), custom_call_target="tpu_custom_call" | custom-call | flops 408944640 | bytes 6389760 | tf_op jit(solution)/shard_map/pallas_call | solution.py:137
  117.8 1.6 %collective-permute-start.8 = (f32[128,384]{1,0:T(8,128)S(1)}, f32[128,384]{1,0:T(8,128)S(1)}, u32[]{:S(2)}, u32[]{:S(2)}) collective-permute-start(f32[128,384]{1,0:T(8,128)S(1)} %bitcast.8), channel_id=1, source_target_pairs={{0,24},{8,16},{16,8},{24,0},{1,25},{9,17},{17,9},{25,1},{2,26},{10... | collective-permute-start | bytes 589832 | tf_op jit(solution)/shard_map/ppermute | solution.py:64
  119.4 1.6 %collective-permute-start.10 = (f32[128,128]{1,0:T(8,128)S(1)}, f32[128,128]{1,0:T(8,128)S(1)}, u32[]{:S(2)}, u32[]{:S(2)}) collective-permute-start(f32[128,128]{1,0:T(8,128)S(1)} %add.9), channel_id=1, source_target_pairs={{0,2},{1,3},{2,0},{3,1},{4,6},{5,7},{6,4},{7,5},{8,10},{9,11},{10,... | collective-permute-start | bytes 196616 | tf_op jit(solution)/shard_map/ppermute | solution.py:291
  123.7 2.7 %collective-permute-start.11 = (f32[128,128]{1,0:T(8,128)S(1)}, f32[128,128]{1,0:T(8,128)S(1)}, u32[]{:S(2)}, u32[]{:S(2)}) collective-permute-start(f32[128,128]{1,0:T(8,128)S(1)} %add.10), channel_id=1, source_target_pairs={{0,4},{1,5},{2,6},{3,7},{4,0},{5,1},{6,2},{7,3},{8,12},{9,13},{10,... | collective-permute-start | bytes 196616 | tf_op jit(solution)/shard_map/ppermute | solution.py:291
  126.4 2.6 %collective-permute-done.11 = f32[128,128]{1,0:T(8,128)S(1)} collective-permute-done((f32[128,128]{1,0:T(8,128)S(1)}, f32[128,128]{1,0:T(8,128)S(1)}, u32[]{:S(2)}, u32[]{:S(2)}) %collective-permute-start.11) | collective-permute-done | bytes 65568 | tf_op jit(solution)/shard_map/ppermute | solution.py:291
  132.6 1.7 %collective-permute-done.14.refs_7_ = f32[128,128]{1,0:T(8,128)S(1)} collective-permute-done((f32[128,128]{1,0:T(8,128)S(1)}, f32[128,128]{1,0:T(8,128)S(1)}, u32[]{:S(2)}, u32[]{:S(2)}) %collective-permute-start.14) | collective-permute-done | bytes 65568 | tf_op jit(solution)/shard_map/ppermute | solution.py:64
  136.9 12.3 %shard_map.47 = (bf16[12480,128]{1,0:T(8,128)(2,1)}, f32[1,512]{1,0:T(1,128)}) custom-call(s32[1]{0:T(128)} %bitcast.own_ref, f32[128,384]{1,0:T(8,128)} %bitcast.11, f32[128,384]{1,0:T(8,128)} %copy-done.6, f32[128,384]{1,0:T(8,128)} %copy-done.5, f32[128,384]{1,0:T(8,128)} %copy-done.4, f32[128,128]{1,0:T(8,128)} %copy-done.3, f32[128,128]{1,0:T(8,128)} %copy-done.9, ...), custom_call_target="tpu_custom_call" | custom-call | flops 1635778560 | bytes 15974400 | tf_op jit(solution)/shard_map/pallas_call | solution.py:225
  (43 shorter events, 11.2 us)
Async XLA Ops:
  4.3 39.6 %collective-permute-start = (bf16[6336,128]{1,0:T(8,128)(2,1)}, bf16[6336,128]{1,0:T(8,128)(2,1)}, u32[]{:S(2)}, u32[]{:S(2)}) collective-permute-start(bf16[6336,128]{1,0:T(8,128)(2,1)} %get-tuple-element.10.refs_2_.refs_9_), channel_id=1, source_target_pairs={{0,8},{8,0},{16,24},{24,16},{1,9},{9,1},{17,25},{25,17},{2,10},{10... | collective-permute-start | bytes 4866056 | tf_op jit(solution)/shard_map/ppermute | solution.py:64
  7.3 38.7 %collective-permute-start.2 = (bf16[6144,128]{1,0:T(8,128)(2,1)}, bf16[6144,128]{1,0:T(8,128)(2,1)}, u32[]{:S(2)}, u32[]{:S(2)}) collective-permute-start(bf16[6144,128]{1,0:T(8,128)(2,1)} %get-tuple-element.9.refs_1_.refs_8_), channel_id=1, source_target_pairs={{0,16},{8,24},{16,0},{24,8},{1,17},{9,25},{17,1},{25,9},{2,18},{10... | collective-permute-start | bytes 4718600 | tf_op jit(solution)/shard_map/ppermute | solution.py:64
  8.8 70.9 %collective-permute-start.3 = (bf16[6336,128]{1,0:T(8,128)(2,1)}, bf16[6336,128]{1,0:T(8,128)(2,1)}, u32[]{:S(2)}, u32[]{:S(2)}) collective-permute-start(bf16[6336,128]{1,0:T(8,128)(2,1)} %get-tuple-element.10.refs_2_.refs_9_), channel_id=1, source_target_pairs={{0,16},{8,24},{16,0},{24,8},{1,17},{9,25},{17,1},{25,9},{2,18},{10... | collective-permute-start | bytes 4866056 | tf_op jit(solution)/shard_map/ppermute | solution.py:64
  9.3 68.3 %collective-permute-start.1 = (bf16[6144,128]{1,0:T(8,128)(2,1)}, bf16[6144,128]{1,0:T(8,128)(2,1)}, u32[]{:S(2)}, u32[]{:S(2)}) collective-permute-start(bf16[6144,128]{1,0:T(8,128)(2,1)} %get-tuple-element.9.refs_1_.refs_8_), channel_id=1, source_target_pairs={{0,8},{8,0},{16,24},{24,16},{1,9},{9,1},{17,25},{25,17},{2,10},{10... | collective-permute-start | bytes 4718600 | tf_op jit(solution)/shard_map/ppermute | solution.py:64
  43.9 69.1 %collective-permute-start.5 = (bf16[6336,128]{1,0:T(8,128)(2,1)}, bf16[6336,128]{1,0:T(8,128)(2,1)}, u32[]{:S(2)}, u32[]{:S(2)}) collective-permute-start(bf16[6336,128]{1,0:T(8,128)(2,1)} %collective-permute-done.refs_1_.refs_11_), channel_id=1, source_target_pairs={{0,16},{8,24},{16,0},{24,8},{1,17},{9,25},{17,1},{25,9},{2,18},{10... | collective-permute-start | bytes 4866056 | tf_op jit(solution)/shard_map/ppermute | solution.py:64
  46.0 64.5 %collective-permute-start.4 = (bf16[6144,128]{1,0:T(8,128)(2,1)}, bf16[6144,128]{1,0:T(8,128)(2,1)}, u32[]{:S(2)}, u32[]{:S(2)}) collective-permute-start(bf16[6144,128]{1,0:T(8,128)(2,1)} %collective-permute-done.2.refs_1_.refs_12_), channel_id=1, source_target_pairs={{0,8},{8,0},{16,24},{24,16},{1,9},{9,1},{17,25},{25,17},{2,10},{10... | collective-permute-start | bytes 4718600 | tf_op jit(solution)/shard_map/ppermute | solution.py:64
  51.6 3.3 %copy-start = (bf16[6336,128]{1,0:T(8,128)(2,1)S(1)}, bf16[6336,128]{1,0:T(8,128)(2,1)}, u32[]{:S(2)}) copy-start(bf16[6336,128]{1,0:T(8,128)(2,1)} %get-tuple-element.10.refs_2_.refs_9_) | copy-start | bytes 4866052
  51.7 3.3 %copy-start.1 = (bf16[6144,128]{1,0:T(8,128)(2,1)S(1)}, bf16[6144,128]{1,0:T(8,128)(2,1)}, u32[]{:S(2)}) copy-start(bf16[6144,128]{1,0:T(8,128)(2,1)} %get-tuple-element.9.refs_1_.refs_8_) | copy-start | bytes 4718596
  108.3 14.0 %copy-start.2 = (f32[8,16,384]{2,1,0:T(8,128)}, f32[8,16,384]{2,1,0:T(8,128)S(1)}, u32[]{:S(2)}) copy-start(f32[8,16,384]{2,1,0:T(8,128)S(1)} %all_to_all.15) | copy-start | bytes 589828
  117.7 1.6 %collective-permute-start.9 = (f32[128,128]{1,0:T(8,128)S(1)}, f32[128,128]{1,0:T(8,128)S(1)}, u32[]{:S(2)}, u32[]{:S(2)}) collective-permute-start(f32[128,128]{1,0:T(8,128)S(1)} %shard_map.46), channel_id=1, source_target_pairs={{0,1},{1,0},{2,3},{3,2},{4,5},{5,4},{6,7},{7,6},{8,9},{9,8},{10,11... | collective-permute-start | bytes 196616 | tf_op jit(solution)/shard_map/ppermute | solution.py:291
  117.8 14.2 %collective-permute-start.8 = (f32[128,384]{1,0:T(8,128)S(1)}, f32[128,384]{1,0:T(8,128)S(1)}, u32[]{:S(2)}, u32[]{:S(2)}) collective-permute-start(f32[128,384]{1,0:T(8,128)S(1)} %bitcast.8), channel_id=1, source_target_pairs={{0,24},{8,16},{16,8},{24,0},{1,25},{9,17},{17,9},{25,1},{2,26},{10... | collective-permute-start | bytes 589832 | tf_op jit(solution)/shard_map/ppermute | solution.py:64
  119.4 4.3 %collective-permute-start.10 = (f32[128,128]{1,0:T(8,128)S(1)}, f32[128,128]{1,0:T(8,128)S(1)}, u32[]{:S(2)}, u32[]{:S(2)}) collective-permute-start(f32[128,128]{1,0:T(8,128)S(1)} %add.9), channel_id=1, source_target_pairs={{0,2},{1,3},{2,0},{3,1},{4,6},{5,7},{6,4},{7,5},{8,10},{9,11},{10,... | collective-permute-start | bytes 196616 | tf_op jit(solution)/shard_map/ppermute | solution.py:291
  121.0 11.6 %collective-permute-start.7 = (f32[128,384]{1,0:T(8,128)S(1)}, f32[128,384]{1,0:T(8,128)S(1)}, u32[]{:S(2)}, u32[]{:S(2)}) collective-permute-start(f32[128,384]{1,0:T(8,128)S(1)} %bitcast.9), channel_id=1, source_target_pairs={{0,16},{8,24},{16,0},{24,8},{1,17},{9,25},{17,1},{25,9},{2,18},{10... | collective-permute-start | bytes 589832 | tf_op jit(solution)/shard_map/ppermute | solution.py:64
  122.2 10.4 %collective-permute-start.6 = (f32[128,384]{1,0:T(8,128)S(1)}, f32[128,384]{1,0:T(8,128)S(1)}, u32[]{:S(2)}, u32[]{:S(2)}) collective-permute-start(f32[128,384]{1,0:T(8,128)S(1)} %bitcast.10), channel_id=1, source_target_pairs={{0,8},{8,0},{16,24},{24,16},{1,9},{9,1},{17,25},{25,17},{2,10},{10... | collective-permute-start | bytes 589832 | tf_op jit(solution)/shard_map/ppermute | solution.py:64
  123.7 5.3 %collective-permute-start.11 = (f32[128,128]{1,0:T(8,128)S(1)}, f32[128,128]{1,0:T(8,128)S(1)}, u32[]{:S(2)}, u32[]{:S(2)}) collective-permute-start(f32[128,128]{1,0:T(8,128)S(1)} %add.10), channel_id=1, source_target_pairs={{0,4},{1,5},{2,6},{3,7},{4,0},{5,1},{6,2},{7,3},{8,12},{9,13},{10,... | collective-permute-start | bytes 196616 | tf_op jit(solution)/shard_map/ppermute | solution.py:291
  129.0 7.3 %copy-start.3 = (f32[128,128]{1,0:T(8,128)}, f32[128,128]{1,0:T(8,128)S(1)}, u32[]{:S(2)}) copy-start(f32[128,128]{1,0:T(8,128)S(1)} %add.11.refs_4_) | copy-start | bytes 196612
  129.0 5.2 %collective-permute-start.14 = (f32[128,128]{1,0:T(8,128)S(1)}, f32[128,128]{1,0:T(8,128)S(1)}, u32[]{:S(2)}, u32[]{:S(2)}) collective-permute-start(f32[128,128]{1,0:T(8,128)S(1)} %add.11.refs_4_), channel_id=1, source_target_pairs={{0,24},{8,16},{16,8},{24,0},{1,25},{9,17},{17,9},{25,1},{2,26},{10... | collective-permute-start | bytes 196616 | tf_op jit(solution)/shard_map/ppermute | solution.py:64
  130.5 4.4 %collective-permute-start.13 = (f32[128,128]{1,0:T(8,128)S(1)}, f32[128,128]{1,0:T(8,128)S(1)}, u32[]{:S(2)}, u32[]{:S(2)}) collective-permute-start(f32[128,128]{1,0:T(8,128)S(1)} %add.11.refs_4_), channel_id=1, source_target_pairs={{0,16},{8,24},{16,0},{24,8},{1,17},{9,25},{17,1},{25,9},{2,18},{10... | collective-permute-start | bytes 196616 | tf_op jit(solution)/shard_map/ppermute | solution.py:64
  132.1 4.3 %copy-start.4 = (f32[128,384]{1,0:T(8,128)}, f32[128,384]{1,0:T(8,128)S(1)}, u32[]{:S(2)}) copy-start(f32[128,384]{1,0:T(8,128)S(1)} %collective-permute-done.8.refs_3_) | copy-start | bytes 589828
  132.1 4.3 %collective-permute-start.12 = (f32[128,128]{1,0:T(8,128)S(1)}, f32[128,128]{1,0:T(8,128)S(1)}, u32[]{:S(2)}, u32[]{:S(2)}) collective-permute-start(f32[128,128]{1,0:T(8,128)S(1)} %add.11.refs_4_), channel_id=1, source_target_pairs={{0,8},{8,0},{16,24},{24,16},{1,9},{9,1},{17,25},{25,17},{2,10},{10... | collective-permute-start | bytes 196616 | tf_op jit(solution)/shard_map/ppermute | solution.py:64
  132.6 3.7 %copy-start.5 = (f32[128,384]{1,0:T(8,128)}, f32[128,384]{1,0:T(8,128)S(1)}, u32[]{:S(2)}) copy-start(f32[128,384]{1,0:T(8,128)S(1)} %collective-permute-done.7.refs_2_) | copy-start | bytes 589828
  132.6 3.7 %copy-start.6 = (f32[128,384]{1,0:T(8,128)}, f32[128,384]{1,0:T(8,128)S(1)}, u32[]{:S(2)}) copy-start(f32[128,384]{1,0:T(8,128)S(1)} %collective-permute-done.6.refs_1_) | copy-start | bytes 589828
  134.3 2.1 %copy-start.7 = (f32[128,128]{1,0:T(8,128)}, f32[128,128]{1,0:T(8,128)S(1)}, u32[]{:S(2)}) copy-start(f32[128,128]{1,0:T(8,128)S(1)} %collective-permute-done.14.refs_7_) | copy-start | bytes 196612
  135.0 1.4 copy-start.8
  (1 other events, 0.6 us)

commit v2 on v1

v2 whole, which is shorter than its diff:
```python
import functools

import jax
import jax.numpy as jnp
from jax import lax
from jax.experimental import pallas as pl
from jax.experimental.pallas import tpu as pltpu
from jax.sharding import PartitionSpec as P

ITERS = 4
FEAT = 99840


def combined_all(value, axis, join):
    pieces = jax.tree.map(lambda part: lax.all_gather(part, axis), value)
    head = jax.tree.map(lambda part: part[0], pieces)
    tail = jax.tree.map(lambda part: part[1:], pieces)
    total, _ = lax.scan(lambda total, slab: (join(total, slab), None), head, tail)
    return total


def combine_parts(first, second):
    top = jnp.maximum(first[0], second[0])
    total = first[1] * jnp.exp(first[0] - top) + second[1] * jnp.exp(second[0] - top)
    return (top, total)


def local_parts(values, axis):
    top = jnp.max(values, axis=axis)
    total = jnp.sum(jnp.exp(values - jnp.expand_dims(top, axis)), axis=axis)
    return (top, total)


def local_any(noise, data):
    eps = 2.0 / jnp.sqrt(jnp.float32(FEAT))
    batch_total = noise.shape[0] * lax.axis_size("batch")
    loga = -jnp.log(jnp.float32(batch_total))
    noise_sq = jnp.sum(jnp.square(noise.astype(jnp.float32)), axis=1)
    all_rows = lax.all_gather(data, "batch", axis=0, tiled=True)
    piece_sq = jnp.sum(jnp.square(all_rows.astype(jnp.float32)), axis=1)
    cross = lax.dot_general(
        noise, all_rows, (((1,), (1,)), ((), ())), preferred_element_type=jnp.float32
    )
    partial_value = noise_sq[:, None] + piece_sq[None, :] - 2.0 * cross
    cost = lax.psum(partial_value, "group") / jnp.float32(FEAT)
    potential = jnp.zeros((batch_total,), jnp.float32)
    for step in range(ITERS):
        top, total = local_parts((potential[None, :] - cost) / eps, 1)
        rowpot = eps * loga - eps * (top + jnp.log(total))
        parts = local_parts((rowpot[:, None] - cost) / eps, 0)
        top, total = combined_all(parts, "batch", combine_parts)
        potential = eps * loga - eps * (top + jnp.log(total))
    scores = (potential[None, :] - cost) / eps
    top, total = local_parts(scores, 1)
    weights = jnp.exp(scores - (top + jnp.log(total))[:, None]).astype(jnp.bfloat16)
    targets = jnp.dot(weights, all_rows, preferred_element_type=jnp.float32)
    return (targets.astype(jnp.bfloat16), potential)


X, Y, DIAG = 1, 2, 3


def swap(value, way):
    return lax.ppermute(value, "batch", [(i, i ^ way) for i in range(4)])


VMEM = pl.BlockSpec(memory_space=pltpu.VMEM)
SMEM = pl.BlockSpec(memory_space=pltpu.SMEM)
HBM = pl.BlockSpec(memory_space=pltpu.HBM)


PARTS = 4


def cross_kernel(spans, noise_ref, *refs):
    *refs, out_ref = refs
    width = noise_ref.shape[0]
    for k, block_spans in enumerate(spans):
        (prior_ref, *pieces), refs = refs[: 1 + len(block_spans)], refs[1 + len(block_spans):]
        total = prior_ref[...]
        for (start, size), piece_ref in zip(block_spans, pieces):
            step = -(-size // (PARTS * 128)) * 128
            sums = []
            for at in range(0, size, step):
                deep = min(step, size - at)
                piece = piece_ref[at : at + deep, :]
                noise = noise_ref[:, start + at : start + at + deep]
                cross = jnp.dot(noise, piece, preferred_element_type=jnp.float32)
                square = jnp.sum(jnp.square(piece.astype(jnp.float32)), axis=0, keepdims=True)
                sums.append(square - 2.0 * cross)
            total = total + functools.reduce(lambda first, second: first + second, sums)
        out_ref[:, k * width : (k + 1) * width] = total


def crossed(noise, *blocks):
    rows = noise.shape[0]
    spans = [block[2::2] for block in blocks]
    values = [value for block in blocks for value in (block[0],) + block[1::2]]
    flops = sum(2 * rows * rows * size for block_spans in spans for _, size in block_spans)
    return pl.pallas_call(
        functools.partial(cross_kernel, spans),
        out_shape=jax.ShapeDtypeStruct((rows, rows * len(blocks)), jnp.float32),
        in_specs=[VMEM] * (1 + len(values)),
        out_specs=VMEM,
        compiler_params=pltpu.CompilerParams(vmem_limit_bytes=16 * 2**20),
        cost_estimate=pl.CostEstimate(flops=flops, bytes_accessed=flops // 64, transcendentals=0),
    )(noise, *values)


STEP = 64
TILES = 5


def pair_kernel(rows, feats, places, index_ref, *refs):
    early_refs, late_refs, refs = (refs[:4], refs[4:8]), refs[8:10], refs[10:]
    pieces, refs = refs[: len(places)], refs[len(places):]
    targets_ref, potential_ref, blocks, held, scores, out, in_sem, out_sem = refs
    batch = 4 * rows
    eps = 2.0 / FEAT**0.5
    scale = -1.0 / (FEAT * eps)
    loga = -jnp.log(jnp.float32(batch))
    own, core = index_ref[0], index_ref[1]
    half = rows // 2

    loads = []
    for k, (start, r) in enumerate(places):
        copy = pltpu.make_async_copy(
            pieces[k],
            held.at[pl.ds(start, pieces[k].shape[0]), pl.ds(r * rows, rows)],
            in_sem.at[k],
        )
        copy.start()
        loads.append(copy)

    def block(i):
        return pl.ds(pl.multiple_of(i * rows, rows), rows)

    for p in range(4):
        for side in range(2):
            part = pl.ds(p * half, half)
            into = pl.ds(pl.multiple_of((own ^ p) * rows + (core ^ side) * half, half), half)
            for r in range(DIAG):
                blocks[into, block(own ^ (p ^ r))] = early_refs[side][p][:, block(r)] * scale
            blocks[into, block(own ^ (p ^ DIAG))] = late_refs[side][part, :] * scale

    def sweep(_, v):
        u = []
        top = jnp.full((1, batch), -jnp.inf, jnp.float32)
        for c in range(batch // STEP):
            k = blocks[pl.ds(c * STEP, STEP), :]
            a = k + v
            m = jnp.max(a, axis=1, keepdims=True)
            s = jnp.sum(jnp.exp(a - m), axis=1, keepdims=True)
            u.append(loga - (m + jnp.log(s)))
            top = jnp.maximum(top, jnp.max(k + u[-1], axis=0, keepdims=True))
        total = jnp.zeros((1, batch), jnp.float32)
        for c in range(batch // STEP):
            a = blocks[pl.ds(c * STEP, STEP), :] + u[c]
            total = total + jnp.sum(jnp.exp(a - top), axis=0, keepdims=True)
        return loga - (top + jnp.log(total))

    v = lax.fori_loop(0, ITERS, sweep, jnp.zeros((1, batch), jnp.float32))
    potential_ref[...] = v * eps

    a = blocks[block(own), :] + v
    m = jnp.max(a, axis=1, keepdims=True)
    s = jnp.sum(jnp.exp(a - m), axis=1, keepdims=True)
    scores[...] = jnp.exp(a - (m + jnp.log(s)))
    w = jnp.concatenate([scores[:, block(own ^ r)].T for r in range(4)], axis=0).astype(jnp.bfloat16)
    tile = feats // TILES

    def stored(t):
        part = pl.ds(pl.multiple_of(t * tile, 16), tile)
        return pltpu.make_async_copy(out.at[part, :], targets_ref.at[part, :], out_sem.at[t])

    def multiply(t, _):
        part = pl.ds(pl.multiple_of(t * tile, 16), tile)
        out[part, :] = jnp.dot(held[part, :], w, preferred_element_type=jnp.float32).astype(jnp.bfloat16)
        stored(t).start()
        return 0

    later = max(start for start, _ in places)
    for copy, (start, _) in zip(loads, places):
        if start < later:
            copy.wait()
    lax.fori_loop(0, later // tile, multiply, 0)
    for copy, (start, _) in zip(loads, places):
        if start >= later:
            copy.wait()
    lax.fori_loop(later // tile, TILES, multiply, 0)
    for t in range(TILES):
        stored(t).wait()


def paired(index, early, late, pieces, places, rows, feats):
    batch = 4 * rows
    return pl.pallas_call(
        functools.partial(pair_kernel, rows, feats, places),
        out_shape=(
            jax.ShapeDtypeStruct((feats, rows), jnp.bfloat16),
            jax.ShapeDtypeStruct((1, batch), jnp.float32),
        ),
        in_specs=[SMEM] + [VMEM] * 10 + [HBM] * len(pieces),
        out_specs=(HBM, VMEM),
        scratch_shapes=[
            pltpu.VMEM((batch, batch), jnp.float32),
            pltpu.VMEM((feats, batch), jnp.bfloat16),
            pltpu.VMEM((rows, batch), jnp.float32),
            pltpu.VMEM((feats, rows), jnp.bfloat16),
            pltpu.SemaphoreType.DMA((len(pieces),)),
            pltpu.SemaphoreType.DMA((TILES,)),
        ],
        compiler_params=pltpu.CompilerParams(vmem_limit_bytes=24 * 2**20),
        cost_estimate=pl.CostEstimate(
            flops=2 * rows * batch * feats, bytes_accessed=10 * rows * feats, transcendentals=9 * batch * batch
        ),
    )(index, *early, *late, *pieces)


def squared(values_t):
    return jnp.sum(jnp.square(values_t.astype(jnp.float32)), axis=0)


def turn(value, way):
    groups = lax.axis_size("group")
    return lax.ppermute(value, "group", [(g, g ^ way) for g in range(groups)])


def core_share(value, core):
    half = value.shape[0] // 2
    kept = lax.dynamic_slice_in_dim(value, core * jnp.uint32(half), half)
    given = lax.dynamic_slice_in_dim(value, (1 - core) * jnp.uint32(half), half)
    return kept + turn(given, 1)


def line_sum(value):
    ways = range(2, lax.axis_size("group"), 2)
    terms = [value] + [turn(value, way) for way in ways]
    while len(terms) > 1:
        terms = [first + second for first, second in zip(terms[::2], terms[1::2])]
    return terms[0]


def group_share(value):
    groups = lax.axis_size("group")
    rows, width = value.shape
    share = rows // groups
    parts = value.reshape(2, groups // 2, share, width).transpose(1, 0, 2, 3).reshape(rows, width)
    parts = lax.all_to_all(parts, "group", 0, 0, tiled=True)
    return jnp.sum(parts.reshape(groups, share, width), axis=0)


def line_gather(value, place):
    lines = lax.axis_size("group") // 2
    shares = jnp.stack([value] + [turn(value, 2 * way) for way in range(1, lines)])
    return jnp.concatenate(
        [lax.dynamic_index_in_dim(shares, place ^ jnp.uint32(z), keepdims=False) for z in range(lines)]
    )


def batch_swaps(value):
    return [value, swap(value, X), swap(value, Y), swap(value, DIAG)]


def local_square(noise, data):
    rows, feats = noise.shape
    noise_t, data_t = noise.T, data.T
    own, group = lax.axis_index("batch"), lax.axis_index("group").astype(jnp.uint32)
    core, line = group & 1, group >> 1
    index = jnp.stack([own.astype(jnp.int32), core.astype(jnp.int32)])

    first = feats * 8 // (15 * 128) * 128
    low, high = (0, first), (first, feats - first)
    d_low, d_high = data_t[:first], data_t[first:]
    x_all, y_low, y_high = swap(data_t, X), swap(d_low, Y), swap(d_high, Y)
    start = jnp.broadcast_to(squared(noise_t)[:, None], (rows, rows))
    own_cost = crossed(noise, (start, d_low, low, d_high, high))
    y_cost = crossed(noise, (start, y_low, low))
    y_low, own_cost, y_cost = lax.optimization_barrier((y_low, own_cost, y_cost))
    diag_low = swap(y_low, X)
    x_tail = x_all[first:]
    diag_high = swap(x_tail, Y)
    x_all, y_high, x_tail = lax.optimization_barrier((x_all, y_high, x_tail))
    early = crossed(noise, (own_cost,), (start, x_all, (0, feats)), (y_cost, y_high, high))
    early_half = line_gather(group_share(early), line)
    early_mine = batch_swaps(early_half)
    _, diag_low = lax.optimization_barrier((early_half, diag_low))
    late = crossed(noise, (start, diag_low, low))
    _, diag_high = lax.optimization_barrier((early_half, diag_high))
    late = crossed(noise, (late, diag_high, high))
    late, *early_mine = lax.optimization_barrier((late, *early_mine))
    early_rows = early_mine + [turn(value, 1) for value in early_mine]
    late_half = core_share(late, core)
    late_half, *early_rows = lax.optimization_barrier((late_half, *early_rows))
    late_half = line_sum(late_half)
    late_mine = jnp.concatenate(batch_swaps(late_half))
    late_rows = [late_mine, turn(late_mine, 1)]

    pieces = [d_low, x_all, y_low, diag_low, d_high, y_high, diag_high]
    places = [(0, 0), (0, X), (0, Y), (0, DIAG), (first, 0), (first, Y), (first, DIAG)]
    targets_t, potential = paired(index, early_rows, late_rows, pieces, places, rows, feats)
    return (targets_t.T, potential[0])


def solution(mesh):
    in_specs = (P("batch", "group"), P("batch", "group"))
    out_specs = (P("batch", "group"), P())
    groups = mesh.shape["group"]
    paired_form = mesh.shape["batch"] == 4 and groups > 1 and groups & (groups - 1) == 0
    local = local_square if paired_form else local_any
    return jax.shard_map(local, mesh=mesh, in_specs=in_specs, out_specs=out_specs, check_vma=False)
```

time: 150 us -> 145 us (0.967)
  Pallas kernels: 34.2 us -> 23.4 us
  blocking collectives: 23.7 us -> 13 us
  local copies, waits for them, and re-layouts: 4.89 us -> 12.4 us
  waiting for transfers between devices: 62.2 us -> 66.9 us
  starting transfers between devices: 20.2 us -> 24.7 us
    all_to_all x2 -> x1, blocking collectives: 23.7 us -> 13 us  [group_share(): parts = lax.all_to_all(parts, 'group', 0, 0, tiled=True)]
    slice x0 -> x3, local copies, waits for them, and re-layouts: none -> 8.06 us  [the longest x2 5.47 us: local_square(): d_low, d_high = (data_t[:first], data_t[first:])]
    ppermute x3 -> x12, starting transfers between devices: 4.36 us -> 10.4 us  [turn(): return lax.ppermute(value, 'group', [(g, g ^ way) for g in range(groups)])]
    ppermute x3 -> x12, waiting for transfers between devices: 3.31 us -> 8.63 us  [turn(): return lax.ppermute(value, 'group', [(g, g ^ way) for g in range(groups)])]
    pallas_call x5, Pallas kernels: 18.2 us -> 13.3 us  [crossed(): pl.pallas_call(functools.partial(cross_kernel, spans), out_shape=jax.Shap...]
    pallas_call x1 -> x0, Pallas kernels: 3.63 us -> none  [split(): pl.pallas_call(split_kernel, out_shape=(jax.ShapeDtypeStruct((size, rows)...]
    pallas_call x1, Pallas kernels: 12.3 us -> 10.1 us  [paired(): pl.pallas_call(functools.partial(pair_kernel, rows, feats, places), out_s...]
    ppermute x12 -> x11, starting transfers between devices: 15.8 us -> 14.3 us  [swap(): return lax.ppermute(value, 'batch', [(i, i ^ way) for i in range(4)])]
  transfers between devices with their start and end apart: 15 -> 23, of which waited for: 10 -> 17; matrix products, arithmetic and copies ran while one was open for 5% -> 11% of each run, Pallas kernels for 9% -> 9%
where the time goes in v2:
time: 145 us; the launch traced here: 144 us
  waiting for transfers between devices  66.9 us (46%)
  starting transfers between devices  24.7 us (17%)
  Pallas kernels  23.4 us (16%)
  blocking collectives  13 us (9%)
  local copies, waits for them, and re-layouts  12.4 us (9%)
  other arithmetic  3.22 us (2%)
    ppermute x11, waiting for transfers between devices, swap(): return lax.ppermute(value, 'batch', [(i, i ^ way) for i in range(4)])  58.3 us
    ppermute x11, starting transfers between devices, swap(): return lax.ppermute(value, 'batch', [(i, i ^ way) for i in range(4)])  14.3 us
    pallas_call x5, Pallas kernels, crossed(): pl.pallas_call(functools.partial(cross_kernel, spans), out_shape=jax.Shap...  13.3 us
    all_to_all x1, blocking collectives, group_share(): parts = lax.all_to_all(parts, 'group', 0, 0, tiled=True)  13 us
    ppermute x12, starting transfers between devices, turn(): return lax.ppermute(value, 'group', [(g, g ^ way) for g in range(groups)])  10.4 us
    pallas_call x1, Pallas kernels, paired(): pl.pallas_call(functools.partial(pair_kernel, rows, feats, places), out_s...  10.1 us
    ppermute x12, waiting for transfers between devices, turn(): return lax.ppermute(value, 'group', [(g, g ^ way) for g in range(groups)])  8.63 us
    slice x2, local copies, waits for them, and re-layouts, local_square(): d_low, d_high = (data_t[:first], data_t[first:])  5.47 us
  transfers between devices with their start and end apart: 23, of which 17 were waited for; matrix products, arithmetic and copies ran while one was open for 11% of the time, Pallas kernels for 9%

profile of v2, /device:TPU:0, one launch (start us, length us, event | category | flops | bytes accessed | tf_op | source)
XLA Modules:
  0.0 144.4 jit_solution(15955854311600592041)
XLA Ops:
  0.6 3.0 %collective-permute-start.1 = (bf16[12480,128]{1,0:T(8,128)(2,1)}, bf16[12480,128]{1,0:T(8,128)(2,1)}, u32[]{:S(2)}, u32[]{:S(2)}) collective-permute-start(bf16[12480,128]{1,0:T(8,128)(2,1)} %bitcast.22), channel_id=1, source_target_pairs={{0,8},{8,0},{16,24},{24,16},{1,9},{9,1},{17,25},{25,17},{2,10},{10... | collective-permute-start | bytes 9584648 | tf_op jit(solution)/shard_map/ppermute | solution.py:64
  3.6 2.8 %slice.12.refs_1_.refs_10_ = bf16[6656,128]{1,0:T(8,128)(2,1)} slice(bf16[12480,128]{1,0:T(8,128)(2,1)} %bitcast.23), slice={[0:6656], [0:128]} | slice | bytes 3407872 | tf_op jit(solution)/shard_map/slice | solution.py:274
  6.5 1.5 %collective-permute-start = (bf16[6656,128]{1,0:T(8,128)(2,1)}, bf16[6656,128]{1,0:T(8,128)(2,1)}, u32[]{:S(2)}, u32[]{:S(2)}) collective-permute-start(bf16[6656,128]{1,0:T(8,128)(2,1)} %slice.12.refs_1_.refs_10_), channel_id=1, source_target_pairs={{0,16},{8,24},{16,0},{24,8},{1,17},{9,25},{17,1},{25,9},{2,18},{10... | collective-permute-start | bytes 5111816 | tf_op jit(solution)/shard_map/ppermute | solution.py:64
  8.0 2.6 %slice.13.refs_2_.refs_14_ = bf16[5824,128]{1,0:T(8,128)(2,1)} slice(bf16[12480,128]{1,0:T(8,128)(2,1)} %bitcast.24), slice={[6656:12480], [0:128]} | slice | bytes 2981888 | tf_op jit(solution)/shard_map/slice | solution.py:274
  11.1 4.2 %copy.14.noise_ref = bf16[128,12480]{1,0:T(8,128)(2,1)S(1)} copy(bf16[128,12480]{0,1:T(8,128)(2,1)} %param.2) | data formatting | bytes 6389760 | tf_op args[0]
  15.3 3.1 %multiply_reduce_fusion = f32[128]{0:T(128)S(1)} fusion(bf16[128,12480]{0,1:T(8,128)(2,1)} %param.2), kind=kLoop, calls=%fused_computation | loop fusion | flops 4792192 | bytes 3195392 | tf_op jit(solution)/shard_map/reduce_sum | solution.py:221
  18.5 3.1 %shard_map.41.refs_0_ = f32[128,128]{1,0:T(8,128)S(1)} custom-call(bf16[128,12480]{1,0:T(8,128)(2,1)S(1)} %copy.14.noise_ref, f32[128,128]{1,0:T(8,128)S(1)} %broadcast_in_dim.2.refs_0_.refs_1_, bf16[6656,128]{1,0:T(8,128)(2,1)} %slice.12.refs_1_.refs_10_, bf16[5824,128]{1,0:T(8,128)(2,1)} %slice.13.refs_2_.refs_14_), custom_call_target="tpu_custom_call" | custom-call | flops 408944640 | bytes 6389760 | tf_op jit(solution)/shard_map/pallas_call | solution.py:100
  21.6 25.3 %collective-permute-done.refs_1_.refs_12_ = bf16[6656,128]{1,0:T(8,128)(2,1)} collective-permute-done((bf16[6656,128]{1,0:T(8,128)(2,1)}, bf16[6656,128]{1,0:T(8,128)(2,1)}, u32[]{:S(2)}, u32[]{:S(2)}) %collective-permute-start) | collective-permute-done | bytes 1703968 | tf_op jit(solution)/shard_map/ppermute | solution.py:64
  46.9 2.1 %shard_map.42.refs_3_ = f32[128,128]{1,0:T(8,128)S(1)} custom-call(bf16[128,12480]{1,0:T(8,128)(2,1)S(1)} %copy.14.noise_ref, f32[128,128]{1,0:T(8,128)S(1)} %broadcast_in_dim.2.refs_0_.refs_1_, bf16[6656,128]{1,0:T(8,128)(2,1)} %collective-permute-done.refs_1_.refs_12_), custom_call_target="tpu_custom_call" | custom-call | flops 218103808 | bytes 3407872 | tf_op jit(solution)/shard_map/pallas_call | solution.py:100
  49.1 24.8 %collective-permute-done.1.refs_2_.refs_11_ = bf16[12480,128]{1,0:T(8,128)(2,1)} collective-permute-done((bf16[12480,128]{1,0:T(8,128)(2,1)}, bf16[12480,128]{1,0:T(8,128)(2,1)}, u32[]{:S(2)}, u32[]{:S(2)}) %collective-permute-start.1) | collective-permute-done | bytes 3194912 | tf_op jit(solution)/shard_map/ppermute | solution.py:64
  73.9 2.6 %slice.14 = bf16[5824,128]{1,0:T(8,128)(2,1)} slice(bf16[12480,128]{1,0:T(8,128)(2,1)} %collective-permute-done.1.refs_2_.refs_11_), slice={[6656:12480], [0:128]} | slice | bytes 2981888 | tf_op jit(solution)/shard_map/slice | solution.py:281
  76.5 2.1 %collective-permute-start.7 = (bf16[5824,128]{1,0:T(8,128)(2,1)}, bf16[5824,128]{1,0:T(8,128)(2,1)}, u32[]{:S(2)}, u32[]{:S(2)}) collective-permute-start(bf16[5824,128]{1,0:T(8,128)(2,1)} %slice.14), channel_id=1, source_target_pairs={{0,16},{8,24},{16,0},{24,8},{1,17},{9,25},{17,1},{25,9},{2,18},{10... | collective-permute-start | bytes 4472840 | tf_op jit(solution)/shard_map/ppermute | solution.py:64
  78.6 4.0 %shard_map.43 = f32[128,384]{1,0:T(8,128)S(1)} custom-call(bf16[128,12480]{1,0:T(8,128)(2,1)S(1)} %copy.14.noise_ref, f32[128,128]{1,0:T(8,128)S(1)} %shard_map.41.refs_0_, f32[128,128]{1,0:T(8,128)S(1)} %broadcast_in_dim.2.refs_0_.refs_1_, bf16[12480,128]{1,0:T(8,128)(2,1)} %collective-permute-done.1.refs_2_.refs_11_, f32[128,128]{1,0:T(8,128)S(1)} %shard_map.42.refs_3_, ...), custom_call_target="tpu_custom_call" | custom-call | flops 599785472 | bytes 9371648 | tf_op jit(solution)/shard_map/pallas_call | solution.py:100
  82.7 13.0 %all_to_all.9 = f32[8,16,384]{2,1,0:T(8,128)S(1)} all-to-all(f32[8,16,384]{2,1,0:T(8,128)S(1)} %bitcast.25), channel_id=1, replica_groups=mesh['batch'=4,'group'=8] {'group'}, dimensions={0} | all-to-all | bytes 393216 | tf_op jit(solution)/shard_map/all_to_all | solution.py:249
  97.7 2.5 %collective-permute-start.3 = (f32[16,384]{1,0:T(8,128)S(1)}, f32[16,384]{1,0:T(8,128)S(1)}, u32[]{:S(2)}, u32[]{:S(2)}) collective-permute-start(f32[16,384]{1,0:T(8,128)S(1)} %reduce_sum.19), channel_id=1, source_target_pairs={{0,2},{1,3},{2,0},{3,1},{4,6},{5,7},{6,4},{7,5},{8,10},{9,11},{10,... | collective-permute-start | bytes 73736 | tf_op jit(solution)/shard_map/ppermute | solution.py:226
  103.6 1.5 %collective-permute-start.9 = (f32[64,384]{1,0:T(8,128)S(1)}, f32[64,384]{1,0:T(8,128)}, u32[]{:S(2)}, u32[]{:S(2)}) collective-permute-start(f32[64,384]{1,0:T(8,128)S(1)} %pad_maximum_fusion.2.refs_0_), channel_id=1, source_target_pairs={{0,16},{8,24},{16,0},{24,8},{1,17},{9,25},{17,1},{25,9},{2,18},{10... | collective-permute-start | bytes 294920 | tf_op jit(solution)/shard_map/ppermute | solution.py:64
  105.7 4.8 %collective-permute-done.6.refs_1_.refs_13_ = bf16[6656,128]{1,0:T(8,128)(2,1)} collective-permute-done((bf16[6656,128]{1,0:T(8,128)(2,1)}, bf16[6656,128]{1,0:T(8,128)(2,1)}, u32[]{:S(2)}, u32[]{:S(2)}) %collective-permute-start.6) | collective-permute-done | bytes 1703968 | tf_op jit(solution)/shard_map/ppermute | solution.py:64
  110.4 2.1 %shard_map.44.refs_0_ = f32[128,128]{1,0:T(8,128)S(1)} custom-call(bf16[128,12480]{1,0:T(8,128)(2,1)S(1)} %copy.14.noise_ref, f32[128,128]{1,0:T(8,128)S(1)} %broadcast_in_dim.2.refs_0_.refs_1_, bf16[6656,128]{1,0:T(8,128)(2,1)} %collective-permute-done.6.refs_1_.refs_13_), custom_call_target="tpu_custom_call" | custom-call | flops 218103808 | bytes 3407872 | tf_op jit(solution)/shard_map/pallas_call | solution.py:100
  112.6 2.0 %shard_map.45 = f32[128,128]{1,0:T(8,128)S(1)} custom-call(bf16[128,12480]{1,0:T(8,128)(2,1)S(1)} %copy.14.noise_ref, f32[128,128]{1,0:T(8,128)S(1)} %shard_map.44.refs_0_, bf16[5824,128]{1,0:T(8,128)(2,1)} %collective-permute-done.7.refs_1_.refs_16_), custom_call_target="tpu_custom_call" | custom-call | flops 190840832 | bytes 2981888 | tf_op jit(solution)/shard_map/pallas_call | solution.py:100
  117.0 4.2 %collective-permute-start.18 = (f32[64,128]{1,0:T(8,128)S(1)}, f32[64,128]{1,0:T(8,128)S(1)}, u32[]{:S(2)}, u32[]{:S(2)}) collective-permute-start(f32[64,128]{1,0:T(8,128)S(1)} %dynamic-slice_add_fusion), channel_id=1, source_target_pairs={{0,6},{1,7},{2,4},{3,5},{4,2},{5,3},{6,0},{7,1},{8,14},{9,15},{10,... | collective-permute-start | bytes 98312 | tf_op jit(solution)/shard_map/ppermute | solution.py:226
  123.1 2.9 %collective-permute-done.17 = f32[64,128]{1,0:T(8,128)S(1)} collective-permute-done((f32[64,128]{1,0:T(8,128)S(1)}, f32[64,128]{1,0:T(8,128)S(1)}, u32[]{:S(2)}, u32[]{:S(2)}) %collective-permute-start.17) | collective-permute-done | bytes 32800 | tf_op jit(solution)/shard_map/ppermute | solution.py:226
  126.0 2.5 %collective-permute-start.21 = (f32[64,128]{1,0:T(8,128)S(1)}, f32[64,128]{1,0:T(8,128)S(1)}, u32[]{:S(2)}, u32[]{:S(2)}) collective-permute-start(f32[64,128]{1,0:T(8,128)S(1)} %add_add_fusion), channel_id=1, source_target_pairs={{0,24},{8,16},{16,8},{24,0},{1,25},{9,17},{17,9},{25,1},{2,26},{10... | collective-permute-start | bytes 98312 | tf_op jit(solution)/shard_map/ppermute | solution.py:64
  130.9 1.5 %collective-permute-done.20 = f32[64,128]{1,0:T(8,128)S(1)} collective-permute-done((f32[64,128]{1,0:T(8,128)S(1)}, f32[64,128]{1,0:T(8,128)S(1)}, u32[]{:S(2)}, u32[]{:S(2)}) %collective-permute-start.20) | collective-permute-done | bytes 32800 | tf_op jit(solution)/shard_map/ppermute | solution.py:64
  134.3 10.1 %shard_map.46 = (bf16[12480,128]{1,0:T(8,128)(2,1)}, f32[1,512]{1,0:T(1,128)}) custom-call(s32[2]{0:T(128)S(1)} %pad_add_fusion.index_ref, f32[64,384]{1,0:T(8,128)S(1)} %pad_maximum_fusion.2.refs_0_, f32[64,384]{1,0:T(8,128)} %collective-permute-done.8.refs_1_, f32[64,384]{1,0:T(8,128)} %collective-permute-done.9.refs_2_, ...), custom_call_target="tpu_custom_call" | custom-call | flops 1635778560 | bytes 15974400 | tf_op jit(solution)/shard_map/pallas_call | solution.py:197
  (45 shorter events, 15.2 us)
Async XLA Ops:
  0.6 73.3 %collective-permute-start.1 = (bf16[12480,128]{1,0:T(8,128)(2,1)}, bf16[12480,128]{1,0:T(8,128)(2,1)}, u32[]{:S(2)}, u32[]{:S(2)}) collective-permute-start(bf16[12480,128]{1,0:T(8,128)(2,1)} %bitcast.22), channel_id=1, source_target_pairs={{0,8},{8,0},{16,24},{24,16},{1,9},{9,1},{17,25},{25,17},{2,10},{10... | collective-permute-start | bytes 9584648 | tf_op jit(solution)/shard_map/ppermute | solution.py:64
  6.5 40.4 %collective-permute-start = (bf16[6656,128]{1,0:T(8,128)(2,1)}, bf16[6656,128]{1,0:T(8,128)(2,1)}, u32[]{:S(2)}, u32[]{:S(2)}) collective-permute-start(bf16[6656,128]{1,0:T(8,128)(2,1)} %slice.12.refs_1_.refs_10_), channel_id=1, source_target_pairs={{0,16},{8,24},{16,0},{24,8},{1,17},{9,25},{17,1},{25,9},{2,18},{10... | collective-permute-start | bytes 5111816 | tf_op jit(solution)/shard_map/ppermute | solution.py:64
  10.6 68.0 %collective-permute-start.2 = (bf16[5824,128]{1,0:T(8,128)(2,1)}, bf16[5824,128]{1,0:T(8,128)(2,1)}, u32[]{:S(2)}, u32[]{:S(2)}) collective-permute-start(bf16[5824,128]{1,0:T(8,128)(2,1)} %slice.13.refs_2_.refs_14_), channel_id=1, source_target_pairs={{0,16},{8,24},{16,0},{24,8},{1,17},{9,25},{17,1},{25,9},{2,18},{10... | collective-permute-start | bytes 4472840 | tf_op jit(solution)/shard_map/ppermute | solution.py:64
  49.0 61.4 %collective-permute-start.6 = (bf16[6656,128]{1,0:T(8,128)(2,1)}, bf16[6656,128]{1,0:T(8,128)(2,1)}, u32[]{:S(2)}, u32[]{:S(2)}) collective-permute-start(bf16[6656,128]{1,0:T(8,128)(2,1)} %collective-permute-done.refs_1_.refs_12_), channel_id=1, source_target_pairs={{0,8},{8,0},{16,24},{24,16},{1,9},{9,1},{17,25},{25,17},{2,10},{10... | collective-permute-start | bytes 5111816 | tf_op jit(solution)/shard_map/ppermute | solution.py:64
  76.5 36.0 %collective-permute-start.7 = (bf16[5824,128]{1,0:T(8,128)(2,1)}, bf16[5824,128]{1,0:T(8,128)(2,1)}, u32[]{:S(2)}, u32[]{:S(2)}) collective-permute-start(bf16[5824,128]{1,0:T(8,128)(2,1)} %slice.14), channel_id=1, source_target_pairs={{0,16},{8,24},{16,0},{24,8},{1,17},{9,25},{17,1},{25,9},{2,18},{10... | collective-permute-start | bytes 4472840 | tf_op jit(solution)/shard_map/ppermute | solution.py:64
  95.7 5.7 %collective-permute-start.5 = (f32[16,384]{1,0:T(8,128)S(1)}, f32[16,384]{1,0:T(8,128)S(1)}, u32[]{:S(2)}, u32[]{:S(2)}) collective-permute-start(f32[16,384]{1,0:T(8,128)S(1)} %reduce_sum.19), channel_id=1, source_target_pairs={{0,6},{1,7},{2,4},{3,5},{4,2},{5,3},{6,0},{7,1},{8,14},{9,15},{10,... | collective-permute-start | bytes 73736 | tf_op jit(solution)/shard_map/ppermute | solution.py:226
  97.0 4.9 %collective-permute-start.4 = (f32[16,384]{1,0:T(8,128)S(1)}, f32[16,384]{1,0:T(8,128)S(1)}, u32[]{:S(2)}, u32[]{:S(2)}) collective-permute-start(f32[16,384]{1,0:T(8,128)S(1)} %reduce_sum.19), channel_id=1, source_target_pairs={{0,4},{1,5},{2,6},{3,7},{4,0},{5,1},{6,2},{7,3},{8,12},{9,13},{10,... | collective-permute-start | bytes 73736 | tf_op jit(solution)/shard_map/ppermute | solution.py:226
  97.7 4.4 %collective-permute-start.3 = (f32[16,384]{1,0:T(8,128)S(1)}, f32[16,384]{1,0:T(8,128)S(1)}, u32[]{:S(2)}, u32[]{:S(2)}) collective-permute-start(f32[16,384]{1,0:T(8,128)S(1)} %reduce_sum.19), channel_id=1, source_target_pairs={{0,2},{1,3},{2,0},{3,1},{4,6},{5,7},{6,4},{7,5},{8,10},{9,11},{10,... | collective-permute-start | bytes 73736 | tf_op jit(solution)/shard_map/ppermute | solution.py:226
  102.1 12.4 %collective-permute-start.10 = (f32[64,384]{1,0:T(8,128)S(1)}, f32[64,384]{1,0:T(8,128)S(1)}, u32[]{:S(2)}, u32[]{:S(2)}) collective-permute-start(f32[64,384]{1,0:T(8,128)S(1)} %pad_maximum_fusion.2.refs_0_), channel_id=1, source_target_pairs={{0,24},{8,16},{16,8},{24,0},{1,25},{9,17},{17,9},{25,1},{2,26},{10... | collective-permute-start | bytes 294920 | tf_op jit(solution)/shard_map/ppermute | solution.py:64
  103.6 10.9 %collective-permute-start.9 = (f32[64,384]{1,0:T(8,128)S(1)}, f32[64,384]{1,0:T(8,128)}, u32[]{:S(2)}, u32[]{:S(2)}) collective-permute-start(f32[64,384]{1,0:T(8,128)S(1)} %pad_maximum_fusion.2.refs_0_), channel_id=1, source_target_pairs={{0,16},{8,24},{16,0},{24,8},{1,17},{9,25},{17,1},{25,9},{2,18},{10... | collective-permute-start | bytes 294920 | tf_op jit(solution)/shard_map/ppermute | solution.py:64
  105.2 9.4 %collective-permute-start.8 = (f32[64,384]{1,0:T(8,128)S(1)}, f32[64,384]{1,0:T(8,128)}, u32[]{:S(2)}, u32[]{:S(2)}) collective-permute-start(f32[64,384]{1,0:T(8,128)S(1)} %pad_maximum_fusion.2.refs_0_), channel_id=1, source_target_pairs={{0,8},{8,0},{16,24},{24,16},{1,9},{9,1},{17,25},{25,17},{2,10},{10... | collective-permute-start | bytes 294920 | tf_op jit(solution)/shard_map/ppermute | solution.py:64
  114.6 1.3 collective-permute-start.11
  114.7 1.4 collective-permute-start.12
  115.2 1.5 %collective-permute-start.13 = (f32[64,384]{1,0:T(8,128)}, f32[64,384]{1,0:T(8,128)S(1)}, u32[]{:S(2)}, u32[]{:S(2)}) collective-permute-start(f32[64,384]{1,0:T(8,128)} %collective-permute-done.8.refs_1_), channel_id=1, source_target_pairs={{0,1},{1,0},{2,3},{3,2},{4,5},{5,4},{6,7},{7,6},{8,9},{9,8},{10,11... | collective-permute-start | bytes 294920 | tf_op jit(solution)/shard_map/ppermute | solution.py:226
  115.2 1.6 %collective-permute-start.14 = (f32[64,384]{1,0:T(8,128)}, f32[64,384]{1,0:T(8,128)S(1)}, u32[]{:S(2)}, u32[]{:S(2)}) collective-permute-start(f32[64,384]{1,0:T(8,128)} %collective-permute-done.9.refs_2_), channel_id=1, source_target_pairs={{0,1},{1,0},{2,3},{3,2},{4,5},{5,4},{6,7},{7,6},{8,9},{9,8},{10,11... | collective-permute-start | bytes 294920 | tf_op jit(solution)/shard_map/ppermute | solution.py:226
  115.7 1.3 collective-permute-start.15
  117.0 6.1 %collective-permute-start.18 = (f32[64,128]{1,0:T(8,128)S(1)}, f32[64,128]{1,0:T(8,128)S(1)}, u32[]{:S(2)}, u32[]{:S(2)}) collective-permute-start(f32[64,128]{1,0:T(8,128)S(1)} %dynamic-slice_add_fusion), channel_id=1, source_target_pairs={{0,6},{1,7},{2,4},{3,5},{4,2},{5,3},{6,0},{7,1},{8,14},{9,15},{10,... | collective-permute-start | bytes 98312 | tf_op jit(solution)/shard_map/ppermute | solution.py:226
  121.1 4.8 %collective-permute-start.17 = (f32[64,128]{1,0:T(8,128)S(1)}, f32[64,128]{1,0:T(8,128)S(1)}, u32[]{:S(2)}, u32[]{:S(2)}) collective-permute-start(f32[64,128]{1,0:T(8,128)S(1)} %dynamic-slice_add_fusion), channel_id=1, source_target_pairs={{0,4},{1,5},{2,6},{3,7},{4,0},{5,1},{6,2},{7,3},{8,12},{9,13},{10,... | collective-permute-start | bytes 98312 | tf_op jit(solution)/shard_map/ppermute | solution.py:226
  121.1 4.8 %collective-permute-start.16 = (f32[64,128]{1,0:T(8,128)S(1)}, f32[64,128]{1,0:T(8,128)S(1)}, u32[]{:S(2)}, u32[]{:S(2)}) collective-permute-start(f32[64,128]{1,0:T(8,128)S(1)} %dynamic-slice_add_fusion), channel_id=1, source_target_pairs={{0,2},{1,3},{2,0},{3,1},{4,6},{5,7},{6,4},{7,5},{8,10},{9,11},{10,... | collective-permute-start | bytes 98312 | tf_op jit(solution)/shard_map/ppermute | solution.py:226
  126.0 4.9 %collective-permute-start.21 = (f32[64,128]{1,0:T(8,128)S(1)}, f32[64,128]{1,0:T(8,128)S(1)}, u32[]{:S(2)}, u32[]{:S(2)}) collective-permute-start(f32[64,128]{1,0:T(8,128)S(1)} %add_add_fusion), channel_id=1, source_target_pairs={{0,24},{8,16},{16,8},{24,0},{1,25},{9,17},{17,9},{25,1},{2,26},{10... | collective-permute-start | bytes 98312 | tf_op jit(solution)/shard_map/ppermute | solution.py:64
  128.5 3.9 %collective-permute-start.20 = (f32[64,128]{1,0:T(8,128)S(1)}, f32[64,128]{1,0:T(8,128)S(1)}, u32[]{:S(2)}, u32[]{:S(2)}) collective-permute-start(f32[64,128]{1,0:T(8,128)S(1)} %add_add_fusion), channel_id=1, source_target_pairs={{0,16},{8,24},{16,0},{24,8},{1,17},{9,25},{17,1},{25,9},{2,18},{10... | collective-permute-start | bytes 98312 | tf_op jit(solution)/shard_map/ppermute | solution.py:64
  129.0 3.9 %collective-permute-start.19 = (f32[64,128]{1,0:T(8,128)S(1)}, f32[64,128]{1,0:T(8,128)S(1)}, u32[]{:S(2)}, u32[]{:S(2)}) collective-permute-start(f32[64,128]{1,0:T(8,128)S(1)} %add_add_fusion), channel_id=1, source_target_pairs={{0,8},{8,0},{16,24},{24,16},{1,9},{9,1},{17,25},{25,17},{2,10},{10... | collective-permute-start | bytes 98312 | tf_op jit(solution)/shard_map/ppermute | solution.py:64
  132.9 1.4 collective-permute-start.22

commit v3 on v2

--- a/solution.py
+++ b/solution.py
@@ -1,4 +1,5 @@
 import functools
+import math
 
 import jax
 import jax.numpy as jnp
@@ -112,13 +113,14 @@
 
 
 def pair_kernel(rows, feats, places, index_ref, *refs):
-    early_refs, late_refs, refs = (refs[:4], refs[4:8]), refs[8:10], refs[10:]
+    early_refs, late_refs, refs = (refs[:4], refs[4:8]), refs[8:12], refs[12:]
     pieces, refs = refs[: len(places)], refs[len(places):]
     targets_ref, potential_ref, blocks, held, scores, out, in_sem, out_sem = refs
     batch = 4 * rows
     eps = 2.0 / FEAT**0.5
-    scale = -1.0 / (FEAT * eps)
-    loga = -jnp.log(jnp.float32(batch))
+    ln2 = math.log(2.0)
+    scale = -1.0 / (FEAT * eps * ln2)
+    loga = -math.log2(batch)
     own, core = index_ref[0], index_ref[1]
     half = rows // 2
 
@@ -137,11 +139,10 @@
 
     for p in range(4):
         for side in range(2):
-            part = pl.ds(p * half, half)
             into = pl.ds(pl.multiple_of((own ^ p) * rows + (core ^ side) * half, half), half)
             for r in range(DIAG):
                 blocks[into, block(own ^ (p ^ r))] = early_refs[side][p][:, block(r)] * scale
-            blocks[into, block(own ^ (p ^ DIAG))] = late_refs[side][part, :] * scale
+        blocks[block(own ^ p), block(own ^ (p ^ DIAG))] = late_refs[p][...].T * scale
 
     def sweep(_, v):
         u = []
@@ -150,22 +151,22 @@
             k = blocks[pl.ds(c * STEP, STEP), :]
             a = k + v
             m = jnp.max(a, axis=1, keepdims=True)
-            s = jnp.sum(jnp.exp(a - m), axis=1, keepdims=True)
-            u.append(loga - (m + jnp.log(s)))
+            s = jnp.sum(jnp.exp2(a - m), axis=1, keepdims=True)
+            u.append(loga - (m + jnp.log2(s)))
             top = jnp.maximum(top, jnp.max(k + u[-1], axis=0, keepdims=True))
         total = jnp.zeros((1, batch), jnp.float32)
         for c in range(batch // STEP):
             a = blocks[pl.ds(c * STEP, STEP), :] + u[c]
-            total = total + jnp.sum(jnp.exp(a - top), axis=0, keepdims=True)
-        return loga - (top + jnp.log(total))
+            total = total + jnp.sum(jnp.exp2(a - top), axis=0, keepdims=True)
+        return loga - (top + jnp.log2(total))
 
     v = lax.fori_loop(0, ITERS, sweep, jnp.zeros((1, batch), jnp.float32))
-    potential_ref[...] = v * eps
+    potential_ref[...] = v * (eps * ln2)
 
     a = blocks[block(own), :] + v
     m = jnp.max(a, axis=1, keepdims=True)
-    s = jnp.sum(jnp.exp(a - m), axis=1, keepdims=True)
-    scores[...] = jnp.exp(a - (m + jnp.log(s)))
+    s = jnp.sum(jnp.exp2(a - m), axis=1, keepdims=True)
+    scores[...] = jnp.exp2(a - (m + jnp.log2(s)))
     w = jnp.concatenate([scores[:, block(own ^ r)].T for r in range(4)], axis=0).astype(jnp.bfloat16)
     tile = feats // TILES
 
@@ -200,7 +201,7 @@
             jax.ShapeDtypeStruct((feats, rows), jnp.bfloat16),
             jax.ShapeDtypeStruct((1, batch), jnp.float32),
         ),
-        in_specs=[SMEM] + [VMEM] * 10 + [HBM] * len(pieces),
+        in_specs=[SMEM] + [VMEM] * 12 + [HBM] * len(pieces),
         out_specs=(HBM, VMEM),
         scratch_shapes=[
             pltpu.VMEM((batch, batch), jnp.float32),
@@ -226,21 +227,6 @@
     return lax.ppermute(value, "group", [(g, g ^ way) for g in range(groups)])
 
 
-def core_share(value, core):
-    half = value.shape[0] // 2
-    kept = lax.dynamic_slice_in_dim(value, core * jnp.uint32(half), half)
-    given = lax.dynamic_slice_in_dim(value, (1 - core) * jnp.uint32(half), half)
-    return kept + turn(given, 1)
-
-
-def line_sum(value):
-    ways = range(2, lax.axis_size("group"), 2)
-    terms = [value] + [turn(value, way) for way in ways]
-    while len(terms) > 1:
-        terms = [first + second for first, second in zip(terms[::2], terms[1::2])]
-    return terms[0]
-
-
 def group_share(value):
     groups = lax.axis_size("group")
     rows, width = value.shape
@@ -258,6 +244,12 @@
     )
 
 
+def product(first_t, second_t):
+    return lax.dot_general(
+        first_t, second_t, (((0,), (0,)), ((), ())), preferred_element_type=jnp.float32
+    )
+
+
 def batch_swaps(value):
     return [value, swap(value, X), swap(value, Y), swap(value, DIAG)]
 
@@ -273,10 +265,15 @@
     low, high = (0, first), (first, feats - first)
     d_low, d_high = data_t[:first], data_t[first:]
     x_all, y_low, y_high = swap(data_t, X), swap(d_low, Y), swap(d_high, Y)
-    start = jnp.broadcast_to(squared(noise_t)[:, None], (rows, rows))
+    noise_sq, data_sq = squared(noise_t), squared(data_t)
+    diag_sq = swap(data_sq, DIAG)
+    n_low, n_high = noise_t[:first], noise_t[first:]
+    start = jnp.broadcast_to(noise_sq[:, None], (rows, rows))
     own_cost = crossed(noise, (start, d_low, low, d_high, high))
     y_cost = crossed(noise, (start, y_low, low))
-    y_low, own_cost, y_cost = lax.optimization_barrier((y_low, own_cost, y_cost))
+    y_low, own_cost, y_cost, data_sq, n_low, n_high = lax.optimization_barrier(
+        (y_low, own_cost, y_cost, data_sq, n_low, n_high)
+    )
     diag_low = swap(y_low, X)
     x_tail = x_all[first:]
     diag_high = swap(x_tail, Y)
@@ -284,17 +281,18 @@
     early = crossed(noise, (own_cost,), (start, x_all, (0, feats)), (y_cost, y_high, high))
     early_half = line_gather(group_share(early), line)
     early_mine = batch_swaps(early_half)
+    _, diag_high, diag_sq = lax.optimization_barrier((early_half, diag_high, diag_sq))
     _, diag_low = lax.optimization_barrier((early_half, diag_low))
-    late = crossed(noise, (start, diag_low, low))
-    _, diag_high = lax.optimization_barrier((early_half, diag_high))
-    late = crossed(noise, (late, diag_high, high))
+    late = noise_sq[None, :] + diag_sq[:, None] - 2.0 * (product(diag_high, n_high) + product(diag_low, n_low))
     late, *early_mine = lax.optimization_barrier((late, *early_mine))
     early_rows = early_mine + [turn(value, 1) for value in early_mine]
-    late_half = core_share(late, core)
-    late_half, *early_rows = lax.optimization_barrier((late_half, *early_rows))
-    late_half = line_sum(late_half)
-    late_mine = jnp.concatenate(batch_swaps(late_half))
-    late_rows = [late_mine, turn(late_mine, 1)]
+    late = late + turn(late, 1)
+    late, *early_rows = lax.optimization_barrier((late, *early_rows))
+    way = 2
+    while way < lax.axis_size("group"):
+        late = late + turn(late, way)
+        way *= 2
+    late_rows = batch_swaps(late)
 
     pieces = [d_low, x_all, y_low, diag_low, d_high, y_high, diag_high]
     places = [(0, 0), (0, X), (0, Y), (0, DIAG), (first, 0), (first, Y), (first, DIAG)]

time: 145 us -> 146 us (level)
  waiting for transfers between devices: 66.9 us -> 62.2 us
  matrix products: 0 us -> 4.59 us
  Pallas kernels: 23.4 us -> 19.1 us
  local copies, waits for them, and re-layouts: 12.4 us -> 16.5 us
  starting transfers between devices: 24.7 us -> 26.3 us
    dot_general x0 -> x2, matrix products: none -> 4.59 us  [product(): lax.dot_general(first_t, second_t, (((0,), (0,)), ((), ())), preferred_el...]
    slice x0 -> x2, local copies, waits for them, and re-layouts: none -> 4.13 us  [local_square(): n_low, n_high = (noise_t[:first], noise_t[first:])]
    pallas_call x5 -> x3, Pallas kernels: 13.3 us -> 9.38 us  [crossed(): pl.pallas_call(functools.partial(cross_kernel, spans), out_shape=jax.Shap...]
    ppermute x11 -> x12, waiting for transfers between devices: 58.3 us -> 54.5 us  [swap(): return lax.ppermute(value, 'batch', [(i, i ^ way) for i in range(4)])]
    ppermute x11 -> x12, starting transfers between devices: 14.3 us -> 16.4 us  [swap(): return lax.ppermute(value, 'batch', [(i, i ^ way) for i in range(4)])]
    ppermute x12 -> x10, waiting for transfers between devices: 8.63 us -> 7.69 us  [turn(): return lax.ppermute(value, 'group', [(g, g ^ way) for g in range(groups)])]
    ppermute x12 -> x10, starting transfers between devices: 10.4 us -> 9.91 us  [turn(): return lax.ppermute(value, 'group', [(g, g ^ way) for g in range(groups)])]
    reduce_sum x1 -> x2, other arithmetic: 3.09 us -> 3.35 us  [squared(): return jnp.sum(jnp.square(values_t.astype(jnp.float32)), axis=0)]
  transfers between devices with their start and end apart: 23 -> 22, of which waited for: 17 -> 10; matrix products, arithmetic and copies ran while one was open for 11% -> 17% of each run, Pallas kernels for 9% -> 6%
where the time goes in v3:
time: 146 us
  waiting for transfers between devices  62.2 us (43%)
  starting transfers between devices  26.3 us (18%)
  Pallas kernels  19.1 us (13%)
  local copies, waits for them, and re-layouts  16.5 us (11%)
  blocking collectives  13 us (9%)
  matrix products  4.59 us (3%)
  other arithmetic  3.49 us (2%)
    ppermute x12, waiting for transfers between devices, swap(): return lax.ppermute(value, 'batch', [(i, i ^ way) for i in range(4)])  54.5 us
    ppermute x12, starting transfers between devices, swap(): return lax.ppermute(value, 'batch', [(i, i ^ way) for i in range(4)])  16.4 us
    all_to_all x1, blocking collectives, group_share(): parts = lax.all_to_all(parts, 'group', 0, 0, tiled=True)  13 us
    ppermute x10, starting transfers between devices, turn(): return lax.ppermute(value, 'group', [(g, g ^ way) for g in range(groups)])  9.91 us
    pallas_call x1, Pallas kernels, paired(): pl.pallas_call(functools.partial(pair_kernel, rows, feats, places), out_s...  9.67 us
    pallas_call x3, Pallas kernels, crossed(): pl.pallas_call(functools.partial(cross_kernel, spans), out_shape=jax.Shap...  9.38 us
    ppermute x10, waiting for transfers between devices, turn(): return lax.ppermute(value, 'group', [(g, g ^ way) for g in range(groups)])  7.69 us
    slice x2, local copies, waits for them, and re-layouts, local_square(): d_low, d_high = (data_t[:first], data_t[first:])  5.48 us
  transfers between devices with their start and end apart: 22, of which 10 were waited for; matrix products, arithmetic and copies ran while one was open for 17% of the time, Pallas kernels for 6%

profile of v3, /device:TPU:0, one launch (start us, length us, event | category | flops | bytes accessed | tf_op | source)
XLA Modules:
  0.0 146.0 jit_solution(18182598063673707084)
XLA Ops:
  0.6 3.0 %collective-permute-start.1 = (bf16[12480,128]{1,0:T(8,128)(2,1)}, bf16[12480,128]{1,0:T(8,128)(2,1)}, u32[]{:S(2)}, u32[]{:S(2)}) collective-permute-start(bf16[12480,128]{1,0:T(8,128)(2,1)} %bitcast.31), channel_id=1, source_target_pairs={{0,8},{8,0},{16,24},{24,16},{1,9},{9,1},{17,25},{25,17},{2,10},{10... | collective-permute-start | bytes 9584648 | tf_op jit(solution)/shard_map/ppermute | solution.py:65
  3.6 2.8 %slice.20.refs_1_.refs_12_ = bf16[6656,128]{1,0:T(8,128)(2,1)} slice(bf16[12480,128]{1,0:T(8,128)(2,1)} %bitcast.32), slice={[0:6656], [0:128]} | slice | bytes 3407872 | tf_op jit(solution)/shard_map/slice | solution.py:266
  8.0 2.7 %slice.21.refs_2_.refs_16_ = bf16[5824,128]{1,0:T(8,128)(2,1)} slice(bf16[12480,128]{1,0:T(8,128)(2,1)} %bitcast.33), slice={[6656:12480], [0:128]} | slice | bytes 2981888 | tf_op jit(solution)/shard_map/slice | solution.py:266
  11.1 4.2 %copy.9.noise_ref = bf16[128,12480]{1,0:T(8,128)(2,1)S(1)} copy(bf16[128,12480]{0,1:T(8,128)(2,1)} %param.2) | data formatting | bytes 6389760 | tf_op args[0]
  15.3 2.9 %slice.22 = bf16[6656,128]{1,0:T(8,128)(2,1)} slice(bf16[12480,128]{1,0:T(8,128)(2,1)} %bitcast.29), slice={[0:6656], [0:128]} | slice | bytes 3407872 | tf_op jit(solution)/shard_map/slice | solution.py:270
  21.2 3.2 %shard_map.41.refs_0_ = f32[128,128]{1,0:T(8,128)S(1)} custom-call(bf16[128,12480]{1,0:T(8,128)(2,1)S(1)} %copy.9.noise_ref, f32[128,128]{1,0:T(8,128)S(1)} %broadcast_in_dim.2.refs_0_.refs_1_, bf16[6656,128]{1,0:T(8,128)(2,1)} %slice.20.refs_1_.refs_12_, bf16[5824,128]{1,0:T(8,128)(2,1)} %slice.21.refs_2_.refs_16_), custom_call_target="tpu_custom_call" | custom-call | flops 408944640 | bytes 6389760 | tf_op jit(solution)/shard_map/pallas_call | solution.py:101
  26.2 20.7 %collective-permute-done.refs_1_.refs_14_ = bf16[6656,128]{1,0:T(8,128)(2,1)} collective-permute-done((bf16[6656,128]{1,0:T(8,128)(2,1)}, bf16[6656,128]{1,0:T(8,128)(2,1)}, u32[]{:S(2)}, u32[]{:S(2)}) %collective-permute-start) | collective-permute-done | bytes 1703968 | tf_op jit(solution)/shard_map/ppermute | solution.py:65
  46.9 2.1 %shard_map.42.refs_3_ = f32[128,128]{1,0:T(8,128)S(1)} custom-call(bf16[128,12480]{1,0:T(8,128)(2,1)S(1)} %copy.9.noise_ref, f32[128,128]{1,0:T(8,128)S(1)} %broadcast_in_dim.2.refs_0_.refs_1_, bf16[6656,128]{1,0:T(8,128)(2,1)} %collective-permute-done.refs_1_.refs_14_), custom_call_target="tpu_custom_call" | custom-call | flops 218103808 | bytes 3407872 | tf_op jit(solution)/shard_map/pallas_call | solution.py:101
  49.1 24.8 %collective-permute-done.1.refs_2_.refs_13_ = bf16[12480,128]{1,0:T(8,128)(2,1)} collective-permute-done((bf16[12480,128]{1,0:T(8,128)(2,1)}, bf16[12480,128]{1,0:T(8,128)(2,1)}, u32[]{:S(2)}, u32[]{:S(2)}) %collective-permute-start.1) | collective-permute-done | bytes 3194912 | tf_op jit(solution)/shard_map/ppermute | solution.py:65
  73.9 2.6 %slice.24 = bf16[5824,128]{1,0:T(8,128)(2,1)} slice(bf16[12480,128]{1,0:T(8,128)(2,1)} %collective-permute-done.1.refs_2_.refs_13_), slice={[6656:12480], [0:128]} | slice | bytes 2981888 | tf_op jit(solution)/shard_map/slice | solution.py:278
  76.5 2.1 %collective-permute-start.6 = (bf16[5824,128]{1,0:T(8,128)(2,1)}, bf16[5824,128]{1,0:T(8,128)(2,1)}, u32[]{:S(2)}, u32[]{:S(2)}) collective-permute-start(bf16[5824,128]{1,0:T(8,128)(2,1)} %slice.24), channel_id=1, source_target_pairs={{0,16},{8,24},{16,0},{24,8},{1,17},{9,25},{17,1},{25,9},{2,18},{10... | collective-permute-start | bytes 4472840 | tf_op jit(solution)/shard_map/ppermute | solution.py:65
  78.6 4.0 %shard_map.43 = f32[128,384]{1,0:T(8,128)S(1)} custom-call(bf16[128,12480]{1,0:T(8,128)(2,1)S(1)} %copy.9.noise_ref, f32[128,128]{1,0:T(8,128)S(1)} %shard_map.41.refs_0_, f32[128,128]{1,0:T(8,128)S(1)} %broadcast_in_dim.2.refs_0_.refs_1_, bf16[12480,128]{1,0:T(8,128)(2,1)} %collective-permute-done.1.refs_2_.refs_13_, f32[128,128]{1,0:T(8,128)S(1)} %shard_map.42.refs_3_, ...), custom_call_target="tpu_custom_call" | custom-call | flops 599785472 | bytes 9371648 | tf_op jit(solution)/shard_map/pallas_call | solution.py:101
  82.7 13.0 %all_to_all.9 = f32[8,16,384]{2,1,0:T(8,128)S(1)} all-to-all(f32[8,16,384]{2,1,0:T(8,128)S(1)} %bitcast.34), channel_id=1, replica_groups=mesh['batch'=4,'group'=8] {'group'}, dimensions={0} | all-to-all | bytes 393216 | tf_op jit(solution)/shard_map/all_to_all | solution.py:235
  97.1 3.1 %collective-permute-start.4 = (f32[16,384]{1,0:T(8,128)S(1)}, f32[16,384]{1,0:T(8,128)S(1)}, u32[]{:S(2)}, u32[]{:S(2)}) collective-permute-start(f32[16,384]{1,0:T(8,128)S(1)} %reduce_sum.29), channel_id=1, source_target_pairs={{0,4},{1,5},{2,6},{3,7},{4,0},{5,1},{6,2},{7,3},{8,12},{9,13},{10,... | collective-permute-start | bytes 73736 | tf_op jit(solution)/shard_map/ppermute | solution.py:227
  105.2 5.3 %collective-permute-done.8.refs_15_ = bf16[6656,128]{1,0:T(8,128)(2,1)} collective-permute-done((bf16[6656,128]{1,0:T(8,128)(2,1)}, bf16[6656,128]{1,0:T(8,128)(2,1)}, u32[]{:S(2)}, u32[]{:S(2)}) %collective-permute-start.8) | collective-permute-done | bytes 1703968 | tf_op jit(solution)/shard_map/ppermute | solution.py:65
  110.4 2.0 %collective-permute-start.9 = (f32[64,384]{1,0:T(8,128)S(1)}, f32[64,384]{1,0:T(8,128)S(1)}, u32[]{:S(2)}, u32[]{:S(2)}) collective-permute-start(f32[64,384]{1,0:T(8,128)S(1)} %pad_maximum_fusion.1.refs_0_), channel_id=1, source_target_pairs={{0,8},{8,0},{16,24},{24,16},{1,9},{9,1},{17,25},{25,17},{2,10},{10... | collective-permute-start | bytes 294920 | tf_op jit(solution)/shard_map/ppermute | solution.py:65
  112.4 2.6 %fusion.1 = f32[128,128]{1,0:T(8,128)S(1)} fusion(bf16[6656,128]{1,0:T(8,128)(2,1)} %collective-permute-done.8.refs_15_, bf16[6656,128]{1,0:T(8,128)(2,1)} %slice.22), kind=kOutput, calls=%fused_computation.12 | convolution fusion | flops 218103808 | bytes 3473408 | tf_op jit(solution)/shard_map/dot_general | solution.py:248
  115.1 2.0 %add_subtract_fusion = f32[128,128]{1,0:T(8,128)S(1)} fusion(f32[128,128]{1,0:T(8,128)S(1)} %fusion.1, bf16[5824,128]{1,0:T(8,128)(2,1)} %collective-permute-done.6.refs_18_, bf16[5824,128]{1,0:T(8,128)(2,1)S(1)} %copy-done.2, f32[128]{0:T(128)S(1)} %collective-permute-done.7, f32[128]{0:T(128)S(1)} %multiply_reduce_fusion.1), kind=kOutput, calls=%fused_computation.6 | convolution fusion | flops 190906368 | bytes 3113984 | tf_op jit(solution)/shard_map/dot_general | solution.py:248
  121.1 2.7 %collective-permute-done.17 = f32[128,128]{1,0:T(8,128)S(1)} collective-permute-done((f32[128,128]{1,0:T(8,128)S(1)}, f32[128,128]{1,0:T(8,128)S(1)}, u32[]{:S(2)}, u32[]{:S(2)}) %collective-permute-start.17) | collective-permute-done | bytes 65568 | tf_op jit(solution)/shard_map/ppermute | solution.py:227
  123.8 2.7 %collective-permute-start.18 = (f32[128,128]{1,0:T(8,128)S(1)}, f32[128,128]{1,0:T(8,128)S(1)}, u32[]{:S(2)}, u32[]{:S(2)}) collective-permute-start(f32[128,128]{1,0:T(8,128)S(1)} %add.30), channel_id=1, source_target_pairs={{0,4},{1,5},{2,6},{3,7},{4,0},{5,1},{6,2},{7,3},{8,12},{9,13},{10,... | collective-permute-start | bytes 196616 | tf_op jit(solution)/shard_map/ppermute | solution.py:227
  126.5 2.6 %collective-permute-done.18 = f32[128,128]{1,0:T(8,128)S(1)} collective-permute-done((f32[128,128]{1,0:T(8,128)S(1)}, f32[128,128]{1,0:T(8,128)S(1)}, u32[]{:S(2)}, u32[]{:S(2)}) %collective-permute-start.18) | collective-permute-done | bytes 65568 | tf_op jit(solution)/shard_map/ppermute | solution.py:227
  129.5 1.7 %collective-permute-start.20 = (f32[128,128]{1,0:T(8,128)S(1)}, f32[128,128]{1,0:T(8,128)S(1)}, u32[]{:S(2)}, u32[]{:S(2)}) collective-permute-start(f32[128,128]{1,0:T(8,128)S(1)} %add.31.refs_8_), channel_id=1, source_target_pairs={{0,16},{8,24},{16,0},{24,8},{1,17},{9,25},{17,1},{25,9},{2,18},{10... | collective-permute-start | bytes 196616 | tf_op jit(solution)/shard_map/ppermute | solution.py:65
  133.7 2.6 %collective-permute-done.21.refs_11_ = f32[128,128]{1,0:T(8,128)S(1)} collective-permute-done((f32[128,128]{1,0:T(8,128)S(1)}, f32[128,128]{1,0:T(8,128)S(1)}, u32[]{:S(2)}, u32[]{:S(2)}) %collective-permute-start.21) | collective-permute-done | bytes 65568 | tf_op jit(solution)/shard_map/ppermute | solution.py:65
  136.3 9.7 %shard_map.44 = (bf16[12480,128]{1,0:T(8,128)(2,1)}, f32[1,512]{1,0:T(1,128)}) custom-call(s32[2]{0:T(128)S(1)} %pad_add_fusion.index_ref, f32[64,384]{1,0:T(8,128)S(1)} %pad_maximum_fusion.1.refs_0_, f32[64,384]{1,0:T(8,128)S(1)} %collective-permute-done.9.refs_1_, f32[64,384]{1,0:T(8,128)S(1)} %collective-permute-done.10.refs_2_, ...), custom_call_target="tpu_custom_call" | custom-call | flops 1635778560 | bytes 15974400 | tf_op jit(solution)/shard_map/pallas_call | solution.py:198
  (51 shorter events, 20.1 us)
Async XLA Ops:
  0.6 73.3 %collective-permute-start.1 = (bf16[12480,128]{1,0:T(8,128)(2,1)}, bf16[12480,128]{1,0:T(8,128)(2,1)}, u32[]{:S(2)}, u32[]{:S(2)}) collective-permute-start(bf16[12480,128]{1,0:T(8,128)(2,1)} %bitcast.31), channel_id=1, source_target_pairs={{0,8},{8,0},{16,24},{24,16},{1,9},{9,1},{17,25},{25,17},{2,10},{10... | collective-permute-start | bytes 9584648 | tf_op jit(solution)/shard_map/ppermute | solution.py:65
  6.5 40.4 %collective-permute-start = (bf16[6656,128]{1,0:T(8,128)(2,1)}, bf16[6656,128]{1,0:T(8,128)(2,1)}, u32[]{:S(2)}, u32[]{:S(2)}) collective-permute-start(bf16[6656,128]{1,0:T(8,128)(2,1)} %slice.20.refs_1_.refs_12_), channel_id=1, source_target_pairs={{0,16},{8,24},{16,0},{24,8},{1,17},{9,25},{17,1},{25,9},{2,18},{10... | collective-permute-start | bytes 5111816 | tf_op jit(solution)/shard_map/ppermute | solution.py:65
  10.6 68.0 %collective-permute-start.2 = (bf16[5824,128]{1,0:T(8,128)(2,1)}, bf16[5824,128]{1,0:T(8,128)(2,1)}, u32[]{:S(2)}, u32[]{:S(2)}) collective-permute-start(bf16[5824,128]{1,0:T(8,128)(2,1)} %slice.21.refs_2_.refs_16_), channel_id=1, source_target_pairs={{0,16},{8,24},{16,0},{24,8},{1,17},{9,25},{17,1},{25,9},{2,18},{10... | collective-permute-start | bytes 4472840 | tf_op jit(solution)/shard_map/ppermute | solution.py:65
  21.2 3.3 %copy-start.1 = (bf16[128,12480]{0,1:T(8,128)(2,1)S(1)}, bf16[128,12480]{0,1:T(8,128)(2,1)}, u32[]{:S(2)}) copy-start(bf16[128,12480]{0,1:T(8,128)(2,1)} %param.3) | copy-start | bytes 9584644
  49.0 61.4 %collective-permute-start.8 = (bf16[6656,128]{1,0:T(8,128)(2,1)}, bf16[6656,128]{1,0:T(8,128)(2,1)}, u32[]{:S(2)}, u32[]{:S(2)}) collective-permute-start(bf16[6656,128]{1,0:T(8,128)(2,1)} %collective-permute-done.refs_1_.refs_14_), channel_id=1, source_target_pairs={{0,8},{8,0},{16,24},{24,16},{1,9},{9,1},{17,25},{25,17},{2,10},{10... | collective-permute-start | bytes 5111816 | tf_op jit(solution)/shard_map/ppermute | solution.py:65
  76.5 38.5 %collective-permute-start.6 = (bf16[5824,128]{1,0:T(8,128)(2,1)}, bf16[5824,128]{1,0:T(8,128)(2,1)}, u32[]{:S(2)}, u32[]{:S(2)}) collective-permute-start(bf16[5824,128]{1,0:T(8,128)(2,1)} %slice.24), channel_id=1, source_target_pairs={{0,16},{8,24},{16,0},{24,8},{1,17},{9,25},{17,1},{25,9},{2,18},{10... | collective-permute-start | bytes 4472840 | tf_op jit(solution)/shard_map/ppermute | solution.py:65
  95.7 5.7 %collective-permute-start.5 = (f32[16,384]{1,0:T(8,128)S(1)}, f32[16,384]{1,0:T(8,128)S(1)}, u32[]{:S(2)}, u32[]{:S(2)}) collective-permute-start(f32[16,384]{1,0:T(8,128)S(1)} %reduce_sum.29), channel_id=1, source_target_pairs={{0,6},{1,7},{2,4},{3,5},{4,2},{5,3},{6,0},{7,1},{8,14},{9,15},{10,... | collective-permute-start | bytes 73736 | tf_op jit(solution)/shard_map/ppermute | solution.py:227
  97.1 5.8 %collective-permute-start.3 = (f32[16,384]{1,0:T(8,128)S(1)}, f32[16,384]{1,0:T(8,128)S(1)}, u32[]{:S(2)}, u32[]{:S(2)}) collective-permute-start(f32[16,384]{1,0:T(8,128)S(1)} %reduce_sum.29), channel_id=1, source_target_pairs={{0,2},{1,3},{2,0},{3,1},{4,6},{5,7},{6,4},{7,5},{8,10},{9,11},{10,... | collective-permute-start | bytes 73736 | tf_op jit(solution)/shard_map/ppermute | solution.py:227
  97.1 5.8 %collective-permute-start.4 = (f32[16,384]{1,0:T(8,128)S(1)}, f32[16,384]{1,0:T(8,128)S(1)}, u32[]{:S(2)}, u32[]{:S(2)}) collective-permute-start(f32[16,384]{1,0:T(8,128)S(1)} %reduce_sum.29), channel_id=1, source_target_pairs={{0,4},{1,5},{2,6},{3,7},{4,0},{5,1},{6,2},{7,3},{8,12},{9,13},{10,... | collective-permute-start | bytes 73736 | tf_op jit(solution)/shard_map/ppermute | solution.py:227
  101.4 13.6 %collective-permute-start.7 = (f32[128]{0:T(128)S(1)}, f32[128]{0:T(128)S(1)}, u32[]{:S(2)}, u32[]{:S(2)}) collective-permute-start(f32[128]{0:T(128)S(1)} %multiply_reduce_fusion), channel_id=1, source_target_pairs={{0,24},{8,16},{16,8},{24,0},{1,25},{9,17},{17,9},{25,1},{2,26},{10... | collective-permute-start | bytes 1544 | tf_op jit(solution)/shard_map/ppermute | solution.py:65
  102.9 12.1 %copy-start.2 = (bf16[5824,128]{1,0:T(8,128)(2,1)S(1)}, bf16[5824,128]{1,0:T(8,128)(2,1)}, u32[]{:S(2)}) copy-start(bf16[5824,128]{1,0:T(8,128)(2,1)} %slice.23) | copy-start | bytes 4472836
  102.9 14.1 %collective-permute-start.10 = (f32[64,384]{1,0:T(8,128)S(1)}, f32[64,384]{1,0:T(8,128)S(1)}, u32[]{:S(2)}, u32[]{:S(2)}) collective-permute-start(f32[64,384]{1,0:T(8,128)S(1)} %pad_maximum_fusion.1.refs_0_), channel_id=1, source_target_pairs={{0,16},{8,24},{16,0},{24,8},{1,17},{9,25},{17,1},{25,9},{2,18},{10... | collective-permute-start | bytes 294920 | tf_op jit(solution)/shard_map/ppermute | solution.py:65
  104.5 12.5 %collective-permute-start.11 = (f32[64,384]{1,0:T(8,128)S(1)}, f32[64,384]{1,0:T(8,128)S(1)}, u32[]{:S(2)}, u32[]{:S(2)}) collective-permute-start(f32[64,384]{1,0:T(8,128)S(1)} %pad_maximum_fusion.1.refs_0_), channel_id=1, source_target_pairs={{0,24},{8,16},{16,8},{24,0},{1,25},{9,17},{17,9},{25,1},{2,26},{10... | collective-permute-start | bytes 294920 | tf_op jit(solution)/shard_map/ppermute | solution.py:65
  110.4 6.6 %collective-permute-start.9 = (f32[64,384]{1,0:T(8,128)S(1)}, f32[64,384]{1,0:T(8,128)S(1)}, u32[]{:S(2)}, u32[]{:S(2)}) collective-permute-start(f32[64,384]{1,0:T(8,128)S(1)} %pad_maximum_fusion.1.refs_0_), channel_id=1, source_target_pairs={{0,8},{8,0},{16,24},{24,16},{1,9},{9,1},{17,25},{25,17},{2,10},{10... | collective-permute-start | bytes 294920 | tf_op jit(solution)/shard_map/ppermute | solution.py:65
  117.1 2.4 %collective-permute-start.13 = (f32[64,384]{1,0:T(8,128)S(1)}, f32[64,384]{1,0:T(8,128)S(1)}, u32[]{:S(2)}, u32[]{:S(2)}) collective-permute-start(f32[64,384]{1,0:T(8,128)S(1)} %pad_maximum_fusion.1.refs_0_), channel_id=1, source_target_pairs={{0,1},{1,0},{2,3},{3,2},{4,5},{5,4},{6,7},{7,6},{8,9},{9,8},{10,11... | collective-permute-start | bytes 294920 | tf_op jit(solution)/shard_map/ppermute | solution.py:227
  117.2 2.3 %collective-permute-start.14 = (f32[64,384]{1,0:T(8,128)S(1)}, f32[64,384]{1,0:T(8,128)S(1)}, u32[]{:S(2)}, u32[]{:S(2)}) collective-permute-start(f32[64,384]{1,0:T(8,128)S(1)} %collective-permute-done.9.refs_1_), channel_id=1, source_target_pairs={{0,1},{1,0},{2,3},{3,2},{4,5},{5,4},{6,7},{7,6},{8,9},{9,8},{10,11... | collective-permute-start | bytes 294920 | tf_op jit(solution)/shard_map/ppermute | solution.py:227
  117.7 1.8 %collective-permute-start.15 = (f32[64,384]{1,0:T(8,128)S(1)}, f32[64,384]{1,0:T(8,128)S(1)}, u32[]{:S(2)}, u32[]{:S(2)}) collective-permute-start(f32[64,384]{1,0:T(8,128)S(1)} %collective-permute-done.10.refs_2_), channel_id=1, source_target_pairs={{0,1},{1,0},{2,3},{3,2},{4,5},{5,4},{6,7},{7,6},{8,9},{9,8},{10,11... | collective-permute-start | bytes 294920 | tf_op jit(solution)/shard_map/ppermute | solution.py:227
  117.7 1.7 %collective-permute-start.16 = (f32[64,384]{1,0:T(8,128)S(1)}, f32[64,384]{1,0:T(8,128)S(1)}, u32[]{:S(2)}, u32[]{:S(2)}) collective-permute-start(f32[64,384]{1,0:T(8,128)S(1)} %collective-permute-done.11.refs_3_), channel_id=1, source_target_pairs={{0,1},{1,0},{2,3},{3,2},{4,5},{5,4},{6,7},{7,6},{8,9},{9,8},{10,11... | collective-permute-start | bytes 294920 | tf_op jit(solution)/shard_map/ppermute | solution.py:227
  118.2 1.3 collective-permute-start.12
  119.5 4.3 %collective-permute-start.17 = (f32[128,128]{1,0:T(8,128)S(1)}, f32[128,128]{1,0:T(8,128)S(1)}, u32[]{:S(2)}, u32[]{:S(2)}) collective-permute-start(f32[128,128]{1,0:T(8,128)S(1)} %add.29), channel_id=1, source_target_pairs={{0,2},{1,3},{2,0},{3,1},{4,6},{5,7},{6,4},{7,5},{8,10},{9,11},{10,... | collective-permute-start | bytes 196616 | tf_op jit(solution)/shard_map/ppermute | solution.py:227
  123.8 5.2 %collective-permute-start.18 = (f32[128,128]{1,0:T(8,128)S(1)}, f32[128,128]{1,0:T(8,128)S(1)}, u32[]{:S(2)}, u32[]{:S(2)}) collective-permute-start(f32[128,128]{1,0:T(8,128)S(1)} %add.30), channel_id=1, source_target_pairs={{0,4},{1,5},{2,6},{3,7},{4,0},{5,1},{6,2},{7,3},{8,12},{9,13},{10,... | collective-permute-start | bytes 196616 | tf_op jit(solution)/shard_map/ppermute | solution.py:227
  129.1 4.3 %collective-permute-start.19 = (f32[128,128]{1,0:T(8,128)S(1)}, f32[128,128]{1,0:T(8,128)S(1)}, u32[]{:S(2)}, u32[]{:S(2)}) collective-permute-start(f32[128,128]{1,0:T(8,128)S(1)} %add.31.refs_8_), channel_id=1, source_target_pairs={{0,8},{8,0},{16,24},{24,16},{1,9},{9,1},{17,25},{25,17},{2,10},{10... | collective-permute-start | bytes 196616 | tf_op jit(solution)/shard_map/ppermute | solution.py:65
  129.5 4.3 %collective-permute-start.20 = (f32[128,128]{1,0:T(8,128)S(1)}, f32[128,128]{1,0:T(8,128)S(1)}, u32[]{:S(2)}, u32[]{:S(2)}) collective-permute-start(f32[128,128]{1,0:T(8,128)S(1)} %add.31.refs_8_), channel_id=1, source_target_pairs={{0,16},{8,24},{16,0},{24,8},{1,17},{9,25},{17,1},{25,9},{2,18},{10... | collective-permute-start | bytes 196616 | tf_op jit(solution)/shard_map/ppermute | solution.py:65
  131.2 5.2 %collective-permute-start.21 = (f32[128,128]{1,0:T(8,128)S(1)}, f32[128,128]{1,0:T(8,128)S(1)}, u32[]{:S(2)}, u32[]{:S(2)}) collective-permute-start(f32[128,128]{1,0:T(8,128)S(1)} %add.31.refs_8_), channel_id=1, source_target_pairs={{0,24},{8,16},{16,8},{24,0},{1,25},{9,17},{17,9},{25,1},{2,26},{10... | collective-permute-start | bytes 196616 | tf_op jit(solution)/shard_map/ppermute | solution.py:65
  (1 other events, 2.9 us)

commit v4 on v2

--- a/solution.py
+++ b/solution.py
@@ -1,4 +1,5 @@
 import functools
+import math
 
 import jax
 import jax.numpy as jnp
@@ -117,8 +118,9 @@
     targets_ref, potential_ref, blocks, held, scores, out, in_sem, out_sem = refs
     batch = 4 * rows
     eps = 2.0 / FEAT**0.5
-    scale = -1.0 / (FEAT * eps)
-    loga = -jnp.log(jnp.float32(batch))
+    ln2 = math.log(2.0)
+    scale = -1.0 / (FEAT * eps * ln2)
+    loga = -math.log2(batch)
     own, core = index_ref[0], index_ref[1]
     half = rows // 2
 
@@ -150,22 +152,22 @@
             k = blocks[pl.ds(c * STEP, STEP), :]
             a = k + v
             m = jnp.max(a, axis=1, keepdims=True)
-            s = jnp.sum(jnp.exp(a - m), axis=1, keepdims=True)
-            u.append(loga - (m + jnp.log(s)))
+            s = jnp.sum(jnp.exp2(a - m), axis=1, keepdims=True)
+            u.append(loga - (m + jnp.log2(s)))
             top = jnp.maximum(top, jnp.max(k + u[-1], axis=0, keepdims=True))
         total = jnp.zeros((1, batch), jnp.float32)
         for c in range(batch // STEP):
             a = blocks[pl.ds(c * STEP, STEP), :] + u[c]
-            total = total + jnp.sum(jnp.exp(a - top), axis=0, keepdims=True)
-        return loga - (top + jnp.log(total))
+            total = total + jnp.sum(jnp.exp2(a - top), axis=0, keepdims=True)
+        return loga - (top + jnp.log2(total))
 
     v = lax.fori_loop(0, ITERS, sweep, jnp.zeros((1, batch), jnp.float32))
-    potential_ref[...] = v * eps
+    potential_ref[...] = v * (eps * ln2)
 
     a = blocks[block(own), :] + v
     m = jnp.max(a, axis=1, keepdims=True)
-    s = jnp.sum(jnp.exp(a - m), axis=1, keepdims=True)
-    scores[...] = jnp.exp(a - (m + jnp.log(s)))
+    s = jnp.sum(jnp.exp2(a - m), axis=1, keepdims=True)
+    scores[...] = jnp.exp2(a - (m + jnp.log2(s)))
     w = jnp.concatenate([scores[:, block(own ^ r)].T for r in range(4)], axis=0).astype(jnp.bfloat16)
     tile = feats // TILES
 
@@ -234,11 +236,11 @@
 
 
 def line_sum(value):
-    ways = range(2, lax.axis_size("group"), 2)
-    terms = [value] + [turn(value, way) for way in ways]
-    while len(terms) > 1:
-        terms = [first + second for first, second in zip(terms[::2], terms[1::2])]
-    return terms[0]
+    way = 2
+    while way < lax.axis_size("group"):
+        value = value + turn(value, way)
+        way *= 2
+    return value
 
 
 def group_share(value):

time: 145 us -> 145 us (level)
    ppermute x12 -> x11, waiting for transfers between devices: 8.63 us -> 8.16 us  [turn(): return lax.ppermute(value, 'group', [(g, g ^ way) for g in range(groups)])]
    ppermute x12 -> x11, starting transfers between devices: 10.4 us -> 10.9 us  [turn(): return lax.ppermute(value, 'group', [(g, g ^ way) for g in range(groups)])]
  transfers between devices with their start and end apart: 23 -> 22, of which waited for: 17 -> 17; matrix products, arithmetic and copies ran while one was open for 11% -> 11% of each run, Pallas kernels for 9% -> 9%
where the time goes in v4:
time: 145 us
  waiting for transfers between devices  66.8 us (46%)
  starting transfers between devices  25.1 us (17%)
  Pallas kernels  23.4 us (16%)
  blocking collectives  13 us (9%)
  local copies, waits for them, and re-layouts  12.4 us (9%)
  other arithmetic  3.22 us (2%)
    ppermute x11, waiting for transfers between devices, swap(): return lax.ppermute(value, 'batch', [(i, i ^ way) for i in range(4)])  58.6 us
    ppermute x11, starting transfers between devices, swap(): return lax.ppermute(value, 'batch', [(i, i ^ way) for i in range(4)])  14.2 us
    pallas_call x5, Pallas kernels, crossed(): pl.pallas_call(functools.partial(cross_kernel, spans), out_shape=jax.Shap...  13.3 us
    all_to_all x1, blocking collectives, group_share(): parts = lax.all_to_all(parts, 'group', 0, 0, tiled=True)  13 us
    ppermute x11, starting transfers between devices, turn(): return lax.ppermute(value, 'group', [(g, g ^ way) for g in range(groups)])  10.9 us
    pallas_call x1, Pallas kernels, paired(): pl.pallas_call(functools.partial(pair_kernel, rows, feats, places), out_s...  10.1 us
    ppermute x11, waiting for transfers between devices, turn(): return lax.ppermute(value, 'group', [(g, g ^ way) for g in range(groups)])  8.16 us
    slice x2, local copies, waits for them, and re-layouts, local_square(): d_low, d_high = (data_t[:first], data_t[first:])  5.48 us
  transfers between devices with their start and end apart: 22, of which 17 were waited for; matrix products, arithmetic and copies ran while one was open for 11% of the time, Pallas kernels for 9%

profile of v4, /device:TPU:0, one launch (start us, length us, event | category | flops | bytes accessed | tf_op | source)
XLA Modules:
  0.0 144.7 jit_solution(11174598963983545021)
XLA Ops:
  0.6 3.0 %collective-permute-start.1 = (bf16[12480,128]{1,0:T(8,128)(2,1)}, bf16[12480,128]{1,0:T(8,128)(2,1)}, u32[]{:S(2)}, u32[]{:S(2)}) collective-permute-start(bf16[12480,128]{1,0:T(8,128)(2,1)} %bitcast.22), channel_id=1, source_target_pairs={{0,8},{8,0},{16,24},{24,16},{1,9},{9,1},{17,25},{25,17},{2,10},{10... | collective-permute-start | bytes 9584648 | tf_op jit(solution)/shard_map/ppermute | solution.py:65
  3.6 2.8 %slice.12.refs_1_.refs_10_ = bf16[6656,128]{1,0:T(8,128)(2,1)} slice(bf16[12480,128]{1,0:T(8,128)(2,1)} %bitcast.23), slice={[0:6656], [0:128]} | slice | bytes 3407872 | tf_op jit(solution)/shard_map/slice | solution.py:276
  8.0 2.7 %slice.13.refs_2_.refs_14_ = bf16[5824,128]{1,0:T(8,128)(2,1)} slice(bf16[12480,128]{1,0:T(8,128)(2,1)} %bitcast.24), slice={[6656:12480], [0:128]} | slice | bytes 2981888 | tf_op jit(solution)/shard_map/slice | solution.py:276
  11.1 4.2 %copy.14.noise_ref = bf16[128,12480]{1,0:T(8,128)(2,1)S(1)} copy(bf16[128,12480]{0,1:T(8,128)(2,1)} %param.2) | data formatting | bytes 6389760 | tf_op args[0]
  15.3 3.1 %multiply_reduce_fusion = f32[128]{0:T(128)S(1)} fusion(bf16[128,12480]{0,1:T(8,128)(2,1)} %param.2), kind=kLoop, calls=%fused_computation | loop fusion | flops 4792192 | bytes 3195392 | tf_op jit(solution)/shard_map/reduce_sum | solution.py:223
  18.5 3.1 %shard_map.41.refs_0_ = f32[128,128]{1,0:T(8,128)S(1)} custom-call(bf16[128,12480]{1,0:T(8,128)(2,1)S(1)} %copy.14.noise_ref, f32[128,128]{1,0:T(8,128)S(1)} %broadcast_in_dim.2.refs_0_.refs_1_, bf16[6656,128]{1,0:T(8,128)(2,1)} %slice.12.refs_1_.refs_10_, bf16[5824,128]{1,0:T(8,128)(2,1)} %slice.13.refs_2_.refs_14_), custom_call_target="tpu_custom_call" | custom-call | flops 408944640 | bytes 6389760 | tf_op jit(solution)/shard_map/pallas_call | solution.py:101
  21.6 25.3 %collective-permute-done.refs_1_.refs_12_ = bf16[6656,128]{1,0:T(8,128)(2,1)} collective-permute-done((bf16[6656,128]{1,0:T(8,128)(2,1)}, bf16[6656,128]{1,0:T(8,128)(2,1)}, u32[]{:S(2)}, u32[]{:S(2)}) %collective-permute-start) | collective-permute-done | bytes 1703968 | tf_op jit(solution)/shard_map/ppermute | solution.py:65
  46.9 2.1 %shard_map.42.refs_3_ = f32[128,128]{1,0:T(8,128)S(1)} custom-call(bf16[128,12480]{1,0:T(8,128)(2,1)S(1)} %copy.14.noise_ref, f32[128,128]{1,0:T(8,128)S(1)} %broadcast_in_dim.2.refs_0_.refs_1_, bf16[6656,128]{1,0:T(8,128)(2,1)} %collective-permute-done.refs_1_.refs_12_), custom_call_target="tpu_custom_call" | custom-call | flops 218103808 | bytes 3407872 | tf_op jit(solution)/shard_map/pallas_call | solution.py:101
  49.1 24.8 %collective-permute-done.1.refs_2_.refs_11_ = bf16[12480,128]{1,0:T(8,128)(2,1)} collective-permute-done((bf16[12480,128]{1,0:T(8,128)(2,1)}, bf16[12480,128]{1,0:T(8,128)(2,1)}, u32[]{:S(2)}, u32[]{:S(2)}) %collective-permute-start.1) | collective-permute-done | bytes 3194912 | tf_op jit(solution)/shard_map/ppermute | solution.py:65
  73.9 2.6 %slice.14 = bf16[5824,128]{1,0:T(8,128)(2,1)} slice(bf16[12480,128]{1,0:T(8,128)(2,1)} %collective-permute-done.1.refs_2_.refs_11_), slice={[6656:12480], [0:128]} | slice | bytes 2981888 | tf_op jit(solution)/shard_map/slice | solution.py:283
  76.5 2.1 %collective-permute-start.7 = (bf16[5824,128]{1,0:T(8,128)(2,1)}, bf16[5824,128]{1,0:T(8,128)(2,1)}, u32[]{:S(2)}, u32[]{:S(2)}) collective-permute-start(bf16[5824,128]{1,0:T(8,128)(2,1)} %slice.14), channel_id=1, source_target_pairs={{0,16},{8,24},{16,0},{24,8},{1,17},{9,25},{17,1},{25,9},{2,18},{10... | collective-permute-start | bytes 4472840 | tf_op jit(solution)/shard_map/ppermute | solution.py:65
  78.6 4.0 %shard_map.43 = f32[128,384]{1,0:T(8,128)S(1)} custom-call(bf16[128,12480]{1,0:T(8,128)(2,1)S(1)} %copy.14.noise_ref, f32[128,128]{1,0:T(8,128)S(1)} %shard_map.41.refs_0_, f32[128,128]{1,0:T(8,128)S(1)} %broadcast_in_dim.2.refs_0_.refs_1_, bf16[12480,128]{1,0:T(8,128)(2,1)} %collective-permute-done.1.refs_2_.refs_11_, f32[128,128]{1,0:T(8,128)S(1)} %shard_map.42.refs_3_, ...), custom_call_target="tpu_custom_call" | custom-call | flops 599785472 | bytes 9371648 | tf_op jit(solution)/shard_map/pallas_call | solution.py:101
  82.7 13.0 %all_to_all.9 = f32[8,16,384]{2,1,0:T(8,128)S(1)} all-to-all(f32[8,16,384]{2,1,0:T(8,128)S(1)} %bitcast.25), channel_id=1, replica_groups=mesh['batch'=4,'group'=8] {'group'}, dimensions={0} | all-to-all | bytes 393216 | tf_op jit(solution)/shard_map/all_to_all | solution.py:251
  97.7 2.5 %collective-permute-start.3 = (f32[16,384]{1,0:T(8,128)S(1)}, f32[16,384]{1,0:T(8,128)S(1)}, u32[]{:S(2)}, u32[]{:S(2)}) collective-permute-start(f32[16,384]{1,0:T(8,128)S(1)} %reduce_sum.19), channel_id=1, source_target_pairs={{0,2},{1,3},{2,0},{3,1},{4,6},{5,7},{6,4},{7,5},{8,10},{9,11},{10,... | collective-permute-start | bytes 73736 | tf_op jit(solution)/shard_map/ppermute | solution.py:228
  105.7 4.8 %collective-permute-done.6.refs_1_.refs_13_ = bf16[6656,128]{1,0:T(8,128)(2,1)} collective-permute-done((bf16[6656,128]{1,0:T(8,128)(2,1)}, bf16[6656,128]{1,0:T(8,128)(2,1)}, u32[]{:S(2)}, u32[]{:S(2)}) %collective-permute-start.6) | collective-permute-done | bytes 1703968 | tf_op jit(solution)/shard_map/ppermute | solution.py:65
  110.4 2.1 %shard_map.44.refs_0_ = f32[128,128]{1,0:T(8,128)S(1)} custom-call(bf16[128,12480]{1,0:T(8,128)(2,1)S(1)} %copy.14.noise_ref, f32[128,128]{1,0:T(8,128)S(1)} %broadcast_in_dim.2.refs_0_.refs_1_, bf16[6656,128]{1,0:T(8,128)(2,1)} %collective-permute-done.6.refs_1_.refs_13_), custom_call_target="tpu_custom_call" | custom-call | flops 218103808 | bytes 3407872 | tf_op jit(solution)/shard_map/pallas_call | solution.py:101
  112.6 2.0 %shard_map.45 = f32[128,128]{1,0:T(8,128)S(1)} custom-call(bf16[128,12480]{1,0:T(8,128)(2,1)S(1)} %copy.14.noise_ref, f32[128,128]{1,0:T(8,128)S(1)} %shard_map.44.refs_0_, bf16[5824,128]{1,0:T(8,128)(2,1)} %collective-permute-done.7.refs_1_.refs_16_), custom_call_target="tpu_custom_call" | custom-call | flops 190840832 | bytes 2981888 | tf_op jit(solution)/shard_map/pallas_call | solution.py:101
  117.0 2.1 %collective-permute-start.16 = (f32[64,128]{1,0:T(8,128)S(1)}, f32[64,128]{1,0:T(8,128)S(1)}, u32[]{:S(2)}, u32[]{:S(2)}) collective-permute-start(f32[64,128]{1,0:T(8,128)S(1)} %dynamic-slice_add_fusion), channel_id=1, source_target_pairs={{0,2},{1,3},{2,0},{3,1},{4,6},{5,7},{6,4},{7,5},{8,10},{9,11},{10,... | collective-permute-start | bytes 98312 | tf_op jit(solution)/shard_map/ppermute | solution.py:228
  119.1 1.9 %collective-permute-done.16 = f32[64,128]{1,0:T(8,128)S(1)} collective-permute-done((f32[64,128]{1,0:T(8,128)S(1)}, f32[64,128]{1,0:T(8,128)S(1)}, u32[]{:S(2)}, u32[]{:S(2)}) %collective-permute-start.16) | collective-permute-done | bytes 32800 | tf_op jit(solution)/shard_map/ppermute | solution.py:228
  121.0 3.0 %collective-permute-start.17 = (f32[64,128]{1,0:T(8,128)S(1)}, f32[64,128]{1,0:T(8,128)S(1)}, u32[]{:S(2)}, u32[]{:S(2)}) collective-permute-start(f32[64,128]{1,0:T(8,128)S(1)} %add.10), channel_id=1, source_target_pairs={{0,4},{1,5},{2,6},{3,7},{4,0},{5,1},{6,2},{7,3},{8,12},{9,13},{10,... | collective-permute-start | bytes 98312 | tf_op jit(solution)/shard_map/ppermute | solution.py:228
  124.1 1.9 %collective-permute-done.17 = f32[64,128]{1,0:T(8,128)S(1)} collective-permute-done((f32[64,128]{1,0:T(8,128)S(1)}, f32[64,128]{1,0:T(8,128)S(1)}, u32[]{:S(2)}, u32[]{:S(2)}) %collective-permute-start.17) | collective-permute-done | bytes 32800 | tf_op jit(solution)/shard_map/ppermute | solution.py:228
  125.9 2.8 %collective-permute-start.20 = (f32[64,128]{1,0:T(8,128)S(1)}, f32[64,128]{1,0:T(8,128)S(1)}, u32[]{:S(2)}, u32[]{:S(2)}) collective-permute-start(f32[64,128]{1,0:T(8,128)S(1)} %add.11), channel_id=1, source_target_pairs={{0,24},{8,16},{16,8},{24,0},{1,25},{9,17},{17,9},{25,1},{2,26},{10... | collective-permute-start | bytes 98312 | tf_op jit(solution)/shard_map/ppermute | solution.py:65
  130.8 1.8 %collective-permute-done.19 = f32[64,128]{1,0:T(8,128)S(1)} collective-permute-done((f32[64,128]{1,0:T(8,128)S(1)}, f32[64,128]{1,0:T(8,128)S(1)}, u32[]{:S(2)}, u32[]{:S(2)}) %collective-permute-start.19) | collective-permute-done | bytes 32800 | tf_op jit(solution)/shard_map/ppermute | solution.py:65
  134.6 10.1 %shard_map.46 = (bf16[12480,128]{1,0:T(8,128)(2,1)}, f32[1,512]{1,0:T(1,128)}) custom-call(s32[2]{0:T(128)S(1)} %pad_add_fusion.index_ref, f32[64,384]{1,0:T(8,128)S(1)} %pad_maximum_fusion.2.refs_0_, f32[64,384]{1,0:T(8,128)} %collective-permute-done.8.refs_1_, f32[64,384]{1,0:T(8,128)} %collective-permute-done.9.refs_2_, ...), custom_call_target="tpu_custom_call" | custom-call | flops 1635778560 | bytes 15974400 | tf_op jit(solution)/shard_map/pallas_call | solution.py:199
  (44 shorter events, 16.1 us)
Async XLA Ops:
  0.6 73.3 %collective-permute-start.1 = (bf16[12480,128]{1,0:T(8,128)(2,1)}, bf16[12480,128]{1,0:T(8,128)(2,1)}, u32[]{:S(2)}, u32[]{:S(2)}) collective-permute-start(bf16[12480,128]{1,0:T(8,128)(2,1)} %bitcast.22), channel_id=1, source_target_pairs={{0,8},{8,0},{16,24},{24,16},{1,9},{9,1},{17,25},{25,17},{2,10},{10... | collective-permute-start | bytes 9584648 | tf_op jit(solution)/shard_map/ppermute | solution.py:65
  6.5 40.4 %collective-permute-start = (bf16[6656,128]{1,0:T(8,128)(2,1)}, bf16[6656,128]{1,0:T(8,128)(2,1)}, u32[]{:S(2)}, u32[]{:S(2)}) collective-permute-start(bf16[6656,128]{1,0:T(8,128)(2,1)} %slice.12.refs_1_.refs_10_), channel_id=1, source_target_pairs={{0,16},{8,24},{16,0},{24,8},{1,17},{9,25},{17,1},{25,9},{2,18},{10... | collective-permute-start | bytes 5111816 | tf_op jit(solution)/shard_map/ppermute | solution.py:65
  10.6 68.0 %collective-permute-start.2 = (bf16[5824,128]{1,0:T(8,128)(2,1)}, bf16[5824,128]{1,0:T(8,128)(2,1)}, u32[]{:S(2)}, u32[]{:S(2)}) collective-permute-start(bf16[5824,128]{1,0:T(8,128)(2,1)} %slice.13.refs_2_.refs_14_), channel_id=1, source_target_pairs={{0,16},{8,24},{16,0},{24,8},{1,17},{9,25},{17,1},{25,9},{2,18},{10... | collective-permute-start | bytes 4472840 | tf_op jit(solution)/shard_map/ppermute | solution.py:65
  49.0 61.4 %collective-permute-start.6 = (bf16[6656,128]{1,0:T(8,128)(2,1)}, bf16[6656,128]{1,0:T(8,128)(2,1)}, u32[]{:S(2)}, u32[]{:S(2)}) collective-permute-start(bf16[6656,128]{1,0:T(8,128)(2,1)} %collective-permute-done.refs_1_.refs_12_), channel_id=1, source_target_pairs={{0,8},{8,0},{16,24},{24,16},{1,9},{9,1},{17,25},{25,17},{2,10},{10... | collective-permute-start | bytes 5111816 | tf_op jit(solution)/shard_map/ppermute | solution.py:65
  76.5 36.0 %collective-permute-start.7 = (bf16[5824,128]{1,0:T(8,128)(2,1)}, bf16[5824,128]{1,0:T(8,128)(2,1)}, u32[]{:S(2)}, u32[]{:S(2)}) collective-permute-start(bf16[5824,128]{1,0:T(8,128)(2,1)} %slice.14), channel_id=1, source_target_pairs={{0,16},{8,24},{16,0},{24,8},{1,17},{9,25},{17,1},{25,9},{2,18},{10... | collective-permute-start | bytes 4472840 | tf_op jit(solution)/shard_map/ppermute | solution.py:65
  95.7 5.7 %collective-permute-start.5 = (f32[16,384]{1,0:T(8,128)S(1)}, f32[16,384]{1,0:T(8,128)S(1)}, u32[]{:S(2)}, u32[]{:S(2)}) collective-permute-start(f32[16,384]{1,0:T(8,128)S(1)} %reduce_sum.19), channel_id=1, source_target_pairs={{0,6},{1,7},{2,4},{3,5},{4,2},{5,3},{6,0},{7,1},{8,14},{9,15},{10,... | collective-permute-start | bytes 73736 | tf_op jit(solution)/shard_map/ppermute | solution.py:228
  97.0 4.9 %collective-permute-start.4 = (f32[16,384]{1,0:T(8,128)S(1)}, f32[16,384]{1,0:T(8,128)S(1)}, u32[]{:S(2)}, u32[]{:S(2)}) collective-permute-start(f32[16,384]{1,0:T(8,128)S(1)} %reduce_sum.19), channel_id=1, source_target_pairs={{0,4},{1,5},{2,6},{3,7},{4,0},{5,1},{6,2},{7,3},{8,12},{9,13},{10,... | collective-permute-start | bytes 73736 | tf_op jit(solution)/shard_map/ppermute | solution.py:228
  97.7 4.4 %collective-permute-start.3 = (f32[16,384]{1,0:T(8,128)S(1)}, f32[16,384]{1,0:T(8,128)S(1)}, u32[]{:S(2)}, u32[]{:S(2)}) collective-permute-start(f32[16,384]{1,0:T(8,128)S(1)} %reduce_sum.19), channel_id=1, source_target_pairs={{0,2},{1,3},{2,0},{3,1},{4,6},{5,7},{6,4},{7,5},{8,10},{9,11},{10,... | collective-permute-start | bytes 73736 | tf_op jit(solution)/shard_map/ppermute | solution.py:228
  102.1 12.4 %collective-permute-start.10 = (f32[64,384]{1,0:T(8,128)S(1)}, f32[64,384]{1,0:T(8,128)S(1)}, u32[]{:S(2)}, u32[]{:S(2)}) collective-permute-start(f32[64,384]{1,0:T(8,128)S(1)} %pad_maximum_fusion.2.refs_0_), channel_id=1, source_target_pairs={{0,24},{8,16},{16,8},{24,0},{1,25},{9,17},{17,9},{25,1},{2,26},{10... | collective-permute-start | bytes 294920 | tf_op jit(solution)/shard_map/ppermute | solution.py:65
  103.6 10.9 %collective-permute-start.9 = (f32[64,384]{1,0:T(8,128)S(1)}, f32[64,384]{1,0:T(8,128)}, u32[]{:S(2)}, u32[]{:S(2)}) collective-permute-start(f32[64,384]{1,0:T(8,128)S(1)} %pad_maximum_fusion.2.refs_0_), channel_id=1, source_target_pairs={{0,16},{8,24},{16,0},{24,8},{1,17},{9,25},{17,1},{25,9},{2,18},{10... | collective-permute-start | bytes 294920 | tf_op jit(solution)/shard_map/ppermute | solution.py:65
  105.2 9.4 %collective-permute-start.8 = (f32[64,384]{1,0:T(8,128)S(1)}, f32[64,384]{1,0:T(8,128)}, u32[]{:S(2)}, u32[]{:S(2)}) collective-permute-start(f32[64,384]{1,0:T(8,128)S(1)} %pad_maximum_fusion.2.refs_0_), channel_id=1, source_target_pairs={{0,8},{8,0},{16,24},{24,16},{1,9},{9,1},{17,25},{25,17},{2,10},{10... | collective-permute-start | bytes 294920 | tf_op jit(solution)/shard_map/ppermute | solution.py:65
  114.6 1.3 collective-permute-start.11
  114.7 1.4 collective-permute-start.12
  115.2 1.5 %collective-permute-start.13 = (f32[64,384]{1,0:T(8,128)}, f32[64,384]{1,0:T(8,128)S(1)}, u32[]{:S(2)}, u32[]{:S(2)}) collective-permute-start(f32[64,384]{1,0:T(8,128)} %collective-permute-done.8.refs_1_), channel_id=1, source_target_pairs={{0,1},{1,0},{2,3},{3,2},{4,5},{5,4},{6,7},{7,6},{8,9},{9,8},{10,11... | collective-permute-start | bytes 294920 | tf_op jit(solution)/shard_map/ppermute | solution.py:228
  115.2 1.6 %collective-permute-start.14 = (f32[64,384]{1,0:T(8,128)}, f32[64,384]{1,0:T(8,128)S(1)}, u32[]{:S(2)}, u32[]{:S(2)}) collective-permute-start(f32[64,384]{1,0:T(8,128)} %collective-permute-done.9.refs_2_), channel_id=1, source_target_pairs={{0,1},{1,0},{2,3},{3,2},{4,5},{5,4},{6,7},{7,6},{8,9},{9,8},{10,11... | collective-permute-start | bytes 294920 | tf_op jit(solution)/shard_map/ppermute | solution.py:228
  115.7 1.3 collective-permute-start.15
  117.0 4.0 %collective-permute-start.16 = (f32[64,128]{1,0:T(8,128)S(1)}, f32[64,128]{1,0:T(8,128)S(1)}, u32[]{:S(2)}, u32[]{:S(2)}) collective-permute-start(f32[64,128]{1,0:T(8,128)S(1)} %dynamic-slice_add_fusion), channel_id=1, source_target_pairs={{0,2},{1,3},{2,0},{3,1},{4,6},{5,7},{6,4},{7,5},{8,10},{9,11},{10,... | collective-permute-start | bytes 98312 | tf_op jit(solution)/shard_map/ppermute | solution.py:228
  121.0 4.9 %collective-permute-start.17 = (f32[64,128]{1,0:T(8,128)S(1)}, f32[64,128]{1,0:T(8,128)S(1)}, u32[]{:S(2)}, u32[]{:S(2)}) collective-permute-start(f32[64,128]{1,0:T(8,128)S(1)} %add.10), channel_id=1, source_target_pairs={{0,4},{1,5},{2,6},{3,7},{4,0},{5,1},{6,2},{7,3},{8,12},{9,13},{10,... | collective-permute-start | bytes 98312 | tf_op jit(solution)/shard_map/ppermute | solution.py:228
  125.9 4.9 %collective-permute-start.20 = (f32[64,128]{1,0:T(8,128)S(1)}, f32[64,128]{1,0:T(8,128)S(1)}, u32[]{:S(2)}, u32[]{:S(2)}) collective-permute-start(f32[64,128]{1,0:T(8,128)S(1)} %add.11), channel_id=1, source_target_pairs={{0,24},{8,16},{16,8},{24,0},{1,25},{9,17},{17,9},{25,1},{2,26},{10... | collective-permute-start | bytes 98312 | tf_op jit(solution)/shard_map/ppermute | solution.py:65
  128.7 3.9 %collective-permute-start.19 = (f32[64,128]{1,0:T(8,128)S(1)}, f32[64,128]{1,0:T(8,128)S(1)}, u32[]{:S(2)}, u32[]{:S(2)}) collective-permute-start(f32[64,128]{1,0:T(8,128)S(1)} %add.11), channel_id=1, source_target_pairs={{0,16},{8,24},{16,0},{24,8},{1,17},{9,25},{17,1},{25,9},{2,18},{10... | collective-permute-start | bytes 98312 | tf_op jit(solution)/shard_map/ppermute | solution.py:65
  129.2 3.9 %collective-permute-start.18 = (f32[64,128]{1,0:T(8,128)S(1)}, f32[64,128]{1,0:T(8,128)S(1)}, u32[]{:S(2)}, u32[]{:S(2)}) collective-permute-start(f32[64,128]{1,0:T(8,128)S(1)} %add.11), channel_id=1, source_target_pairs={{0,8},{8,0},{16,24},{24,16},{1,9},{9,1},{17,25},{25,17},{2,10},{10... | collective-permute-start | bytes 98312 | tf_op jit(solution)/shard_map/ppermute | solution.py:65
  133.2 1.4 collective-permute-start.21

commit v5 on v4

--- a/solution.py
+++ b/solution.py
@@ -113,7 +113,7 @@
 
 
 def pair_kernel(rows, feats, places, index_ref, *refs):
-    early_refs, late_refs, refs = (refs[:4], refs[4:8]), refs[8:10], refs[10:]
+    early_refs, late_ref, refs = (refs[:4], refs[4:8]), refs[8], refs[9:]
     pieces, refs = refs[: len(places)], refs[len(places):]
     targets_ref, potential_ref, blocks, held, scores, out, in_sem, out_sem = refs
     batch = 4 * rows
@@ -139,11 +139,10 @@
 
     for p in range(4):
         for side in range(2):
-            part = pl.ds(p * half, half)
             into = pl.ds(pl.multiple_of((own ^ p) * rows + (core ^ side) * half, half), half)
             for r in range(DIAG):
                 blocks[into, block(own ^ (p ^ r))] = early_refs[side][p][:, block(r)] * scale
-            blocks[into, block(own ^ (p ^ DIAG))] = late_refs[side][part, :] * scale
+        blocks[block(own ^ p), block(own ^ (p ^ DIAG))] = late_ref[block(p), :] * scale
 
     def sweep(_, v):
         u = []
@@ -202,7 +201,7 @@
             jax.ShapeDtypeStruct((feats, rows), jnp.bfloat16),
             jax.ShapeDtypeStruct((1, batch), jnp.float32),
         ),
-        in_specs=[SMEM] + [VMEM] * 10 + [HBM] * len(pieces),
+        in_specs=[SMEM] + [VMEM] * 9 + [HBM] * len(pieces),
         out_specs=(HBM, VMEM),
         scratch_shapes=[
             pltpu.VMEM((batch, batch), jnp.float32),
@@ -212,7 +211,7 @@
             pltpu.SemaphoreType.DMA((len(pieces),)),
             pltpu.SemaphoreType.DMA((TILES,)),
         ],
-        compiler_params=pltpu.CompilerParams(vmem_limit_bytes=24 * 2**20),
+        compiler_params=pltpu.CompilerParams(vmem_limit_bytes=20 * 2**20),
         cost_estimate=pl.CostEstimate(
             flops=2 * rows * batch * feats, bytes_accessed=10 * rows * feats, transcendentals=9 * batch * batch
         ),
@@ -226,21 +225,6 @@
 def turn(value, way):
     groups = lax.axis_size("group")
     return lax.ppermute(value, "group", [(g, g ^ way) for g in range(groups)])
-
-
-def core_share(value, core):
-    half = value.shape[0] // 2
-    kept = lax.dynamic_slice_in_dim(value, core * jnp.uint32(half), half)
-    given = lax.dynamic_slice_in_dim(value, (1 - core) * jnp.uint32(half), half)
-    return kept + turn(given, 1)
-
-
-def line_sum(value):
-    way = 2
-    while way < lax.axis_size("group"):
-        value = value + turn(value, way)
-        way *= 2
-    return value
 
 
 def group_share(value):
@@ -292,11 +276,13 @@
     late = crossed(noise, (late, diag_high, high))
     late, *early_mine = lax.optimization_barrier((late, *early_mine))
     early_rows = early_mine + [turn(value, 1) for value in early_mine]
-    late_half = core_share(late, core)
-    late_half, *early_rows = lax.optimization_barrier((late_half, *early_rows))
-    late_half = line_sum(late_half)
-    late_mine = jnp.concatenate(batch_swaps(late_half))
-    late_rows = [late_mine, turn(late_mine, 1)]
+    way = 1
+    while way < lax.axis_size("group"):
+        late = late + turn(late, way)
+        if way == 2:
+            late, *early_rows = lax.optimization_barrier((late, *early_rows))
+        way *= 2
+    late_rows = [jnp.concatenate(batch_swaps(late))]
 
     pieces = [d_low, x_all, y_low, diag_low, d_high, y_high, diag_high]
     places = [(0, 0), (0, X), (0, Y), (0, DIAG), (first, 0), (first, Y), (first, DIAG)]

time: 145 us -> 146 us (level)
  local copies, waits for them, and re-layouts: 12.4 us -> 14.1 us
    unnamed x1 -> x9, local copies, waits for them, and re-layouts: 4.19 us -> 5.98 us
    ppermute x11 -> x10, waiting for transfers between devices: 8.16 us -> 7.41 us  [turn(): return lax.ppermute(value, 'group', [(g, g ^ way) for g in range(groups)])]
    ppermute x11 -> x10, starting transfers between devices: 10.9 us -> 10.6 us  [turn(): return lax.ppermute(value, 'group', [(g, g ^ way) for g in range(groups)])]
  transfers between devices with their start and end apart: 22 -> 21, of which waited for: 17 -> 12; matrix products, arithmetic and copies ran while one was open for 11% -> 11% of each run, Pallas kernels for 9% -> 9%
where the time goes in v5:
time: 146 us; the launch traced here: 145 us
  waiting for transfers between devices  66 us (45%)
  starting transfers between devices  24.9 us (17%)
  Pallas kernels  23 us (16%)
  local copies, waits for them, and re-layouts  14.1 us (10%)
  blocking collectives  13 us (9%)
  other arithmetic  3.24 us (2%)
    ppermute x11, waiting for transfers between devices, swap(): return lax.ppermute(value, 'batch', [(i, i ^ way) for i in range(4)])  58.6 us
    ppermute x11, starting transfers between devices, swap(): return lax.ppermute(value, 'batch', [(i, i ^ way) for i in range(4)])  14.3 us
    pallas_call x5, Pallas kernels, crossed(): pl.pallas_call(functools.partial(cross_kernel, spans), out_shape=jax.Shap...  13.3 us
    all_to_all x1, blocking collectives, group_share(): parts = lax.all_to_all(parts, 'group', 0, 0, tiled=True)  13 us
    ppermute x10, starting transfers between devices, turn(): return lax.ppermute(value, 'group', [(g, g ^ way) for g in range(groups)])  10.6 us
    pallas_call x1, Pallas kernels, paired(): pl.pallas_call(functools.partial(pair_kernel, rows, feats, places), out_s...  9.69 us
    ppermute x10, waiting for transfers between devices, turn(): return lax.ppermute(value, 'group', [(g, g ^ way) for g in range(groups)])  7.41 us
    unnamed x9, local copies, waits for them, and re-layouts  5.98 us
  transfers between devices with their start and end apart: 21, of which 12 were waited for; matrix products, arithmetic and copies ran while one was open for 11% of the time, Pallas kernels for 9%

profile of v5, /device:TPU:0, one launch (start us, length us, event | category | flops | bytes accessed | tf_op | source)
XLA Modules:
  0.0 145.2 jit_solution(982659163503869346)
XLA Ops:
  0.6 3.0 %collective-permute-start.1 = (bf16[12480,128]{1,0:T(8,128)(2,1)}, bf16[12480,128]{1,0:T(8,128)(2,1)}, u32[]{:S(2)}, u32[]{:S(2)}) collective-permute-start(bf16[12480,128]{1,0:T(8,128)(2,1)} %bitcast.22), channel_id=1, source_target_pairs={{0,8},{8,0},{16,24},{24,16},{1,9},{9,1},{17,25},{25,17},{2,10},{10... | collective-permute-start | bytes 9584648 | tf_op jit(solution)/shard_map/ppermute | solution.py:65
  3.6 2.8 %slice.12.refs_1_.refs_9_ = bf16[6656,128]{1,0:T(8,128)(2,1)} slice(bf16[12480,128]{1,0:T(8,128)(2,1)} %bitcast.23), slice={[0:6656], [0:128]} | slice | bytes 3407872 | tf_op jit(solution)/shard_map/slice | solution.py:260
  8.0 2.6 %slice.13.refs_2_.refs_13_ = bf16[5824,128]{1,0:T(8,128)(2,1)} slice(bf16[12480,128]{1,0:T(8,128)(2,1)} %bitcast.24), slice={[6656:12480], [0:128]} | slice | bytes 2981888 | tf_op jit(solution)/shard_map/slice | solution.py:260
  11.1 4.2 %copy.14.noise_ref = bf16[128,12480]{1,0:T(8,128)(2,1)S(1)} copy(bf16[128,12480]{0,1:T(8,128)(2,1)} %param.2) | data formatting | bytes 6389760 | tf_op args[0]
  15.3 3.1 %multiply_reduce_fusion = f32[128]{0:T(128)S(1)} fusion(bf16[128,12480]{0,1:T(8,128)(2,1)} %param.2), kind=kLoop, calls=%fused_computation | loop fusion | flops 4792192 | bytes 3195392 | tf_op jit(solution)/shard_map/reduce_sum | solution.py:222
  18.5 3.1 %shard_map.41.refs_0_ = f32[128,128]{1,0:T(8,128)S(1)} custom-call(bf16[128,12480]{1,0:T(8,128)(2,1)S(1)} %copy.14.noise_ref, f32[128,128]{1,0:T(8,128)S(1)} %broadcast_in_dim.2.refs_0_.refs_1_, bf16[6656,128]{1,0:T(8,128)(2,1)} %slice.12.refs_1_.refs_9_, bf16[5824,128]{1,0:T(8,128)(2,1)} %slice.13.refs_2_.refs_13_), custom_call_target="tpu_custom_call" | custom-call | flops 408944640 | bytes 6389760 | tf_op jit(solution)/shard_map/pallas_call | solution.py:101
  21.6 25.3 %collective-permute-done.refs_1_.refs_11_ = bf16[6656,128]{1,0:T(8,128)(2,1)} collective-permute-done((bf16[6656,128]{1,0:T(8,128)(2,1)}, bf16[6656,128]{1,0:T(8,128)(2,1)}, u32[]{:S(2)}, u32[]{:S(2)}) %collective-permute-start) | collective-permute-done | bytes 1703968 | tf_op jit(solution)/shard_map/ppermute | solution.py:65
  46.9 2.1 %shard_map.42.refs_3_ = f32[128,128]{1,0:T(8,128)S(1)} custom-call(bf16[128,12480]{1,0:T(8,128)(2,1)S(1)} %copy.14.noise_ref, f32[128,128]{1,0:T(8,128)S(1)} %broadcast_in_dim.2.refs_0_.refs_1_, bf16[6656,128]{1,0:T(8,128)(2,1)} %collective-permute-done.refs_1_.refs_11_), custom_call_target="tpu_custom_call" | custom-call | flops 218103808 | bytes 3407872 | tf_op jit(solution)/shard_map/pallas_call | solution.py:101
  49.1 24.8 %collective-permute-done.1.refs_2_.refs_10_ = bf16[12480,128]{1,0:T(8,128)(2,1)} collective-permute-done((bf16[12480,128]{1,0:T(8,128)(2,1)}, bf16[12480,128]{1,0:T(8,128)(2,1)}, u32[]{:S(2)}, u32[]{:S(2)}) %collective-permute-start.1) | collective-permute-done | bytes 3194912 | tf_op jit(solution)/shard_map/ppermute | solution.py:65
  73.9 2.6 %slice.14 = bf16[5824,128]{1,0:T(8,128)(2,1)} slice(bf16[12480,128]{1,0:T(8,128)(2,1)} %collective-permute-done.1.refs_2_.refs_10_), slice={[6656:12480], [0:128]} | slice | bytes 2981888 | tf_op jit(solution)/shard_map/slice | solution.py:267
  76.5 2.1 %collective-permute-start.7 = (bf16[5824,128]{1,0:T(8,128)(2,1)}, bf16[5824,128]{1,0:T(8,128)(2,1)}, u32[]{:S(2)}, u32[]{:S(2)}) collective-permute-start(bf16[5824,128]{1,0:T(8,128)(2,1)} %slice.14), channel_id=1, source_target_pairs={{0,16},{8,24},{16,0},{24,8},{1,17},{9,25},{17,1},{25,9},{2,18},{10... | collective-permute-start | bytes 4472840 | tf_op jit(solution)/shard_map/ppermute | solution.py:65
  78.6 4.0 %shard_map.43 = f32[128,384]{1,0:T(8,128)S(1)} custom-call(bf16[128,12480]{1,0:T(8,128)(2,1)S(1)} %copy.14.noise_ref, f32[128,128]{1,0:T(8,128)S(1)} %shard_map.41.refs_0_, f32[128,128]{1,0:T(8,128)S(1)} %broadcast_in_dim.2.refs_0_.refs_1_, bf16[12480,128]{1,0:T(8,128)(2,1)} %collective-permute-done.1.refs_2_.refs_10_, f32[128,128]{1,0:T(8,128)S(1)} %shard_map.42.refs_3_, ...), custom_call_target="tpu_custom_call" | custom-call | flops 599785472 | bytes 9371648 | tf_op jit(solution)/shard_map/pallas_call | solution.py:101
  82.7 13.0 %all_to_all.9 = f32[8,16,384]{2,1,0:T(8,128)S(1)} all-to-all(f32[8,16,384]{2,1,0:T(8,128)S(1)} %bitcast.25), channel_id=1, replica_groups=mesh['batch'=4,'group'=8] {'group'}, dimensions={0} | all-to-all | bytes 393216 | tf_op jit(solution)/shard_map/all_to_all | solution.py:235
  97.7 2.5 %collective-permute-start.3 = (f32[16,384]{1,0:T(8,128)S(1)}, f32[16,384]{1,0:T(8,128)S(1)}, u32[]{:S(2)}, u32[]{:S(2)}) collective-permute-start(f32[16,384]{1,0:T(8,128)S(1)} %reduce_sum.19), channel_id=1, source_target_pairs={{0,2},{1,3},{2,0},{3,1},{4,6},{5,7},{6,4},{7,5},{8,10},{9,11},{10,... | collective-permute-start | bytes 73736 | tf_op jit(solution)/shard_map/ppermute | solution.py:227
  105.7 4.8 %collective-permute-done.6.refs_1_.refs_12_ = bf16[6656,128]{1,0:T(8,128)(2,1)} collective-permute-done((bf16[6656,128]{1,0:T(8,128)(2,1)}, bf16[6656,128]{1,0:T(8,128)(2,1)}, u32[]{:S(2)}, u32[]{:S(2)}) %collective-permute-start.6) | collective-permute-done | bytes 1703968 | tf_op jit(solution)/shard_map/ppermute | solution.py:65
  110.4 2.1 %shard_map.44.refs_0_ = f32[128,128]{1,0:T(8,128)S(1)} custom-call(bf16[128,12480]{1,0:T(8,128)(2,1)S(1)} %copy.14.noise_ref, f32[128,128]{1,0:T(8,128)S(1)} %broadcast_in_dim.2.refs_0_.refs_1_, bf16[6656,128]{1,0:T(8,128)(2,1)} %collective-permute-done.6.refs_1_.refs_12_), custom_call_target="tpu_custom_call" | custom-call | flops 218103808 | bytes 3407872 | tf_op jit(solution)/shard_map/pallas_call | solution.py:101
  112.6 2.0 %shard_map.45 = f32[128,128]{1,0:T(8,128)S(1)} custom-call(bf16[128,12480]{1,0:T(8,128)(2,1)S(1)} %copy.14.noise_ref, f32[128,128]{1,0:T(8,128)S(1)} %shard_map.44.refs_0_, bf16[5824,128]{1,0:T(8,128)(2,1)} %collective-permute-done.7.refs_1_.refs_15_), custom_call_target="tpu_custom_call" | custom-call | flops 190840832 | bytes 2981888 | tf_op jit(solution)/shard_map/pallas_call | solution.py:101
  115.9 2.2 %collective-permute-start.12 = (f32[128,128]{1,0:T(8,128)S(1)}, f32[128,128]{1,0:T(8,128)S(1)}, u32[]{:S(2)}, u32[]{:S(2)}) collective-permute-start(f32[128,128]{1,0:T(8,128)S(1)} %add.9), channel_id=1, source_target_pairs={{0,2},{1,3},{2,0},{3,1},{4,6},{5,7},{6,4},{7,5},{8,10},{9,11},{10,... | collective-permute-start | bytes 196616 | tf_op jit(solution)/shard_map/ppermute | solution.py:227
  118.1 2.5 %collective-permute-done.12 = f32[128,128]{1,0:T(8,128)S(1)} collective-permute-done((f32[128,128]{1,0:T(8,128)S(1)}, f32[128,128]{1,0:T(8,128)S(1)}, u32[]{:S(2)}, u32[]{:S(2)}) %collective-permute-start.12) | collective-permute-done | bytes 65568 | tf_op jit(solution)/shard_map/ppermute | solution.py:227
  120.7 2.8 %collective-permute-start.17 = (f32[128,128]{1,0:T(8,128)S(1)}, f32[128,128]{1,0:T(8,128)S(1)}, u32[]{:S(2)}, u32[]{:S(2)}) collective-permute-start(f32[128,128]{1,0:T(8,128)S(1)} %add.10), channel_id=1, source_target_pairs={{0,4},{1,5},{2,6},{3,7},{4,0},{5,1},{6,2},{7,3},{8,12},{9,13},{10,... | collective-permute-start | bytes 196616 | tf_op jit(solution)/shard_map/ppermute | solution.py:227
  123.6 2.8 %collective-permute-done.17 = f32[128,128]{1,0:T(8,128)S(1)} collective-permute-done((f32[128,128]{1,0:T(8,128)S(1)}, f32[128,128]{1,0:T(8,128)S(1)}, u32[]{:S(2)}, u32[]{:S(2)}) %collective-permute-start.17) | collective-permute-done | bytes 65568 | tf_op jit(solution)/shard_map/ppermute | solution.py:227
  126.4 2.5 %collective-permute-start.20 = (f32[128,128]{1,0:T(8,128)S(1)}, f32[128,128]{1,0:T(8,128)S(1)}, u32[]{:S(2)}, u32[]{:S(2)}) collective-permute-start(f32[128,128]{1,0:T(8,128)S(1)} %add.11), channel_id=1, source_target_pairs={{0,24},{8,16},{16,8},{24,0},{1,25},{9,17},{17,9},{25,1},{2,26},{10... | collective-permute-start | bytes 196616 | tf_op jit(solution)/shard_map/ppermute | solution.py:65
  130.0 1.9 %collective-permute-done.20 = f32[128,128]{1,0:T(8,128)S(1)} collective-permute-done((f32[128,128]{1,0:T(8,128)S(1)}, f32[128,128]{1,0:T(8,128)S(1)}, u32[]{:S(2)}, u32[]{:S(2)}) %collective-permute-start.20) | collective-permute-done | bytes 65568 | tf_op jit(solution)/shard_map/ppermute | solution.py:65
  135.5 9.7 %shard_map.46 = (bf16[12480,128]{1,0:T(8,128)(2,1)}, f32[1,512]{1,0:T(1,128)}) custom-call(s32[2]{0:T(128)S(1)} %pad_add_fusion.index_ref, f32[64,384]{1,0:T(8,128)S(1)} %pad_maximum_fusion.2.refs_0_, f32[64,384]{1,0:T(8,128)S(1)} %copy-done.3, f32[64,384]{1,0:T(8,128)S(1)} %copy-done.1, f32[64,384]{1,0:T(8,128)S(1)} %collective-permute-done.10.refs_3_, ...), custom_call_target="tpu_custom_call" | custom-call | flops 1635778560 | bytes 15974400 | tf_op jit(solution)/shard_map/pallas_call | solution.py:198
  (49 shorter events, 15.7 us)
Async XLA Ops:
  0.6 73.3 %collective-permute-start.1 = (bf16[12480,128]{1,0:T(8,128)(2,1)}, bf16[12480,128]{1,0:T(8,128)(2,1)}, u32[]{:S(2)}, u32[]{:S(2)}) collective-permute-start(bf16[12480,128]{1,0:T(8,128)(2,1)} %bitcast.22), channel_id=1, source_target_pairs={{0,8},{8,0},{16,24},{24,16},{1,9},{9,1},{17,25},{25,17},{2,10},{10... | collective-permute-start | bytes 9584648 | tf_op jit(solution)/shard_map/ppermute | solution.py:65
  6.5 40.4 %collective-permute-start = (bf16[6656,128]{1,0:T(8,128)(2,1)}, bf16[6656,128]{1,0:T(8,128)(2,1)}, u32[]{:S(2)}, u32[]{:S(2)}) collective-permute-start(bf16[6656,128]{1,0:T(8,128)(2,1)} %slice.12.refs_1_.refs_9_), channel_id=1, source_target_pairs={{0,16},{8,24},{16,0},{24,8},{1,17},{9,25},{17,1},{25,9},{2,18},{10... | collective-permute-start | bytes 5111816 | tf_op jit(solution)/shard_map/ppermute | solution.py:65
  10.6 68.0 %collective-permute-start.2 = (bf16[5824,128]{1,0:T(8,128)(2,1)}, bf16[5824,128]{1,0:T(8,128)(2,1)}, u32[]{:S(2)}, u32[]{:S(2)}) collective-permute-start(bf16[5824,128]{1,0:T(8,128)(2,1)} %slice.13.refs_2_.refs_13_), channel_id=1, source_target_pairs={{0,16},{8,24},{16,0},{24,8},{1,17},{9,25},{17,1},{25,9},{2,18},{10... | collective-permute-start | bytes 4472840 | tf_op jit(solution)/shard_map/ppermute | solution.py:65
  49.0 61.4 %collective-permute-start.6 = (bf16[6656,128]{1,0:T(8,128)(2,1)}, bf16[6656,128]{1,0:T(8,128)(2,1)}, u32[]{:S(2)}, u32[]{:S(2)}) collective-permute-start(bf16[6656,128]{1,0:T(8,128)(2,1)} %collective-permute-done.refs_1_.refs_11_), channel_id=1, source_target_pairs={{0,8},{8,0},{16,24},{24,16},{1,9},{9,1},{17,25},{25,17},{2,10},{10... | collective-permute-start | bytes 5111816 | tf_op jit(solution)/shard_map/ppermute | solution.py:65
  76.5 36.0 %collective-permute-start.7 = (bf16[5824,128]{1,0:T(8,128)(2,1)}, bf16[5824,128]{1,0:T(8,128)(2,1)}, u32[]{:S(2)}, u32[]{:S(2)}) collective-permute-start(bf16[5824,128]{1,0:T(8,128)(2,1)} %slice.14), channel_id=1, source_target_pairs={{0,16},{8,24},{16,0},{24,8},{1,17},{9,25},{17,1},{25,9},{2,18},{10... | collective-permute-start | bytes 4472840 | tf_op jit(solution)/shard_map/ppermute | solution.py:65
  95.7 5.7 %collective-permute-start.5 = (f32[16,384]{1,0:T(8,128)S(1)}, f32[16,384]{1,0:T(8,128)S(1)}, u32[]{:S(2)}, u32[]{:S(2)}) collective-permute-start(f32[16,384]{1,0:T(8,128)S(1)} %reduce_sum.19), channel_id=1, source_target_pairs={{0,6},{1,7},{2,4},{3,5},{4,2},{5,3},{6,0},{7,1},{8,14},{9,15},{10,... | collective-permute-start | bytes 73736 | tf_op jit(solution)/shard_map/ppermute | solution.py:227
  97.0 4.9 %collective-permute-start.4 = (f32[16,384]{1,0:T(8,128)S(1)}, f32[16,384]{1,0:T(8,128)S(1)}, u32[]{:S(2)}, u32[]{:S(2)}) collective-permute-start(f32[16,384]{1,0:T(8,128)S(1)} %reduce_sum.19), channel_id=1, source_target_pairs={{0,4},{1,5},{2,6},{3,7},{4,0},{5,1},{6,2},{7,3},{8,12},{9,13},{10,... | collective-permute-start | bytes 73736 | tf_op jit(solution)/shard_map/ppermute | solution.py:227
  97.7 4.4 %collective-permute-start.3 = (f32[16,384]{1,0:T(8,128)S(1)}, f32[16,384]{1,0:T(8,128)S(1)}, u32[]{:S(2)}, u32[]{:S(2)}) collective-permute-start(f32[16,384]{1,0:T(8,128)S(1)} %reduce_sum.19), channel_id=1, source_target_pairs={{0,2},{1,3},{2,0},{3,1},{4,6},{5,7},{6,4},{7,5},{8,10},{9,11},{10,... | collective-permute-start | bytes 73736 | tf_op jit(solution)/shard_map/ppermute | solution.py:227
  102.1 12.4 %collective-permute-start.10 = (f32[64,384]{1,0:T(8,128)S(1)}, f32[64,384]{1,0:T(8,128)S(1)}, u32[]{:S(2)}, u32[]{:S(2)}) collective-permute-start(f32[64,384]{1,0:T(8,128)S(1)} %pad_maximum_fusion.2.refs_0_), channel_id=1, source_target_pairs={{0,24},{8,16},{16,8},{24,0},{1,25},{9,17},{17,9},{25,1},{2,26},{10... | collective-permute-start | bytes 294920 | tf_op jit(solution)/shard_map/ppermute | solution.py:65
  103.6 10.9 %collective-permute-start.9 = (f32[64,384]{1,0:T(8,128)S(1)}, f32[64,384]{1,0:T(8,128)S(1)}, u32[]{:S(2)}, u32[]{:S(2)}) collective-permute-start(f32[64,384]{1,0:T(8,128)S(1)} %pad_maximum_fusion.2.refs_0_), channel_id=1, source_target_pairs={{0,16},{8,24},{16,0},{24,8},{1,17},{9,25},{17,1},{25,9},{2,18},{10... | collective-permute-start | bytes 294920 | tf_op jit(solution)/shard_map/ppermute | solution.py:65
  105.2 9.4 %collective-permute-start.8 = (f32[64,384]{1,0:T(8,128)S(1)}, f32[64,384]{1,0:T(8,128)S(1)}, u32[]{:S(2)}, u32[]{:S(2)}) collective-permute-start(f32[64,384]{1,0:T(8,128)S(1)} %pad_maximum_fusion.2.refs_0_), channel_id=1, source_target_pairs={{0,8},{8,0},{16,24},{24,16},{1,9},{9,1},{17,25},{25,17},{2,10},{10... | collective-permute-start | bytes 294920 | tf_op jit(solution)/shard_map/ppermute | solution.py:65
  114.6 6.2 %copy-start = (f32[64,384]{1,0:T(8,128)}, f32[64,384]{1,0:T(8,128)S(1)}, u32[]{:S(2)}) copy-start(f32[64,384]{1,0:T(8,128)S(1)} %collective-permute-done.9.refs_2_) | copy-start | bytes 294916
  114.6 6.2 %copy-start.2 = (f32[64,384]{1,0:T(8,128)}, f32[64,384]{1,0:T(8,128)S(1)}, u32[]{:S(2)}) copy-start(f32[64,384]{1,0:T(8,128)S(1)} %collective-permute-done.8.refs_1_) | copy-start | bytes 294916
  114.6 1.3 collective-permute-start.11
  114.7 6.0 %collective-permute-start.13 = (f32[64,384]{1,0:T(8,128)S(1)}, f32[64,384]{1,0:T(8,128)S(1)}, u32[]{:S(2)}, u32[]{:S(2)}) collective-permute-start(f32[64,384]{1,0:T(8,128)S(1)} %pad_maximum_fusion.2.refs_0_), channel_id=1, source_target_pairs={{0,1},{1,0},{2,3},{3,2},{4,5},{5,4},{6,7},{7,6},{8,9},{9,8},{10,11... | collective-permute-start | bytes 294920 | tf_op jit(solution)/shard_map/ppermute | solution.py:227
  115.2 5.5 %collective-permute-start.14 = (f32[64,384]{1,0:T(8,128)S(1)}, f32[64,384]{1,0:T(8,128)S(1)}, u32[]{:S(2)}, u32[]{:S(2)}) collective-permute-start(f32[64,384]{1,0:T(8,128)S(1)} %collective-permute-done.8.refs_1_), channel_id=1, source_target_pairs={{0,1},{1,0},{2,3},{3,2},{4,5},{5,4},{6,7},{7,6},{8,9},{9,8},{10,11... | collective-permute-start | bytes 294920 | tf_op jit(solution)/shard_map/ppermute | solution.py:227
  115.2 5.5 %collective-permute-start.15 = (f32[64,384]{1,0:T(8,128)S(1)}, f32[64,384]{1,0:T(8,128)S(1)}, u32[]{:S(2)}, u32[]{:S(2)}) collective-permute-start(f32[64,384]{1,0:T(8,128)S(1)} %collective-permute-done.9.refs_2_), channel_id=1, source_target_pairs={{0,1},{1,0},{2,3},{3,2},{4,5},{5,4},{6,7},{7,6},{8,9},{9,8},{10,11... | collective-permute-start | bytes 294920 | tf_op jit(solution)/shard_map/ppermute | solution.py:227
  115.7 5.0 %collective-permute-start.16 = (f32[64,384]{1,0:T(8,128)S(1)}, f32[64,384]{1,0:T(8,128)S(1)}, u32[]{:S(2)}, u32[]{:S(2)}) collective-permute-start(f32[64,384]{1,0:T(8,128)S(1)} %collective-permute-done.10.refs_3_), channel_id=1, source_target_pairs={{0,1},{1,0},{2,3},{3,2},{4,5},{5,4},{6,7},{7,6},{8,9},{9,8},{10,11... | collective-permute-start | bytes 294920 | tf_op jit(solution)/shard_map/ppermute | solution.py:227
  115.9 4.7 %collective-permute-start.12 = (f32[128,128]{1,0:T(8,128)S(1)}, f32[128,128]{1,0:T(8,128)S(1)}, u32[]{:S(2)}, u32[]{:S(2)}) collective-permute-start(f32[128,128]{1,0:T(8,128)S(1)} %add.9), channel_id=1, source_target_pairs={{0,2},{1,3},{2,0},{3,1},{4,6},{5,7},{6,4},{7,5},{8,10},{9,11},{10,... | collective-permute-start | bytes 196616 | tf_op jit(solution)/shard_map/ppermute | solution.py:227
  120.7 5.6 %collective-permute-start.17 = (f32[128,128]{1,0:T(8,128)S(1)}, f32[128,128]{1,0:T(8,128)S(1)}, u32[]{:S(2)}, u32[]{:S(2)}) collective-permute-start(f32[128,128]{1,0:T(8,128)S(1)} %add.10), channel_id=1, source_target_pairs={{0,4},{1,5},{2,6},{3,7},{4,0},{5,1},{6,2},{7,3},{8,12},{9,13},{10,... | collective-permute-start | bytes 196616 | tf_op jit(solution)/shard_map/ppermute | solution.py:227
  126.4 5.5 %collective-permute-start.20 = (f32[128,128]{1,0:T(8,128)S(1)}, f32[128,128]{1,0:T(8,128)S(1)}, u32[]{:S(2)}, u32[]{:S(2)}) collective-permute-start(f32[128,128]{1,0:T(8,128)S(1)} %add.11), channel_id=1, source_target_pairs={{0,24},{8,16},{16,8},{24,0},{1,25},{9,17},{17,9},{25,1},{2,26},{10... | collective-permute-start | bytes 196616 | tf_op jit(solution)/shard_map/ppermute | solution.py:65
  128.9 4.3 %collective-permute-start.19 = (f32[128,128]{1,0:T(8,128)S(1)}, f32[128,128]{1,0:T(8,128)S(1)}, u32[]{:S(2)}, u32[]{:S(2)}) collective-permute-start(f32[128,128]{1,0:T(8,128)S(1)} %add.11), channel_id=1, source_target_pairs={{0,16},{8,24},{16,0},{24,8},{1,17},{9,25},{17,1},{25,9},{2,18},{10... | collective-permute-start | bytes 196616 | tf_op jit(solution)/shard_map/ppermute | solution.py:65
  129.4 4.3 %collective-permute-start.18 = (f32[128,128]{1,0:T(8,128)S(1)}, f32[128,128]{1,0:T(8,128)S(1)}, u32[]{:S(2)}, u32[]{:S(2)}) collective-permute-start(f32[128,128]{1,0:T(8,128)S(1)} %add.11), channel_id=1, source_target_pairs={{0,8},{8,0},{16,24},{24,16},{1,9},{9,1},{17,25},{25,17},{2,10},{10... | collective-permute-start | bytes 196616 | tf_op jit(solution)/shard_map/ppermute | solution.py:65
  133.7 0.9 copy-start.1
  (1 other events, 0.9 us)

commit v6 on v5

--- a/solution.py
+++ b/solution.py
@@ -103,7 +103,7 @@
         out_shape=jax.ShapeDtypeStruct((rows, rows * len(blocks)), jnp.float32),
         in_specs=[VMEM] * (1 + len(values)),
         out_specs=VMEM,
-        compiler_params=pltpu.CompilerParams(vmem_limit_bytes=16 * 2**20),
+        compiler_params=pltpu.CompilerParams(vmem_limit_bytes=12 * 2**20),
         cost_estimate=pl.CostEstimate(flops=flops, bytes_accessed=flops // 64, transcendentals=0),
     )(noise, *values)
 

time: 146 us -> 146 us (level)
  no operation moved by 1% of the time
where the time goes in v6:
time: 146 us; the launch traced here: 145 us
  waiting for transfers between devices  66 us (45%)
  starting transfers between devices  24.9 us (17%)
  Pallas kernels  23 us (16%)
  local copies, waits for them, and re-layouts  14.1 us (10%)
  blocking collectives  13 us (9%)
  other arithmetic  3.24 us (2%)
    ppermute x11, waiting for transfers between devices, swap(): return lax.ppermute(value, 'batch', [(i, i ^ way) for i in range(4)])  58.6 us
    ppermute x11, starting transfers between devices, swap(): return lax.ppermute(value, 'batch', [(i, i ^ way) for i in range(4)])  14.3 us
    pallas_call x5, Pallas kernels, crossed(): pl.pallas_call(functools.partial(cross_kernel, spans), out_shape=jax.Shap...  13.3 us
    all_to_all x1, blocking collectives, group_share(): parts = lax.all_to_all(parts, 'group', 0, 0, tiled=True)  13 us
    ppermute x10, starting transfers between devices, turn(): return lax.ppermute(value, 'group', [(g, g ^ way) for g in range(groups)])  10.6 us
    pallas_call x1, Pallas kernels, paired(): pl.pallas_call(functools.partial(pair_kernel, rows, feats, places), out_s...  9.69 us
    ppermute x10, waiting for transfers between devices, turn(): return lax.ppermute(value, 'group', [(g, g ^ way) for g in range(groups)])  7.41 us
    unnamed x9, local copies, waits for them, and re-layouts  5.98 us
  transfers between devices with their start and end apart: 21, of which 12 were waited for; matrix products, arithmetic and copies ran while one was open for 11% of the time, Pallas kernels for 9%

profile of v6, /device:TPU:0, one launch (start us, length us, event | category | flops | bytes accessed | tf_op | source)
XLA Modules:
  0.0 145.2 jit_solution(1494153949240541916)
XLA Ops:
  0.6 3.0 %collective-permute-start.1 = (bf16[12480,128]{1,0:T(8,128)(2,1)}, bf16[12480,128]{1,0:T(8,128)(2,1)}, u32[]{:S(2)}, u32[]{:S(2)}) collective-permute-start(bf16[12480,128]{1,0:T(8,128)(2,1)} %bitcast.22), channel_id=1, source_target_pairs={{0,8},{8,0},{16,24},{24,16},{1,9},{9,1},{17,25},{25,17},{2,10},{10... | collective-permute-start | bytes 9584648 | tf_op jit(solution)/shard_map/ppermute | solution.py:65
  3.6 2.8 %slice.12.refs_1_.refs_9_ = bf16[6656,128]{1,0:T(8,128)(2,1)} slice(bf16[12480,128]{1,0:T(8,128)(2,1)} %bitcast.23), slice={[0:6656], [0:128]} | slice | bytes 3407872 | tf_op jit(solution)/shard_map/slice | solution.py:260
  8.0 2.6 %slice.13.refs_2_.refs_13_ = bf16[5824,128]{1,0:T(8,128)(2,1)} slice(bf16[12480,128]{1,0:T(8,128)(2,1)} %bitcast.24), slice={[6656:12480], [0:128]} | slice | bytes 2981888 | tf_op jit(solution)/shard_map/slice | solution.py:260
  11.1 4.2 %copy.14.noise_ref = bf16[128,12480]{1,0:T(8,128)(2,1)S(1)} copy(bf16[128,12480]{0,1:T(8,128)(2,1)} %param.2) | data formatting | bytes 6389760 | tf_op args[0]
  15.3 3.1 %multiply_reduce_fusion = f32[128]{0:T(128)S(1)} fusion(bf16[128,12480]{0,1:T(8,128)(2,1)} %param.2), kind=kLoop, calls=%fused_computation | loop fusion | flops 4792192 | bytes 3195392 | tf_op jit(solution)/shard_map/reduce_sum | solution.py:222
  18.5 3.1 %shard_map.41.refs_0_ = f32[128,128]{1,0:T(8,128)S(1)} custom-call(bf16[128,12480]{1,0:T(8,128)(2,1)S(1)} %copy.14.noise_ref, f32[128,128]{1,0:T(8,128)S(1)} %broadcast_in_dim.2.refs_0_.refs_1_, bf16[6656,128]{1,0:T(8,128)(2,1)} %slice.12.refs_1_.refs_9_, bf16[5824,128]{1,0:T(8,128)(2,1)} %slice.13.refs_2_.refs_13_), custom_call_target="tpu_custom_call" | custom-call | flops 408944640 | bytes 6389760 | tf_op jit(solution)/shard_map/pallas_call | solution.py:101
  21.6 25.3 %collective-permute-done.refs_1_.refs_11_ = bf16[6656,128]{1,0:T(8,128)(2,1)} collective-permute-done((bf16[6656,128]{1,0:T(8,128)(2,1)}, bf16[6656,128]{1,0:T(8,128)(2,1)}, u32[]{:S(2)}, u32[]{:S(2)}) %collective-permute-start) | collective-permute-done | bytes 1703968 | tf_op jit(solution)/shard_map/ppermute | solution.py:65
  46.9 2.1 %shard_map.42.refs_3_ = f32[128,128]{1,0:T(8,128)S(1)} custom-call(bf16[128,12480]{1,0:T(8,128)(2,1)S(1)} %copy.14.noise_ref, f32[128,128]{1,0:T(8,128)S(1)} %broadcast_in_dim.2.refs_0_.refs_1_, bf16[6656,128]{1,0:T(8,128)(2,1)} %collective-permute-done.refs_1_.refs_11_), custom_call_target="tpu_custom_call" | custom-call | flops 218103808 | bytes 3407872 | tf_op jit(solution)/shard_map/pallas_call | solution.py:101
  49.1 24.8 %collective-permute-done.1.refs_2_.refs_10_ = bf16[12480,128]{1,0:T(8,128)(2,1)} collective-permute-done((bf16[12480,128]{1,0:T(8,128)(2,1)}, bf16[12480,128]{1,0:T(8,128)(2,1)}, u32[]{:S(2)}, u32[]{:S(2)}) %collective-permute-start.1) | collective-permute-done | bytes 3194912 | tf_op jit(solution)/shard_map/ppermute | solution.py:65
  73.9 2.6 %slice.14 = bf16[5824,128]{1,0:T(8,128)(2,1)} slice(bf16[12480,128]{1,0:T(8,128)(2,1)} %collective-permute-done.1.refs_2_.refs_10_), slice={[6656:12480], [0:128]} | slice | bytes 2981888 | tf_op jit(solution)/shard_map/slice | solution.py:267
  76.5 2.1 %collective-permute-start.7 = (bf16[5824,128]{1,0:T(8,128)(2,1)}, bf16[5824,128]{1,0:T(8,128)(2,1)}, u32[]{:S(2)}, u32[]{:S(2)}) collective-permute-start(bf16[5824,128]{1,0:T(8,128)(2,1)} %slice.14), channel_id=1, source_target_pairs={{0,16},{8,24},{16,0},{24,8},{1,17},{9,25},{17,1},{25,9},{2,18},{10... | collective-permute-start | bytes 4472840 | tf_op jit(solution)/shard_map/ppermute | solution.py:65
  78.6 4.0 %shard_map.43 = f32[128,384]{1,0:T(8,128)S(1)} custom-call(bf16[128,12480]{1,0:T(8,128)(2,1)S(1)} %copy.14.noise_ref, f32[128,128]{1,0:T(8,128)S(1)} %shard_map.41.refs_0_, f32[128,128]{1,0:T(8,128)S(1)} %broadcast_in_dim.2.refs_0_.refs_1_, bf16[12480,128]{1,0:T(8,128)(2,1)} %collective-permute-done.1.refs_2_.refs_10_, f32[128,128]{1,0:T(8,128)S(1)} %shard_map.42.refs_3_, ...), custom_call_target="tpu_custom_call" | custom-call | flops 599785472 | bytes 9371648 | tf_op jit(solution)/shard_map/pallas_call | solution.py:101
  82.7 13.0 %all_to_all.9 = f32[8,16,384]{2,1,0:T(8,128)S(1)} all-to-all(f32[8,16,384]{2,1,0:T(8,128)S(1)} %bitcast.25), channel_id=1, replica_groups=mesh['batch'=4,'group'=8] {'group'}, dimensions={0} | all-to-all | bytes 393216 | tf_op jit(solution)/shard_map/all_to_all | solution.py:235
  97.7 2.5 %collective-permute-start.3 = (f32[16,384]{1,0:T(8,128)S(1)}, f32[16,384]{1,0:T(8,128)S(1)}, u32[]{:S(2)}, u32[]{:S(2)}) collective-permute-start(f32[16,384]{1,0:T(8,128)S(1)} %reduce_sum.19), channel_id=1, source_target_pairs={{0,2},{1,3},{2,0},{3,1},{4,6},{5,7},{6,4},{7,5},{8,10},{9,11},{10,... | collective-permute-start | bytes 73736 | tf_op jit(solution)/shard_map/ppermute | solution.py:227
  105.7 4.8 %collective-permute-done.6.refs_1_.refs_12_ = bf16[6656,128]{1,0:T(8,128)(2,1)} collective-permute-done((bf16[6656,128]{1,0:T(8,128)(2,1)}, bf16[6656,128]{1,0:T(8,128)(2,1)}, u32[]{:S(2)}, u32[]{:S(2)}) %collective-permute-start.6) | collective-permute-done | bytes 1703968 | tf_op jit(solution)/shard_map/ppermute | solution.py:65
  110.4 2.1 %shard_map.44.refs_0_ = f32[128,128]{1,0:T(8,128)S(1)} custom-call(bf16[128,12480]{1,0:T(8,128)(2,1)S(1)} %copy.14.noise_ref, f32[128,128]{1,0:T(8,128)S(1)} %broadcast_in_dim.2.refs_0_.refs_1_, bf16[6656,128]{1,0:T(8,128)(2,1)} %collective-permute-done.6.refs_1_.refs_12_), custom_call_target="tpu_custom_call" | custom-call | flops 218103808 | bytes 3407872 | tf_op jit(solution)/shard_map/pallas_call | solution.py:101
  112.6 2.0 %shard_map.45 = f32[128,128]{1,0:T(8,128)S(1)} custom-call(bf16[128,12480]{1,0:T(8,128)(2,1)S(1)} %copy.14.noise_ref, f32[128,128]{1,0:T(8,128)S(1)} %shard_map.44.refs_0_, bf16[5824,128]{1,0:T(8,128)(2,1)} %collective-permute-done.7.refs_1_.refs_15_), custom_call_target="tpu_custom_call" | custom-call | flops 190840832 | bytes 2981888 | tf_op jit(solution)/shard_map/pallas_call | solution.py:101
  115.9 2.2 %collective-permute-start.12 = (f32[128,128]{1,0:T(8,128)S(1)}, f32[128,128]{1,0:T(8,128)S(1)}, u32[]{:S(2)}, u32[]{:S(2)}) collective-permute-start(f32[128,128]{1,0:T(8,128)S(1)} %add.9), channel_id=1, source_target_pairs={{0,2},{1,3},{2,0},{3,1},{4,6},{5,7},{6,4},{7,5},{8,10},{9,11},{10,... | collective-permute-start | bytes 196616 | tf_op jit(solution)/shard_map/ppermute | solution.py:227
  118.1 2.5 %collective-permute-done.12 = f32[128,128]{1,0:T(8,128)S(1)} collective-permute-done((f32[128,128]{1,0:T(8,128)S(1)}, f32[128,128]{1,0:T(8,128)S(1)}, u32[]{:S(2)}, u32[]{:S(2)}) %collective-permute-start.12) | collective-permute-done | bytes 65568 | tf_op jit(solution)/shard_map/ppermute | solution.py:227
  120.7 2.8 %collective-permute-start.17 = (f32[128,128]{1,0:T(8,128)S(1)}, f32[128,128]{1,0:T(8,128)S(1)}, u32[]{:S(2)}, u32[]{:S(2)}) collective-permute-start(f32[128,128]{1,0:T(8,128)S(1)} %add.10), channel_id=1, source_target_pairs={{0,4},{1,5},{2,6},{3,7},{4,0},{5,1},{6,2},{7,3},{8,12},{9,13},{10,... | collective-permute-start | bytes 196616 | tf_op jit(solution)/shard_map/ppermute | solution.py:227
  123.6 2.8 %collective-permute-done.17 = f32[128,128]{1,0:T(8,128)S(1)} collective-permute-done((f32[128,128]{1,0:T(8,128)S(1)}, f32[128,128]{1,0:T(8,128)S(1)}, u32[]{:S(2)}, u32[]{:S(2)}) %collective-permute-start.17) | collective-permute-done | bytes 65568 | tf_op jit(solution)/shard_map/ppermute | solution.py:227
  126.4 2.5 %collective-permute-start.20 = (f32[128,128]{1,0:T(8,128)S(1)}, f32[128,128]{1,0:T(8,128)S(1)}, u32[]{:S(2)}, u32[]{:S(2)}) collective-permute-start(f32[128,128]{1,0:T(8,128)S(1)} %add.11), channel_id=1, source_target_pairs={{0,24},{8,16},{16,8},{24,0},{1,25},{9,17},{17,9},{25,1},{2,26},{10... | collective-permute-start | bytes 196616 | tf_op jit(solution)/shard_map/ppermute | solution.py:65
  130.0 1.9 %collective-permute-done.20 = f32[128,128]{1,0:T(8,128)S(1)} collective-permute-done((f32[128,128]{1,0:T(8,128)S(1)}, f32[128,128]{1,0:T(8,128)S(1)}, u32[]{:S(2)}, u32[]{:S(2)}) %collective-permute-start.20) | collective-permute-done | bytes 65568 | tf_op jit(solution)/shard_map/ppermute | solution.py:65
  135.5 9.7 %shard_map.46 = (bf16[12480,128]{1,0:T(8,128)(2,1)}, f32[1,512]{1,0:T(1,128)}) custom-call(s32[2]{0:T(128)S(1)} %pad_add_fusion.index_ref, f32[64,384]{1,0:T(8,128)S(1)} %pad_maximum_fusion.2.refs_0_, f32[64,384]{1,0:T(8,128)S(1)} %copy-done.3, f32[64,384]{1,0:T(8,128)S(1)} %copy-done.1, f32[64,384]{1,0:T(8,128)S(1)} %collective-permute-done.10.refs_3_, ...), custom_call_target="tpu_custom_call" | custom-call | flops 1635778560 | bytes 15974400 | tf_op jit(solution)/shard_map/pallas_call | solution.py:198
  (49 shorter events, 15.7 us)
Async XLA Ops:
  0.6 73.3 %collective-permute-start.1 = (bf16[12480,128]{1,0:T(8,128)(2,1)}, bf16[12480,128]{1,0:T(8,128)(2,1)}, u32[]{:S(2)}, u32[]{:S(2)}) collective-permute-start(bf16[12480,128]{1,0:T(8,128)(2,1)} %bitcast.22), channel_id=1, source_target_pairs={{0,8},{8,0},{16,24},{24,16},{1,9},{9,1},{17,25},{25,17},{2,10},{10... | collective-permute-start | bytes 9584648 | tf_op jit(solution)/shard_map/ppermute | solution.py:65
  6.5 40.4 %collective-permute-start = (bf16[6656,128]{1,0:T(8,128)(2,1)}, bf16[6656,128]{1,0:T(8,128)(2,1)}, u32[]{:S(2)}, u32[]{:S(2)}) collective-permute-start(bf16[6656,128]{1,0:T(8,128)(2,1)} %slice.12.refs_1_.refs_9_), channel_id=1, source_target_pairs={{0,16},{8,24},{16,0},{24,8},{1,17},{9,25},{17,1},{25,9},{2,18},{10... | collective-permute-start | bytes 5111816 | tf_op jit(solution)/shard_map/ppermute | solution.py:65
  10.6 68.0 %collective-permute-start.2 = (bf16[5824,128]{1,0:T(8,128)(2,1)}, bf16[5824,128]{1,0:T(8,128)(2,1)}, u32[]{:S(2)}, u32[]{:S(2)}) collective-permute-start(bf16[5824,128]{1,0:T(8,128)(2,1)} %slice.13.refs_2_.refs_13_), channel_id=1, source_target_pairs={{0,16},{8,24},{16,0},{24,8},{1,17},{9,25},{17,1},{25,9},{2,18},{10... | collective-permute-start | bytes 4472840 | tf_op jit(solution)/shard_map/ppermute | solution.py:65
  49.0 61.4 %collective-permute-start.6 = (bf16[6656,128]{1,0:T(8,128)(2,1)}, bf16[6656,128]{1,0:T(8,128)(2,1)}, u32[]{:S(2)}, u32[]{:S(2)}) collective-permute-start(bf16[6656,128]{1,0:T(8,128)(2,1)} %collective-permute-done.refs_1_.refs_11_), channel_id=1, source_target_pairs={{0,8},{8,0},{16,24},{24,16},{1,9},{9,1},{17,25},{25,17},{2,10},{10... | collective-permute-start | bytes 5111816 | tf_op jit(solution)/shard_map/ppermute | solution.py:65
  76.5 36.0 %collective-permute-start.7 = (bf16[5824,128]{1,0:T(8,128)(2,1)}, bf16[5824,128]{1,0:T(8,128)(2,1)}, u32[]{:S(2)}, u32[]{:S(2)}) collective-permute-start(bf16[5824,128]{1,0:T(8,128)(2,1)} %slice.14), channel_id=1, source_target_pairs={{0,16},{8,24},{16,0},{24,8},{1,17},{9,25},{17,1},{25,9},{2,18},{10... | collective-permute-start | bytes 4472840 | tf_op jit(solution)/shard_map/ppermute | solution.py:65
  95.7 5.7 %collective-permute-start.5 = (f32[16,384]{1,0:T(8,128)S(1)}, f32[16,384]{1,0:T(8,128)S(1)}, u32[]{:S(2)}, u32[]{:S(2)}) collective-permute-start(f32[16,384]{1,0:T(8,128)S(1)} %reduce_sum.19), channel_id=1, source_target_pairs={{0,6},{1,7},{2,4},{3,5},{4,2},{5,3},{6,0},{7,1},{8,14},{9,15},{10,... | collective-permute-start | bytes 73736 | tf_op jit(solution)/shard_map/ppermute | solution.py:227
  97.0 4.9 %collective-permute-start.4 = (f32[16,384]{1,0:T(8,128)S(1)}, f32[16,384]{1,0:T(8,128)S(1)}, u32[]{:S(2)}, u32[]{:S(2)}) collective-permute-start(f32[16,384]{1,0:T(8,128)S(1)} %reduce_sum.19), channel_id=1, source_target_pairs={{0,4},{1,5},{2,6},{3,7},{4,0},{5,1},{6,2},{7,3},{8,12},{9,13},{10,... | collective-permute-start | bytes 73736 | tf_op jit(solution)/shard_map/ppermute | solution.py:227
  97.7 4.4 %collective-permute-start.3 = (f32[16,384]{1,0:T(8,128)S(1)}, f32[16,384]{1,0:T(8,128)S(1)}, u32[]{:S(2)}, u32[]{:S(2)}) collective-permute-start(f32[16,384]{1,0:T(8,128)S(1)} %reduce_sum.19), channel_id=1, source_target_pairs={{0,2},{1,3},{2,0},{3,1},{4,6},{5,7},{6,4},{7,5},{8,10},{9,11},{10,... | collective-permute-start | bytes 73736 | tf_op jit(solution)/shard_map/ppermute | solution.py:227
  102.1 12.4 %collective-permute-start.10 = (f32[64,384]{1,0:T(8,128)S(1)}, f32[64,384]{1,0:T(8,128)S(1)}, u32[]{:S(2)}, u32[]{:S(2)}) collective-permute-start(f32[64,384]{1,0:T(8,128)S(1)} %pad_maximum_fusion.2.refs_0_), channel_id=1, source_target_pairs={{0,24},{8,16},{16,8},{24,0},{1,25},{9,17},{17,9},{25,1},{2,26},{10... | collective-permute-start | bytes 294920 | tf_op jit(solution)/shard_map/ppermute | solution.py:65
  103.6 10.9 %collective-permute-start.9 = (f32[64,384]{1,0:T(8,128)S(1)}, f32[64,384]{1,0:T(8,128)S(1)}, u32[]{:S(2)}, u32[]{:S(2)}) collective-permute-start(f32[64,384]{1,0:T(8,128)S(1)} %pad_maximum_fusion.2.refs_0_), channel_id=1, source_target_pairs={{0,16},{8,24},{16,0},{24,8},{1,17},{9,25},{17,1},{25,9},{2,18},{10... | collective-permute-start | bytes 294920 | tf_op jit(solution)/shard_map/ppermute | solution.py:65
  105.2 9.4 %collective-permute-start.8 = (f32[64,384]{1,0:T(8,128)S(1)}, f32[64,384]{1,0:T(8,128)S(1)}, u32[]{:S(2)}, u32[]{:S(2)}) collective-permute-start(f32[64,384]{1,0:T(8,128)S(1)} %pad_maximum_fusion.2.refs_0_), channel_id=1, source_target_pairs={{0,8},{8,0},{16,24},{24,16},{1,9},{9,1},{17,25},{25,17},{2,10},{10... | collective-permute-start | bytes 294920 | tf_op jit(solution)/shard_map/ppermute | solution.py:65
  114.6 6.2 %copy-start = (f32[64,384]{1,0:T(8,128)}, f32[64,384]{1,0:T(8,128)S(1)}, u32[]{:S(2)}) copy-start(f32[64,384]{1,0:T(8,128)S(1)} %collective-permute-done.9.refs_2_) | copy-start | bytes 294916
  114.6 6.2 %copy-start.2 = (f32[64,384]{1,0:T(8,128)}, f32[64,384]{1,0:T(8,128)S(1)}, u32[]{:S(2)}) copy-start(f32[64,384]{1,0:T(8,128)S(1)} %collective-permute-done.8.refs_1_) | copy-start | bytes 294916
  114.6 1.3 collective-permute-start.11
  114.7 6.0 %collective-permute-start.13 = (f32[64,384]{1,0:T(8,128)S(1)}, f32[64,384]{1,0:T(8,128)S(1)}, u32[]{:S(2)}, u32[]{:S(2)}) collective-permute-start(f32[64,384]{1,0:T(8,128)S(1)} %pad_maximum_fusion.2.refs_0_), channel_id=1, source_target_pairs={{0,1},{1,0},{2,3},{3,2},{4,5},{5,4},{6,7},{7,6},{8,9},{9,8},{10,11... | collective-permute-start | bytes 294920 | tf_op jit(solution)/shard_map/ppermute | solution.py:227
  115.2 5.5 %collective-permute-start.14 = (f32[64,384]{1,0:T(8,128)S(1)}, f32[64,384]{1,0:T(8,128)S(1)}, u32[]{:S(2)}, u32[]{:S(2)}) collective-permute-start(f32[64,384]{1,0:T(8,128)S(1)} %collective-permute-done.8.refs_1_), channel_id=1, source_target_pairs={{0,1},{1,0},{2,3},{3,2},{4,5},{5,4},{6,7},{7,6},{8,9},{9,8},{10,11... | collective-permute-start | bytes 294920 | tf_op jit(solution)/shard_map/ppermute | solution.py:227
  115.2 5.5 %collective-permute-start.15 = (f32[64,384]{1,0:T(8,128)S(1)}, f32[64,384]{1,0:T(8,128)S(1)}, u32[]{:S(2)}, u32[]{:S(2)}) collective-permute-start(f32[64,384]{1,0:T(8,128)S(1)} %collective-permute-done.9.refs_2_), channel_id=1, source_target_pairs={{0,1},{1,0},{2,3},{3,2},{4,5},{5,4},{6,7},{7,6},{8,9},{9,8},{10,11... | collective-permute-start | bytes 294920 | tf_op jit(solution)/shard_map/ppermute | solution.py:227
  115.7 5.0 %collective-permute-start.16 = (f32[64,384]{1,0:T(8,128)S(1)}, f32[64,384]{1,0:T(8,128)S(1)}, u32[]{:S(2)}, u32[]{:S(2)}) collective-permute-start(f32[64,384]{1,0:T(8,128)S(1)} %collective-permute-done.10.refs_3_), channel_id=1, source_target_pairs={{0,1},{1,0},{2,3},{3,2},{4,5},{5,4},{6,7},{7,6},{8,9},{9,8},{10,11... | collective-permute-start | bytes 294920 | tf_op jit(solution)/shard_map/ppermute | solution.py:227
  115.9 4.7 %collective-permute-start.12 = (f32[128,128]{1,0:T(8,128)S(1)}, f32[128,128]{1,0:T(8,128)S(1)}, u32[]{:S(2)}, u32[]{:S(2)}) collective-permute-start(f32[128,128]{1,0:T(8,128)S(1)} %add.9), channel_id=1, source_target_pairs={{0,2},{1,3},{2,0},{3,1},{4,6},{5,7},{6,4},{7,5},{8,10},{9,11},{10,... | collective-permute-start | bytes 196616 | tf_op jit(solution)/shard_map/ppermute | solution.py:227
  120.7 5.6 %collective-permute-start.17 = (f32[128,128]{1,0:T(8,128)S(1)}, f32[128,128]{1,0:T(8,128)S(1)}, u32[]{:S(2)}, u32[]{:S(2)}) collective-permute-start(f32[128,128]{1,0:T(8,128)S(1)} %add.10), channel_id=1, source_target_pairs={{0,4},{1,5},{2,6},{3,7},{4,0},{5,1},{6,2},{7,3},{8,12},{9,13},{10,... | collective-permute-start | bytes 196616 | tf_op jit(solution)/shard_map/ppermute | solution.py:227
  126.4 5.5 %collective-permute-start.20 = (f32[128,128]{1,0:T(8,128)S(1)}, f32[128,128]{1,0:T(8,128)S(1)}, u32[]{:S(2)}, u32[]{:S(2)}) collective-permute-start(f32[128,128]{1,0:T(8,128)S(1)} %add.11), channel_id=1, source_target_pairs={{0,24},{8,16},{16,8},{24,0},{1,25},{9,17},{17,9},{25,1},{2,26},{10... | collective-permute-start | bytes 196616 | tf_op jit(solution)/shard_map/ppermute | solution.py:65
  128.9 4.3 %collective-permute-start.19 = (f32[128,128]{1,0:T(8,128)S(1)}, f32[128,128]{1,0:T(8,128)S(1)}, u32[]{:S(2)}, u32[]{:S(2)}) collective-permute-start(f32[128,128]{1,0:T(8,128)S(1)} %add.11), channel_id=1, source_target_pairs={{0,16},{8,24},{16,0},{24,8},{1,17},{9,25},{17,1},{25,9},{2,18},{10... | collective-permute-start | bytes 196616 | tf_op jit(solution)/shard_map/ppermute | solution.py:65
  129.4 4.3 %collective-permute-start.18 = (f32[128,128]{1,0:T(8,128)S(1)}, f32[128,128]{1,0:T(8,128)S(1)}, u32[]{:S(2)}, u32[]{:S(2)}) collective-permute-start(f32[128,128]{1,0:T(8,128)S(1)} %add.11), channel_id=1, source_target_pairs={{0,8},{8,0},{16,24},{24,16},{1,9},{9,1},{17,25},{25,17},{2,10},{10... | collective-permute-start | bytes 196616 | tf_op jit(solution)/shard_map/ppermute | solution.py:65
  133.7 0.9 copy-start.1
  (1 other events, 0.9 us)
